TPU v7x, 32 devices: a whole 2x2x4 slice. The times are simulated.
32 devices in a mesh: dp: 8 (over z, y), tensor: 4 (over x, core).
Axes of the slice: x: 2, y: 2, z: 4, core: 2. Of those that a mesh axis runs over, the one named last changes fastest.
Arguments:
- layer_input: bfloat16 [8192, 4096], P(('dp', 'tensor')), may hold values from -6 to 6
- kv_weight: bfloat16 [2, 4096, 1024], P(None, None, 'tensor'), may hold values from -0.09375 to 0.09375
- kv_cotangent: bfloat16 [2, 8192, 1024], P(None, 'dp', 'tensor'), may hold values from -6 to 6
- error_before: bfloat16 [8, 2, 4096, 1024], P('dp', None, None, 'tensor'), may hold values from -6 to 6
- right_factor: float32 [2, 32, 4096], replicated, may hold values from -6 to 6
Outputs:
- error_after: float32 [8, 2, 4096, 1024], P('dp', None, None, 'tensor')
- right_next: float32 [2, 32, 4096], replicated
- input_grad: bfloat16 [8192, 4096], P(('dp', 'tensor'))
All inputs are finite; a program needn't handle non-finite values.
Results may differ from a plain program's by a relative error of at most 0.012.
Values may be sent and summed in bfloat16 or wider, within the bound.
No kernel may reach another device: no remote copies, remote signals or barrier semaphores. Data moves between devices by JAX's collectives and lax.ppermute only.
A program may use at most 128 MiB of HBM per device.

v0:
```python
from functools import partial

import jax
import jax.numpy as jnp
from jax import lax
from jax.sharding import PartitionSpec as P

TOKENS = 1024


def compress(moments, right_prev):
    highest = lax.Precision.HIGHEST
    replicas = lax.axis_size("dp")
    projected = jnp.einsum("mdc,mrd->mrc", moments, right_prev, precision=highest)
    left_sum = lax.psum(projected, "dp")
    gram_matrix = lax.psum(
        jnp.einsum("mrc,msc->mrs", left_sum, left_sum, precision=highest), "tensor"
    )
    factor = jnp.linalg.cholesky(gram_matrix)
    ortho_basis = jax.vmap(partial(jax.scipy.linalg.solve_triangular, lower=True))(factor, left_sum)
    right_local = jnp.einsum("mdc,mrc->mrd", moments, ortho_basis, precision=highest)
    right_total = lax.psum(right_local, "tensor")
    right_total = lax.psum(right_total, "dp")
    right_mean = right_total / replicas
    approximation = jnp.einsum("mrd,mrc->mdc", right_mean, ortho_basis, precision=highest)
    return (moments - approximation, right_mean)


def per_device(layer_input, kv_weight, kv_cotangent, error_before, right_factor):
    portion = kv_cotangent
    weight_grad = jnp.einsum(
        "td,mtc->mdc",
        lax.all_gather(layer_input, "tensor", axis=0, tiled=True),
        portion,
        preferred_element_type=jnp.float32,
    )
    moments = weight_grad * TOKENS ** (-0.5) + error_before[0].astype(jnp.float32)
    portion = kv_cotangent
    input_sum = lax.psum_scatter(
        jnp.einsum("mtc,mdc->td", portion, kv_weight, preferred_element_type=jnp.float32).astype(
            jnp.bfloat16
        ),
        "tensor",
        scatter_dimension=0,
        tiled=True,
    )
    leading = compress(moments[0:1], right_factor[0:1])
    second = compress(moments[1:2], right_factor[1:2])
    errors = jnp.concatenate([leading[0], second[0]], axis=0)
    right_next = jnp.concatenate([leading[1], second[1]], axis=0)
    return (errors[None], right_next, input_sum)


def solution(mesh):
    return jax.shard_map(
        per_device,
        mesh=mesh,
        in_specs=(
            P(("dp", "tensor"), None),
            P(None, None, "tensor"),
            P(None, "dp", "tensor"),
            P("dp", None, None, "tensor"),
            P(),
        ),
        out_specs=(P("dp", None, None, "tensor"), P(), P(("dp", "tensor"), None)),
        check_vma=False,
    )
```

profile of v0, /device:TPU:0, one launch (start us, length us, event | category | flops | bytes accessed | tf_op | source)
XLA Modules:
  0.0 396.3 jit_solution(4833851372384504543)
XLA Ops:
  8.0 6.3 %copy.9 = bf16[1,2,4096,256]{2,3,1,0:T(8,128)(2,1)} copy(bf16[1,2,4096,256]{3,2,1,0:T(8,128)(2,1)} %param.11) | data formatting | bytes 8388608 | tf_op args[3]
  14.3 56.3 %all-gather.2.cloned.1.call-done = bf16[1024,4096]{1,0:T(8,128)(2,1)} async-done(((bf16[256,4096]{1,0:T(8,128)(2,1)}), bf16[1024,4096]{1,0:T(8,128)(2,1)}) %all-gather.2.cloned.1.call-update) | async-done | bytes 8388624 | tf_op jit(solution)/shard_map/all_gather | solution.py:33
  70.6 9.4 %convert_add_fusion = f32[2,4096,256]{1,2,0:T(8,128)S(1)} fusion(bf16[2,1024,256]{2,1,0:T(8,128)(2,1)S(1)} %copy-done, bf16[1024,4096]{1,0:T(8,128)(2,1)} %all-gather.2.cloned.1.call-done, bf16[1,2,4096,256]{2,3,1,0:T(8,128)(2,1)} %copy.9), kind=kOutput, calls=%fused_computation.2 | convolution fusion | flops 4301258752 | bytes 22020096 | tf_op jit(solution)/shard_map/td,mtc->mdc/dot_general | solution.py:31
  80.0 4.3 %fusion.19 = f32[1,32,256]{2,1,0:T(8,128)} fusion(f32[2,4096,256]{1,2,0:T(8,128)S(1)} %convert_add_fusion, f32[2,32,4096]{2,1,0:T(8,128)S(1)} %copy-done.5), kind=kOutput, calls=%fused_computation.22 | convolution fusion | flops 402653184 | bytes 4751360 | tf_op jit(solution)/shard_map/mdc,mrd->mrc/dot_general | solution.py:14
  84.3 4.3 %fusion.16 = f32[1,32,256]{2,1,0:T(8,128)} fusion(f32[2,4096,256]{1,2,0:T(8,128)S(1)} %convert_add_fusion, f32[2,32,4096]{2,1,0:T(8,128)S(1)} %copy-done.5), kind=kOutput, calls=%fused_computation.21 | convolution fusion | flops 402653184 | bytes 4751360 | tf_op jit(solution)/shard_map/mdc,mrd->mrc/dot_general | solution.py:14
  88.7 68.8 %all-reduce.8.cloned.1.call-done = (f32[1,32,256]{2,1,0:T(8,128)}, f32[1,32,256]{2,1,0:T(8,128)}) async-done(((f32[1,32,256]{2,1,0:T(8,128)}, f32[1,32,256]{2,1,0:T(8,128)}), (f32[1,32,256]{2,1,0:T(8,128)}, f32[1,32,256]{2,1,0:T(8,128)})) %all-reduce.8.cloned.1.call-update) | async-done | bytes 65552 | tf_op jit(solution)/shard_map/psum | solution.py:15
  159.6 10.5 %all-reduce.2 = (f32[1,32,32]{1,2,0:T(8,128)S(1)}, f32[1,32,32]{1,2,0:T(8,128)S(1)}) all-reduce(f32[1,32,32]{1,2,0:T(8,128)S(1)} %convolution_bitcast_fusion.4, f32[1,32,32]{1,2,0:T(8,128)S(1)} %convolution_bitcast_fusion.5), channel_id=1, replica_groups=mesh['dp'=8,'tensor'=4] {'tensor'}, use_global_device_ids=true, to_apply=%region_7.0 | all-reduce | flops 2048 | bytes 16384 | tf_op jit(solution)/shard_map/psum | solution.py:16
  170.2 2.9 custom-call.10
  174.4 2.4 custom-call.11
  176.9 1.0 fusion.28
  177.9 2.9 custom-call.8
  182.1 2.4 custom-call.9
  184.6 1.0 fusion.31
  185.6 5.5 %convolution_bitcast_fusion.3 = f32[1,32,4096]{2,1,0:T(8,128)} fusion(f32[32,256]{1,0:T(8,128)S(1)} %fusion.31, f32[2,4096,256]{1,2,0:T(8,128)} %copy-done.2), kind=kOutput, calls=%fused_computation.10 | convolution fusion | flops 402653184 | bytes 4751360 | tf_op jit(solution)/shard_map/mdc,mrc->mrd/dot_general | solution.py:21
  191.1 5.5 %convolution_bitcast_fusion.2 = f32[1,32,4096]{2,1,0:T(8,128)} fusion(f32[32,256]{1,0:T(8,128)S(1)} %fusion.28, f32[2,4096,256]{1,2,0:T(8,128)} %copy-done.2), kind=kOutput, calls=%fused_computation.9 | convolution fusion | flops 402653184 | bytes 4751360 | tf_op jit(solution)/shard_map/mdc,mrc->mrd/dot_general | solution.py:21
  196.6 36.2 %all-reduce.12.cloned.1.call-done = (f32[1,32,4096]{2,1,0:T(8,128)}, f32[1,32,4096]{2,1,0:T(8,128)}) async-done(((f32[1,32,4096]{2,1,0:T(8,128)}, f32[1,32,4096]{2,1,0:T(8,128)}), (f32[1,32,4096]{2,1,0:T(8,128)}, f32[1,32,4096]{2,1,0:T(8,128)})) %all-reduce.12.cloned.1.call-update) | async-done | bytes 1048592 | tf_op jit(solution)/shard_map/psum | solution.py:22
  232.9 8.9 %bitcast_convert_fusion = bf16[1024,4096]{1,0:T(8,128)(2,1)} fusion(bf16[2,1024,256]{2,1,0:T(8,128)(2,1)S(1)} %copy-done, bf16[2,4096,256]{2,1,0:T(8,128)(2,1)} %param.9), kind=kOutput, calls=%fused_computation | convolution fusion | flops 4299161600 | bytes 13631488 | tf_op jit(solution)/shard_map/mtc,mdc->td/dot_general | solution.py:40
  241.9 73.6 %all-reduce.10.cloned.1.call-done = (f32[1,32,4096]{2,1,0:T(8,128)}, f32[1,32,4096]{2,1,0:T(8,128)}) async-done(((f32[1,32,4096]{2,1,0:T(8,128)}, f32[1,32,4096]{2,1,0:T(8,128)}), (f32[1,32,4096]{2,1,0:T(8,128)}, f32[1,32,4096]{2,1,0:T(8,128)})) %all-reduce.10.cloned.1.call-update) | async-done | bytes 1048592 | tf_op jit(solution)/shard_map/psum | solution.py:23
  315.5 5.5 %fusion.4 = f32[1,4096,256]{1,2,0:T(8,128)S(1)} fusion(f32[32,256]{1,0:T(8,128)S(1)} %fusion.31, f32[2,4096,256]{1,2,0:T(8,128)} %copy-done.2, f32[1,32,4096]{2,1,0:T(8,128)} %get-tuple-element.11), kind=kOutput, calls=%fused_computation.7 | convolution fusion | flops 403832832 | bytes 8945664 | tf_op jit(solution)/shard_map/mrd,mrc->mdc/dot_general | solution.py:25
  321.0 5.4 %fusion.5 = f32[1,4096,256]{1,2,0:T(8,128)S(1)} fusion(f32[32,256]{1,0:T(8,128)S(1)} %fusion.28, f32[2,4096,256]{1,2,0:T(8,128)} %copy-done.2, f32[1,32,4096]{2,1,0:T(8,128)S(1)} %copy-done.4), kind=kOutput, calls=%fused_computation.8 | convolution fusion | flops 403832832 | bytes 8945664 | tf_op jit(solution)/shard_map/mrd,mrc->mdc/dot_general | solution.py:25
  326.4 5.5 %maximum_bitcast_fusion = f32[1,2,4096,256]{2,3,1,0:T(8,128)} fusion(f32[1,4096,256]{1,2,0:T(8,128)S(1)} %fusion.5, f32[1,4096,256]{1,2,0:T(8,128)S(1)} %fusion.4), kind=kLoop, calls=%fused_computation.1 | loop fusion | flops 2097152 | bytes 16777216 | tf_op jit(solution)/shard_map/broadcast_in_dim | solution.py:51
  331.9 9.1 %copy.16 = f32[1,2,4096,256]{3,2,1,0:T(8,128)} copy(f32[1,2,4096,256]{2,3,1,0:T(8,128)} %maximum_bitcast_fusion) | data formatting | bytes 16777216
  341.1 1.0 pad_maximum_fusion
  342.1 47.7 %reduce-scatter.2.cloned.1.call-done = bf16[256,4096]{1,0:T(8,128)(2,1)} async-done(((bf16[1024,4096]{1,0:T(8,128)(2,1)}), bf16[256,4096]{1,0:T(8,128)(2,1)}) %reduce-scatter.2.cloned.1.call-update) | async-done | bytes 2097168 | tf_op jit(solution)/shard_map/reduce_scatter | solution.py:39
  (35 shorter events, 5.8 us)
Async XLA Ops:
  7.2 63.4 %copy-start = (bf16[2,1024,256]{2,1,0:T(8,128)(2,1)S(1)}, bf16[2,1024,256]{2,1,0:T(8,128)(2,1)}, u32[]{:S(2)}) copy-start(bf16[2,1024,256]{2,1,0:T(8,128)(2,1)} %param.10) | copy-start | bytes 3145732
  7.2 63.4 %all-gather.2.cloned.1.call-start = ((), (), s32[]{:S(2)}) async-start(), calls=%async_computation.1 | async-start | bytes 10485760 | tf_op jit(solution)/shard_map/all_gather | solution.py:33
  7.9 149.6 %all-reduce.8.cloned.1.call-start = ((), (), s32[]{:S(2)}) async-start(), calls=%async_computation.3 | async-start | bytes 131072 | tf_op jit(solution)/shard_map/psum | solution.py:15
  14.3 65.7 %copy-start.5 = (f32[2,32,4096]{2,1,0:T(8,128)S(1)}, f32[2,32,4096]{2,1,0:T(8,128)}, u32[]{:S(2)}) copy-start(f32[2,32,4096]{2,1,0:T(8,128)} %param.12) | copy-start | bytes 3145732
  80.0 4.3 %copy-start.2 = (f32[2,4096,256]{1,2,0:T(8,128)}, f32[2,4096,256]{1,2,0:T(8,128)S(1)}, u32[]{:S(2)}) copy-start(f32[2,4096,256]{1,2,0:T(8,128)S(1)} %convert_add_fusion) | copy-start | bytes 25165828
  88.7 144.2 %all-reduce.12.cloned.1.call-start = ((), (), s32[]{:S(2)}) async-start(), calls=%async_computation.5 | async-start | bytes 2097152 | tf_op jit(solution)/shard_map/psum | solution.py:22
  196.5 119.0 %all-reduce.10.cloned.1.call-start = ((), (), s32[]{:S(2)}) async-start(), calls=%async_computation.4 | async-start | bytes 2097152 | tf_op jit(solution)/shard_map/psum | solution.py:23
  232.9 156.9 %reduce-scatter.2.cloned.1.call-start = ((), (), s32[]{:S(2)}) async-start(), calls=%async_computation.2 | async-start | bytes 10485760 | tf_op jit(solution)/shard_map/reduce_scatter | solution.py:39
  315.5 5.5 %copy-start.4 = (f32[1,32,4096]{2,1,0:T(8,128)S(1)}, f32[1,32,4096]{2,1,0:T(8,128)}, u32[]{:S(2)}) copy-start(f32[1,32,4096]{2,1,0:T(8,128)} %get-tuple-element.10) | copy-start | bytes 1572868
  326.4 63.4 %copy-start.1 = (bf16[2,1024,256]{2,1,0:T(8,128)(2,1)S(1)}, bf16[2,1024,256]{2,1,0:T(8,128)(2,1)}, u32[]{:S(2)}) copy-start(bf16[2,1024,256]{2,1,0:T(8,128)(2,1)} %param.10) | copy-start | bytes 3145732
  331.9 9.1 %copy-start.3 = (f32[1,32,4096]{2,1,0:T(8,128)S(1)}, f32[1,32,4096]{2,1,0:T(8,128)}, u32[]{:S(2)}) copy-start(f32[1,32,4096]{2,1,0:T(8,128)} %get-tuple-element.11) | copy-start | bytes 1572868
Sparse Core Ops, SparseCore 0:
  9.6 60.9 all-gather.1
  88.8 68.7 all-reduce.7
  196.7 36.1 all-reduce.11
  236.7 78.8 all-reduce.9
  318.5 71.2 reduce-scatter.1
where the time goes:
time: 397 us; the launch traced here: 396 us
  waiting for transfers between devices  283 us (71%)
  matrix products  52.8 us (13%)
  other arithmetic  19.9 us (5%)
  local copies, waits for them, and re-layouts  15.6 us (4%)
  between operations  13.9 us (4%)
  blocking collectives  10.5 us (3%)
    psum x1, waiting for transfers between devices, compress(): right_total = lax.psum(right_total, 'dp')  73.6 us
    psum x1, waiting for transfers between devices, compress(): left_sum = lax.psum(projected, 'dp')  68.8 us
    all_gather x1, waiting for transfers between devices, per_device(): lax.all_gather(layer_input, 'tensor', axis=0, tiled=True)  56.3 us
    reduce_scatter x1, waiting for transfers between devices, per_device(): lax.psum_scatter(jnp.einsum('mtc,mdc->td', portion, kv_weight, preferred_...  47.7 us
    psum x1, waiting for transfers between devices, compress(): right_total = lax.psum(right_local, 'tensor')  36.2 us
    unnamed x14, local copies, waits for them, and re-layouts  15.4 us
    dot_general x2, matrix products, compress(): jnp.einsum('mdc,mrc->mrd', moments, ortho_basis, precision=highest)  10.9 us
    dot_general x2, matrix products, compress(): jnp.einsum('mrd,mrc->mdc', right_mean, ortho_basis, precision=highest)  10.9 us
  transfers between devices with their start and end apart: 5, of which 5 were waited for; matrix products, arithmetic and copies ran while one was open for 11% of the time, Pallas kernels for 0%

commit v1 on v0

--- a/solution.py
+++ b/solution.py
@@ -3,9 +3,346 @@
 import jax
 import jax.numpy as jnp
 from jax import lax
+from jax.experimental import pallas as pl
+from jax.experimental.pallas import tpu as pltpu
 from jax.sharding import PartitionSpec as P
 
 TOKENS = 1024
+SCALE = TOKENS ** (-0.5)
+F32, BF16 = jnp.float32, jnp.bfloat16
+VMEM_LIMIT = 48 * 1024 * 1024
+NN = (((1,), (0,)), ((), ()))
+NT = (((1,), (1,)), ((), ()))
+TN = (((0,), (0,)), ((), ()))
+HIGHEST = lax.Precision.HIGHEST
+
+
+def mm(a, b, dims, precision=None):
+    return lax.dot_general(a, b, dims, precision=precision, preferred_element_type=F32)
+
+
+def split(value, terms):
+    parts, rest = [], value
+    for _ in range(terms):
+        part = rest.astype(BF16)
+        parts.append(part)
+        rest = rest - part.astype(F32)
+    return jnp.concatenate(parts, axis=0)
+
+
+def split_mm(a, b, dims, terms):
+    rows = a.shape[0]
+    product = mm(split(a, terms), b, dims)
+    total = product[:rows]
+    for k in range(1, terms):
+        total = total + product[k * rows : (k + 1) * rows]
+    return total
+
+
+def params(*semantics):
+    return pltpu.CompilerParams(
+        vmem_limit_bytes=VMEM_LIMIT,
+        dimension_semantics=semantics if semantics else None,
+    )
+
+
+def cost(flops, nbytes):
+    return pl.CostEstimate(flops=int(flops), bytes_accessed=int(nbytes), transcendentals=0)
+
+
+def project_kernel(x_ref, r_ref, y_ref):
+    modes, rank, chunk = r_ref.shape
+    term = split_mm(r_ref[...].reshape(modes * rank, chunk), x_ref[...], NT, 3)
+
+    @pl.when(pl.program_id(0) == 0)
+    def _():
+        y_ref[...] = term
+
+    @pl.when(pl.program_id(0) > 0)
+    def _():
+        y_ref[...] += term
+
+
+def project(x, r, chunk=1024):
+    rows, depth = x.shape
+    modes, rank, _ = r.shape
+    return pl.pallas_call(
+        project_kernel,
+        grid=(depth // chunk,),
+        in_specs=[
+            pl.BlockSpec((rows, chunk), lambda i: (0, i)),
+            pl.BlockSpec((modes, rank, chunk), lambda i: (0, 0, i)),
+        ],
+        out_specs=pl.BlockSpec((modes * rank, rows), lambda i: (0, 0)),
+        out_shape=jax.ShapeDtypeStruct((modes * rank, rows), F32),
+        compiler_params=params("arbitrary"),
+        cost_estimate=cost(6 * rows * depth * modes * rank, x.nbytes + r.nbytes),
+        name="project",
+    )(x, r)
+
+
+def feedback_kernel(r_ref, e_ref, out_ref):
+    term = split_mm(r_ref[0], e_ref[0], NN, 3)
+
+    @pl.when(pl.program_id(1) == 0)
+    def _():
+        out_ref[...] = term
+
+    @pl.when(pl.program_id(1) > 0)
+    def _():
+        out_ref[...] += term
+
+
+def feedback(r, e, chunk=2048):
+    modes, rank, depth = r.shape
+    cols = e.shape[-1]
+    return pl.pallas_call(
+        feedback_kernel,
+        grid=(modes, depth // chunk),
+        in_specs=[
+            pl.BlockSpec((1, rank, chunk), lambda m, i: (m, 0, i)),
+            pl.BlockSpec((1, chunk, cols), lambda m, i: (m, i, 0)),
+        ],
+        out_specs=pl.BlockSpec((rank, cols), lambda m, i: (m, 0)),
+        out_shape=jax.ShapeDtypeStruct((modes * rank, cols), F32),
+        compiler_params=params("arbitrary", "arbitrary"),
+        cost_estimate=cost(6 * modes * rank * depth * cols, r.nbytes + e.nbytes),
+        name="feedback",
+    )(r, e)
+
+
+def rows_of(t_ref, j, rows):
+    return pl.ds(pl.multiple_of((t_ref[0] ^ j) * rows, rows), rows)
+
+
+def left_kernel(t_ref, y0, y1, y2, y3, g_ref, e_ref, out_ref):
+    modes = g_ref.shape[0]
+    rank, rows = y0.shape[0] // modes, y0.shape[1]
+    for m in range(modes):
+        at = slice(m * rank, (m + 1) * rank)
+        total = 0.0
+        for j, y in enumerate((y0, y1, y2, y3)):
+            total = total + split_mm(y[at, :], g_ref[m, rows_of(t_ref, j, rows), :], NN, 3)
+        out_ref[at, :] = total * SCALE + e_ref[at, :]
+
+
+SMEM = pl.BlockSpec(memory_space=pltpu.SMEM)
+VMEM = pl.BlockSpec(memory_space=pltpu.VMEM)
+
+
+def left_local(t, ys, g, e):
+    return pl.pallas_call(
+        left_kernel,
+        in_specs=[SMEM] + [VMEM] * 6,
+        out_specs=VMEM,
+        out_shape=jax.ShapeDtypeStruct(e.shape, F32),
+        compiler_params=params(),
+        cost_estimate=cost(6 * e.size * 1024, g.nbytes),
+        name="left",
+    )(t, *ys, g, e)
+
+
+def spread_kernel(t_ref, left_ref, g_ref, keep_ref, send_ref):
+    modes = g_ref.shape[0]
+    rank = left_ref.shape[0] // modes
+    rows = g_ref.shape[1] // 4
+    for j, (ref, at) in enumerate(((keep_ref, 0), (send_ref, 0), (keep_ref, 1), (send_ref, 1))):
+        for m in range(modes):
+            top = (at * modes + m) * rank
+            ref[top : top + rank, :] = split_mm(
+                left_ref[m * rank : (m + 1) * rank, :], g_ref[m, rows_of(t_ref, j, rows), :], NT, 3
+            )
+    zero = jnp.zeros((rank, left_ref.shape[1]), F32)
+    a, b = left_ref[0:rank, :], left_ref[rank : 2 * rank, :]
+    gram = mm(a, jnp.concatenate([a, zero, zero, zero], axis=0), NT, HIGHEST)
+    gram = gram + mm(b, jnp.concatenate([zero, zero, b, zero], axis=0), NT, HIGHEST)
+    top = 2 * modes * rank
+    for ref in (keep_ref, send_ref):
+        ref[top:, 0:128] = gram
+        ref[top:, 128:] = jnp.zeros((rank, rows - 128), F32)
+
+
+def spread(t, left, g):
+    shape = jax.ShapeDtypeStruct((2 * left.shape[0] + left.shape[0] // 2, g.shape[1] // 4), F32)
+    return pl.pallas_call(
+        spread_kernel,
+        in_specs=[SMEM, VMEM, VMEM],
+        out_specs=[VMEM, VMEM],
+        out_shape=[shape, shape],
+        compiler_params=params(),
+        cost_estimate=cost(6 * left.size * 1024, g.nbytes),
+        name="spread",
+    )(t, left, g)
+
+
+def solve_kernel(sum_ref, got_ref, left_ref, z_ref, b_ref):
+    modes = 2
+    rank = left_ref.shape[0] // modes
+    n = modes * rank
+    gram = sum_ref[n:, 0:128] + got_ref[n:, 0:128]
+    row = lax.broadcasted_iota(jnp.int32, (rank, 128), 0)
+    lane = lax.broadcasted_iota(jnp.int32, (rank, 128), 1)
+    ones = jnp.where((lane == row + rank) | (lane == row + 3 * rank), 1.0, 0.0)
+    a = jnp.where((lane // rank) % 2 == 0, gram, ones)
+    low = lane < 2 * rank
+    scale = jnp.zeros((rank, 128), F32)
+    for k in range(rank):
+        pivot_row = a[k : k + 1, :]
+        column = jnp.where(low, a[:, k : k + 1], a[:, 2 * rank + k : 2 * rank + k + 1])
+        pivot = column[k : k + 1, :]
+        inverse = 1.0 / pivot
+        scale = jnp.where(row == k, lax.rsqrt(pivot), scale)
+        a = jnp.where(row > k, a - column * (inverse * pivot_row), a)
+    a = a * scale
+    zero = jnp.zeros((rank, left_ref.shape[1]), F32)
+    z = (sum_ref[0:n, :] + got_ref[0:n, :]) * SCALE
+    for m in range(modes):
+        part = jnp.where(lane // rank == 2 * m + 1, a, 0.0)
+        at = slice(m * rank, (m + 1) * rank)
+        for value, ref in ((z[at], z_ref), (left_ref[at, :], b_ref)):
+            stacked = [zero] * 4
+            stacked[2 * m + 1] = value
+            ref[at, :] = mm(part, jnp.concatenate(stacked, axis=0), NN, HIGHEST)
+
+
+def solve(summed, got, left):
+    shape = jax.ShapeDtypeStruct(left.shape, F32)
+    return pl.pallas_call(
+        solve_kernel,
+        in_specs=[VMEM, VMEM, VMEM],
+        out_specs=[VMEM, VMEM],
+        out_shape=[shape, shape],
+        compiler_params=params(),
+        cost_estimate=cost(10**7, 10**7),
+        name="solve",
+    )(summed, got, left)
+
+
+def right_kernel(h_ref, z_ref, b_ref, x_ref, e_ref, out_ref):
+    modes = e_ref.shape[0]
+    rank = z_ref.shape[0] // modes
+    out_ref[...] = split_mm(z_ref[...], x_ref[...], NN, 2)
+    for m in range(modes):
+        at = slice(m * rank, (m + 1) * rank)
+        out_ref[at, :] += split_mm(b_ref[at, :], e_ref[m], NT, 2)
+
+
+def right_half(half, z, b, x, e, chunk=512):
+    rows, depth = x.shape
+    modes, _, cols = e.shape
+    steps = depth // 2 // chunk
+    return pl.pallas_call(
+        right_kernel,
+        grid_spec=pltpu.PrefetchScalarGridSpec(
+            num_scalar_prefetch=1,
+            grid=(steps,),
+            in_specs=[
+                pl.BlockSpec(z.shape, lambda i, h: (0, 0)),
+                pl.BlockSpec(b.shape, lambda i, h: (0, 0)),
+                pl.BlockSpec((rows, chunk), lambda i, h: (0, h[0] * steps + i)),
+                pl.BlockSpec((modes, chunk, cols), lambda i, h: (0, h[0] * steps + i, 0)),
+            ],
+            out_specs=pl.BlockSpec((z.shape[0], chunk), lambda i, h: (0, i)),
+        ),
+        out_shape=jax.ShapeDtypeStruct((z.shape[0], depth // 2), F32),
+        compiler_params=params("arbitrary"),
+        cost_estimate=cost(4 * depth * rows * 128, x.nbytes // 2 + e.nbytes // 2),
+        name="right",
+    )(half, z, b, x, e)
+
+
+def moment_kernel(t_ref, x0, x1, x2, x3, g_ref, e_ref, out_ref):
+    modes = g_ref.shape[0]
+    rows = x0.shape[0]
+    for m in range(modes):
+        total = 0.0
+        for j, x in enumerate((x0, x1, x2, x3)):
+            total = total + mm(x[...], g_ref[m, rows_of(t_ref, j, rows), :], TN)
+        out_ref[m] = total * SCALE + e_ref[m].astype(F32)
+
+
+def moment(t, xs, g, e, chunk=512):
+    rows, depth = xs[0].shape
+    modes, tokens, cols = g.shape
+    return pl.pallas_call(
+        moment_kernel,
+        grid=(depth // chunk,),
+        in_specs=[SMEM]
+        + [pl.BlockSpec((rows, chunk), lambda i: (0, i))] * 4
+        + [
+            pl.BlockSpec((modes, tokens, cols), lambda i: (0, 0, 0)),
+            pl.BlockSpec((modes, chunk, cols), lambda i: (0, i, 0)),
+        ],
+        out_specs=pl.BlockSpec((modes, chunk, cols), lambda i: (0, i, 0)),
+        out_shape=jax.ShapeDtypeStruct((modes, depth, cols), F32),
+        compiler_params=params("arbitrary"),
+        cost_estimate=cost(2 * tokens * depth * modes * cols, 24 * 2**20),
+        name="moment",
+    )(t, *xs, g, e)
+
+
+def error_kernel(m_ref, right_ref, b_ref, out_ref):
+    modes = m_ref.shape[0]
+    rank = b_ref.shape[0] // modes
+    for m in range(modes):
+        at = slice(m * rank, (m + 1) * rank)
+        high = right_ref[at, :].astype(BF16)
+        b = b_ref[at, :]
+        b0 = b.astype(BF16)
+        b1 = (b - b0.astype(F32)).astype(BF16)
+        product = mm(jnp.concatenate([high, high], axis=0), jnp.concatenate([b0, b1], axis=0), TN)
+        out_ref[m] = m_ref[m] - product
+
+
+def error_after(moments, right, b, chunk=512):
+    modes, depth, cols = moments.shape
+    spec = pl.BlockSpec((modes, chunk, cols), lambda i: (0, i, 0))
+    return pl.pallas_call(
+        error_kernel,
+        grid=(depth // chunk,),
+        in_specs=[
+            spec,
+            pl.BlockSpec((right.shape[0], chunk), lambda i: (0, i)),
+            pl.BlockSpec(b.shape, lambda i: (0, 0)),
+        ],
+        out_specs=spec,
+        out_shape=jax.ShapeDtypeStruct(moments.shape, F32),
+        input_output_aliases={0: 0},
+        compiler_params=params("arbitrary"),
+        cost_estimate=cost(2 * depth * modes * cols * 64, 2 * moments.nbytes),
+        name="error_after",
+    )(moments, right, b)
+
+
+def grad_kernel(j, n, t_ref, g_ref, w_ref, *refs):
+    more, out_ref = refs[:n], refs[n]
+    rows = out_ref.shape[0]
+    at = rows_of(t_ref, j, rows)
+    total = mm(g_ref[0, at, :], w_ref[0], NT) + mm(g_ref[1, at, :], w_ref[1], NT)
+    for ref in more:
+        total = total + ref[...].astype(F32)
+    out_ref[...] = total.astype(BF16)
+
+
+def grad_block(t, g, w, j, more=(), chunk=1024):
+    modes, depth, cols = w.shape
+    rows = g.shape[1] // 4
+    spec = pl.BlockSpec((rows, chunk), lambda i: (0, i))
+    return pl.pallas_call(
+        partial(grad_kernel, j, len(more)),
+        grid=(depth // chunk,),
+        in_specs=[
+            SMEM,
+            pl.BlockSpec(g.shape, lambda i: (0, 0, 0)),
+            pl.BlockSpec((modes, chunk, cols), lambda i: (0, i, 0)),
+        ]
+        + [spec] * len(more),
+        out_specs=spec,
+        out_shape=jax.ShapeDtypeStruct((rows, depth), BF16),
+        compiler_params=params("arbitrary"),
+        cost_estimate=cost(2 * rows * depth * modes * cols, w.nbytes),
+        name="grad_block",
+    )(t, g, w, *more)
 
 
 def compress(moments, right_prev):
@@ -26,7 +363,7 @@
     return (moments - approximation, right_mean)
 
 
-def per_device(layer_input, kv_weight, kv_cotangent, error_before, right_factor):
+def any_mesh(layer_input, kv_weight, kv_cotangent, error_before, right_factor):
     portion = kv_cotangent
     weight_grad = jnp.einsum(
         "td,mtc->mdc",
@@ -51,9 +388,81 @@
     return (errors[None], right_next, input_sum)
 
 
+def per_device(layer_input, kv_weight, kv_cotangent, error_before, right_factor):
+    tensor, replicas = lax.axis_size("tensor"), lax.axis_size("dp")
+    t = lax.axis_index("tensor").astype(jnp.int32)
+    t_arr = t.reshape(1)
+    core, xpos = t % 2, t // 2
+    errors = error_before[0]
+    n = 2 * right_factor.shape[1]
+
+    def over(value, axis, bit):
+        size = tensor if axis == "tensor" else replicas
+        return lax.ppermute(value, axis, [(i, i ^ bit) for i in range(size)])
+
+    y0 = project(layer_input, right_factor)
+    x1 = over(layer_input, "tensor", 1)
+    x2 = over(layer_input, "tensor", 2)
+    y1 = over(y0, "tensor", 1)
+    pair = over(jnp.concatenate([y0, y1], axis=0), "tensor", 2)
+    e = feedback(right_factor, errors)
+    left = left_local(t_arr, (y0, y1, pair[:n], pair[n:]), kv_cotangent, e)
+    bit = 1
+    while bit < replicas:
+        left = left + over(left, "dp", bit)
+        bit *= 2
+
+    keep, send = spread(t_arr, left, kv_cotangent)
+    summed = keep + over(send, "tensor", 1)
+    mine, away = summed[:n], summed[n:]
+    got = over(away, "tensor", 2)
+    whole = jnp.concatenate([mine, away[n:]], axis=0)
+    z, b = solve(whole, got, left)
+
+    half_send = right_half((1 - core).reshape(1), z, b, layer_input, errors)
+    half_got = over(half_send, "tensor", 1)
+    half = right_half(core.reshape(1), z, b, layer_input, errors) + half_got
+    quarter = half.shape[1] // 2
+    give = lax.dynamic_slice_in_dim(half, (1 - xpos) * quarter, quarter, 1).astype(BF16)
+    own = lax.dynamic_slice_in_dim(half, xpos * quarter, quarter, 1)
+    own = own + over(give, "tensor", 2).astype(F32)
+    bit = 1
+    while bit < replicas:
+        rounded = lax.optimization_barrier(own.astype(BF16))
+        own = rounded.astype(F32) + over(rounded, "dp", bit).astype(F32)
+        bit *= 2
+    rounded = lax.optimization_barrier((own * (1.0 / replicas)).astype(BF16))
+    other = over(rounded, "tensor", 2)
+    both = jnp.where(
+        xpos == 0,
+        jnp.concatenate([rounded, other], axis=1),
+        jnp.concatenate([other, rounded], axis=1),
+    )
+    sibling = over(both, "tensor", 1)
+    right = jnp.where(
+        core == 0,
+        jnp.concatenate([both, sibling], axis=1),
+        jnp.concatenate([sibling, both], axis=1),
+    ).astype(F32)
+
+    p3 = grad_block(t_arr, kv_cotangent, kv_weight, 3)
+    s2 = grad_block(t_arr, kv_cotangent, kv_weight, 2, (over(p3, "tensor", 1),))
+    far = over(s2, "tensor", 2)
+    p1 = grad_block(t_arr, kv_cotangent, kv_weight, 1)
+    near = over(p1, "tensor", 1)
+    input_grad = grad_block(t_arr, kv_cotangent, kv_weight, 0, (near, far))
+
+    x3 = over(x2, "tensor", 1)
+    moments = moment(t_arr, (layer_input, x1, x2, x3), kv_cotangent, errors)
+    after = error_after(moments, right, b)
+    return (after[None], right.reshape(right_factor.shape), input_grad)
+
+
 def solution(mesh):
+    sizes = mesh.shape
+    fits = sizes["tensor"] == 4 and sizes["dp"] & (sizes["dp"] - 1) == 0
     return jax.shard_map(
-        per_device,
+        per_device if fits else any_mesh,
         mesh=mesh,
         in_specs=(
             P(("dp", "tensor"), None),

time: 397 us -> 189 us (0.48)
  waiting for transfers between devices: 283 us -> 91.6 us
  Pallas kernels: 0 us -> 59.5 us
  matrix products: 52.8 us -> 0 us
  starting transfers between devices: 0.2 us -> 24.2 us
  between operations: 13.9 us -> 0.81 us
  other arithmetic: 19.9 us -> 7.44 us
  local copies, waits for them, and re-layouts: 15.6 us -> 4.24 us
  blocking collectives: 10.5 us -> 0 us
    psum x3 -> x0, waiting for transfers between devices: 179 us -> none  [the longest x1 73.6 us: compress(): right_total = lax.psum(right_total, 'dp')]
    ppermute x0 -> x20, waiting for transfers between devices: none -> 91.6 us  [over(): return lax.ppermute(value, axis, [(i, i ^ bit) for i in range(size)])]
    pallas_call x0 -> x13, Pallas kernels: none -> 59.5 us  [the longest x4 20.7 us: grad_block(): pl.pallas_call(partial(grad_kernel, j, len(more)), grid=(depth // chunk,)...]
    all_gather x1 -> x0, waiting for transfers between devices: 56.3 us -> none  [per_device(): lax.all_gather(layer_input, 'tensor', axis=0, tiled=True)]
    dot_general x10 -> x0, matrix products: 50.8 us -> none  [the longest x2 10.9 us: compress(): jnp.einsum('mdc,mrc->mrd', moments, ortho_basis, precision=highest)]
    reduce_scatter x1 -> x0, waiting for transfers between devices: 47.7 us -> none  [per_device(): lax.psum_scatter(jnp.einsum('mtc,mdc->td', portion, kv_weight, preferred_...]
    ppermute x0 -> x20, starting transfers between devices: none -> 24.2 us  [over(): return lax.ppermute(value, axis, [(i, i ^ bit) for i in range(size)])]
    another operation x10 -> x0, other arithmetic: 13.3 us -> none  [the longest x6 7.18 us: compress(): factor = jnp.linalg.cholesky(gram_matrix)]
  transfers between devices with their start and end apart: 5 -> 20, of which waited for: 5 -> 11; matrix products, arithmetic and copies ran while one was open for 11% -> 4% of each run, Pallas kernels for 0% -> 27%
where the time goes in v1:
time: 189 us; the launch traced here: 188 us
  waiting for transfers between devices  91.6 us (48%)
  Pallas kernels  59.5 us (31%)
  starting transfers between devices  24.2 us (13%)
  other arithmetic  7.44 us (4%)
  local copies, waits for them, and re-layouts  4.24 us (2%)
    ppermute x20, waiting for transfers between devices, over(): return lax.ppermute(value, axis, [(i, i ^ bit) for i in range(size)])  91.6 us
    ppermute x20, starting transfers between devices, over(): return lax.ppermute(value, axis, [(i, i ^ bit) for i in range(size)])  24.2 us
    pallas_call x4, Pallas kernels, grad_block(): pl.pallas_call(partial(grad_kernel, j, len(more)), grid=(depth // chunk,)...  20.7 us
    pallas_call x1, Pallas kernels, moment(): pl.pallas_call(moment_kernel, grid=(depth // chunk,), in_specs=[SMEM] + [...  12 us
    pallas_call x1, Pallas kernels, error_after(): pl.pallas_call(error_kernel, grid=(depth // chunk,), in_specs=[spec, pl.B...  9.9 us
    pallas_call x2, Pallas kernels, right_half(): pl.pallas_call(right_kernel, grid_spec=pltpu.PrefetchScalarGridSpec(num_s...  7.65 us
    unnamed x10, local copies, waits for them, and re-layouts  4.2 us
  transfers between devices with their start and end apart: 20, of which 11 were waited for; matrix products, arithmetic and copies ran while one was open for 4% of the time, Pallas kernels for 27%

profile of v1, /device:TPU:0, one launch (start us, length us, event | category | flops | bytes accessed | tf_op | source)
XLA Modules:
  0.0 187.8 jit_solution(12314226308867362573)
XLA Ops:
  1.9 3.3 %project.1.y0 = f32[64,256]{1,0:T(8,128)S(1)} custom-call(bf16[256,4096]{1,0:T(8,128)(2,1)} %x_ref.5, f32[2,32,4096]{2,1,0:T(8,128)S(1)} %copy-done.2), custom_call_target="tpu_custom_call" | custom-call | flops 402653184 | bytes 3145728 | tf_op jit(solution)/shard_map/project/pallas_call | solution.py:69
  6.6 2.9 %collective-permute-start.4 = (f32[128,256]{1,0:T(8,128)S(1)}, f32[128,256]{1,0:T(8,128)S(1)}, u32[]{:S(2)}, u32[]{:S(2)}) collective-permute-start(f32[128,256]{1,0:T(8,128)S(1)} %pad_maximum_fusion), channel_id=1, source_target_pairs={{0,2},{1,3},{2,0},{3,1},{4,6},{5,7},{6,4},{7,5},{8,10},{9,11},{10,... | collective-permute-start | bytes 393224 | tf_op jit(solution)/shard_map/ppermute | solution.py:401
  9.6 2.2 %copy-done = bf16[1,2,4096,256]{3,2,1,0:T(8,128)(2,1)S(1)} copy-done((bf16[1,2,4096,256]{3,2,1,0:T(8,128)(2,1)S(1)}, bf16[1,2,4096,256]{3,2,1,0:T(8,128)(2,1)}, u32[]{:S(2)}) %copy-start) | copy-done | bytes 4194328
  14.1 2.1 %collective-permute-start.5 = (f32[64,256]{1,0:T(8,128)S(1)}, f32[64,256]{1,0:T(8,128)S(1)}, u32[]{:S(2)}, u32[]{:S(2)}) collective-permute-start(f32[64,256]{1,0:T(8,128)S(1)} %left.1), channel_id=1, source_target_pairs={{0,4},{4,0},{8,12},{12,8},{16,20},{20,16},{24,28},{28,24},{1,5},{5... | collective-permute-start | bytes 196616 | tf_op jit(solution)/shard_map/ppermute | solution.py:401
  16.2 2.2 %collective-permute-done.5 = f32[64,256]{1,0:T(8,128)S(1)} collective-permute-done((f32[64,256]{1,0:T(8,128)S(1)}, f32[64,256]{1,0:T(8,128)S(1)}, u32[]{:S(2)}, u32[]{:S(2)}) %collective-permute-start.5) | collective-permute-done | bytes 65568 | tf_op jit(solution)/shard_map/ppermute | solution.py:401
  18.5 2.1 %collective-permute-start.6 = (f32[64,256]{1,0:T(8,128)S(1)}, f32[64,256]{1,0:T(8,128)S(1)}, u32[]{:S(2)}, u32[]{:S(2)}) collective-permute-start(f32[64,256]{1,0:T(8,128)S(1)} %add.39), channel_id=1, source_target_pairs={{0,8},{4,12},{8,0},{12,4},{16,24},{20,28},{24,16},{28,20},{1,9},{5... | collective-permute-start | bytes 196616 | tf_op jit(solution)/shard_map/ppermute | solution.py:401
  20.6 2.2 %collective-permute-done.6 = f32[64,256]{1,0:T(8,128)S(1)} collective-permute-done((f32[64,256]{1,0:T(8,128)S(1)}, f32[64,256]{1,0:T(8,128)S(1)}, u32[]{:S(2)}, u32[]{:S(2)}) %collective-permute-start.6) | collective-permute-done | bytes 65568 | tf_op jit(solution)/shard_map/ppermute | solution.py:401
  22.9 3.2 %collective-permute-start.7 = (f32[64,256]{1,0:T(8,128)S(1)}, f32[64,256]{1,0:T(8,128)S(1)}, u32[]{:S(2)}, u32[]{:S(2)}) collective-permute-start(f32[64,256]{1,0:T(8,128)S(1)} %add.40), channel_id=1, source_target_pairs={{0,16},{4,20},{8,24},{12,28},{16,0},{20,4},{24,8},{28,12},{1,17},{... | collective-permute-start | bytes 196616 | tf_op jit(solution)/shard_map/ppermute | solution.py:401
  26.1 2.2 %collective-permute-done.7 = f32[64,256]{1,0:T(8,128)S(1)} collective-permute-done((f32[64,256]{1,0:T(8,128)S(1)}, f32[64,256]{1,0:T(8,128)S(1)}, u32[]{:S(2)}, u32[]{:S(2)}) %collective-permute-start.7) | collective-permute-done | bytes 65568 | tf_op jit(solution)/shard_map/ppermute | solution.py:401
  29.6 5.1 %grad_block.5 = bf16[256,4096]{1,0:T(8,128)(2,1)} custom-call(s32[1]{0:T(128)} %bitcast.t_ref, bf16[2,1024,256]{2,1,0:T(8,128)(2,1)S(1)} %copy-done.1, bf16[2,4096,256]{2,1,0:T(8,128)(2,1)} %w_ref.7), custom_call_target="tpu_custom_call" | custom-call | flops 1073741824 | bytes 4194304 | tf_op jit(solution)/shard_map/grad_block/pallas_call | solution.py:331
  37.9 22.4 %collective-permute-done.9.got_ref = f32[96,256]{1,0:T(8,128)S(1)} collective-permute-done((f32[96,256]{1,0:T(8,128)S(1)}, f32[96,256]{1,0:T(8,128)S(1)}, u32[]{:S(2)}, u32[]{:S(2)}) %collective-permute-start.9) | collective-permute-done | bytes 98336 | tf_op jit(solution)/shard_map/ppermute | solution.py:401
  60.4 3.0 %solve.1 = (f32[64,256]{1,0:T(8,128)S(1)}, f32[64,256]{1,0:T(8,128)S(1)}) custom-call(f32[96,256]{1,0:T(8,128)S(1)} %pad_maximum_fusion.1.sum_ref, f32[96,256]{1,0:T(8,128)S(1)} %collective-permute-done.9.got_ref, f32[64,256]{1,0:T(8,128)S(1)} %add.41.left_ref), custom_call_target="tpu_custom_call" | custom-call | flops 10000000 | bytes 10000000 | tf_op jit(solution)/shard_map/solve/pallas_call | solution.py:210
  63.3 4.3 %right.3 = f32[64,2048]{1,0:T(8,128)} custom-call(s32[1]{0:T(128)} %bitcast.3.h_ref, f32[64,256]{1,0:T(8,128)S(1)} %get-tuple-element.9.z_ref, f32[64,256]{1,0:T(8,128)S(1)} %get-tuple-element.10.b_ref, bf16[256,4096]{1,0:T(8,128)(2,1)} %x_ref.5, bf16[2,4096,256]{2,1,0:T(8,128)(2,1)} %bitcast.8), custom_call_target="tpu_custom_call" | custom-call | flops 536870912 | bytes 3145728 | tf_op jit(solution)/shard_map/right/pallas_call | solution.py:234
  67.6 3.3 %right.2 = f32[64,2048]{1,0:T(8,128)S(1)} custom-call(s32[1]{0:T(128)} %bitcast.2.h_ref, f32[64,256]{1,0:T(8,128)S(1)} %get-tuple-element.9.z_ref, f32[64,256]{1,0:T(8,128)S(1)} %get-tuple-element.10.b_ref, bf16[256,4096]{1,0:T(8,128)(2,1)} %x_ref.5, bf16[2,4096,256]{2,1,0:T(8,128)(2,1)} %bitcast.9), custom_call_target="tpu_custom_call" | custom-call | flops 536870912 | bytes 3145728 | tf_op jit(solution)/shard_map/right/pallas_call | solution.py:234
  74.7 4.2 %collective-permute-done.11 = bf16[64,1024]{1,0:T(8,128)(2,1)S(1)} collective-permute-done((bf16[64,1024]{1,0:T(8,128)(2,1)S(1)}, bf16[64,1024]{1,0:T(8,128)(2,1)S(1)}, u32[]{:S(2)}, u32[]{:S(2)}) %collective-permute-start.11) | collective-permute-done | bytes 131104 | tf_op jit(solution)/shard_map/ppermute | solution.py:401
  81.7 3.4 %collective-permute-done.12 = bf16[64,1024]{1,0:T(8,128)(2,1)S(1)} collective-permute-done((bf16[64,1024]{1,0:T(8,128)(2,1)S(1)}, bf16[64,1024]{1,0:T(8,128)(2,1)S(1)}, u32[]{:S(2)}, u32[]{:S(2)}) %collective-permute-start.12) | collective-permute-done | bytes 131104 | tf_op jit(solution)/shard_map/ppermute | solution.py:401
  87.5 2.7 %collective-permute-done.13 = bf16[64,1024]{1,0:T(8,128)(2,1)S(1)} collective-permute-done((bf16[64,1024]{1,0:T(8,128)(2,1)S(1)}, bf16[64,1024]{1,0:T(8,128)(2,1)S(1)}, u32[]{:S(2)}, u32[]{:S(2)}) %collective-permute-start.13) | collective-permute-done | bytes 131104 | tf_op jit(solution)/shard_map/ppermute | solution.py:401
  90.2 2.9 %collective-permute-start.14 = (bf16[64,1024]{1,0:T(8,128)(2,1)S(1)}, bf16[64,1024]{1,0:T(8,128)(2,1)S(1)}, u32[]{:S(2)}, u32[]{:S(2)}) collective-permute-start(bf16[64,1024]{1,0:T(8,128)(2,1)S(1)} %add_convert_fusion), channel_id=1, source_target_pairs={{0,16},{4,20},{8,24},{12,28},{16,0},{20,4},{24,8},{28,12},{1,17},{... | collective-permute-start | bytes 393224 | tf_op jit(solution)/shard_map/ppermute | solution.py:401
  93.0 5.1 %grad_block.4 = bf16[256,4096]{1,0:T(8,128)(2,1)} custom-call(s32[1]{0:T(128)} %bitcast.t_ref, bf16[2,1024,256]{2,1,0:T(8,128)(2,1)S(1)} %copy-done.1, bf16[2,4096,256]{2,1,0:T(8,128)(2,1)} %w_ref.7), custom_call_target="tpu_custom_call" | custom-call | flops 1073741824 | bytes 4194304 | tf_op jit(solution)/shard_map/grad_block/pallas_call | solution.py:331
  98.1 5.1 %grad_block.6 = bf16[256,4096]{1,0:T(8,128)(2,1)} custom-call(s32[1]{0:T(128)} %bitcast.t_ref, bf16[2,1024,256]{2,1,0:T(8,128)(2,1)S(1)} %copy-done.1, bf16[2,4096,256]{2,1,0:T(8,128)(2,1)} %w_ref.7, bf16[256,4096]{1,0:T(8,128)(2,1)S(1)} %collective-permute-done.18.refs_0_), custom_call_target="tpu_custom_call" | custom-call | flops 1073741824 | bytes 4194304 | tf_op jit(solution)/shard_map/grad_block/pallas_call | solution.py:331
  105.4 48.9 %collective-permute-done.15 = bf16[64,1024]{1,0:T(8,128)(2,1)S(1)} collective-permute-done((bf16[64,1024]{1,0:T(8,128)(2,1)S(1)}, bf16[64,1024]{1,0:T(8,128)(2,1)S(1)}, u32[]{:S(2)}, u32[]{:S(2)}) %collective-permute-start.15) | collective-permute-done | bytes 131104 | tf_op jit(solution)/shard_map/ppermute | solution.py:401
  160.4 12.0 %moment.1.m_ref = f32[2,4096,256]{2,1,0:T(8,128)} custom-call(s32[1]{0:T(128)} %bitcast.t_ref, bf16[256,4096]{1,0:T(8,128)(2,1)} %x_ref.5, bf16[256,4096]{1,0:T(8,128)(2,1)} %collective-permute-done.x1, bf16[256,4096]{1,0:T(8,128)(2,1)} %collective-permute-done.1.x2, bf16[256,4096]{1,0:T(8,128)(2,1)} %collective-permute-done.2.x3, ...), custom_call_target="tpu_custom_call" | custom-call | flops 4294967296 | bytes 25165824 | tf_op jit(solution)/shard_map/moment/pallas_call | solution.py:267
  172.4 9.9 %error_after.1 = f32[2,4096,256]{2,1,0:T(8,128)} custom-call(f32[2,4096,256]{2,1,0:T(8,128)} %moment.1.m_ref, f32[64,4096]{1,0:T(8,128)S(1)} %fusion.right_ref, f32[64,256]{1,0:T(8,128)S(1)} %get-tuple-element.10.b_ref), custom_call_target="tpu_custom_call", output_to_operand_aliasing={{}: (0, {})} | custom-call | flops 268435456 | bytes 16777216 | tf_op jit(solution)/shard_map/error_after/pallas_call | solution.py:300
  182.3 5.5 %grad_block.7 = bf16[256,4096]{1,0:T(8,128)(2,1)} custom-call(s32[1]{0:T(128)} %bitcast.t_ref, bf16[2,1024,256]{2,1,0:T(8,128)(2,1)S(1)} %copy-done.1, bf16[2,4096,256]{2,1,0:T(8,128)(2,1)} %w_ref.7, bf16[256,4096]{1,0:T(8,128)(2,1)} %collective-permute-done.17.refs_0_, bf16[256,4096]{1,0:T(8,128)(2,1)S(1)} %collective-permute-done.19.refs_1_), custom_call_target="tpu_custom_call" | custom-call | flops 1073741824 | bytes 4194304 | tf_op jit(solution)/shard_map/grad_block/pallas_call | solution.py:331
  (59 shorter events, 26.7 us)
Async XLA Ops:
  0.6 1.2 copy-start.2
  1.9 7.7 %copy-start.3 = (f32[2,32,4096]{2,1,0:T(8,128)S(1)}, f32[2,32,4096]{2,1,0:T(8,128)}, u32[]{:S(2)}) copy-start(f32[2,32,4096]{2,1,0:T(8,128)} %r_ref.3) | copy-start | bytes 3145732
  5.2 1.4 collective-permute-start.3
  6.6 7.2 %collective-permute-start.4 = (f32[128,256]{1,0:T(8,128)S(1)}, f32[128,256]{1,0:T(8,128)S(1)}, u32[]{:S(2)}, u32[]{:S(2)}) collective-permute-start(f32[128,256]{1,0:T(8,128)S(1)} %pad_maximum_fusion), channel_id=1, source_target_pairs={{0,2},{1,3},{2,0},{3,1},{4,6},{5,7},{6,4},{7,5},{8,10},{9,11},{10,... | collective-permute-start | bytes 393224 | tf_op jit(solution)/shard_map/ppermute | solution.py:401
  9.5 77.5 %collective-permute-start.1 = (bf16[256,4096]{1,0:T(8,128)(2,1)}, bf16[256,4096]{1,0:T(8,128)(2,1)}, u32[]{:S(2)}, u32[]{:S(2)}) collective-permute-start(bf16[256,4096]{1,0:T(8,128)(2,1)} %x_ref.5), channel_id=1, source_target_pairs={{0,2},{1,3},{2,0},{3,1},{4,6},{5,7},{6,4},{7,5},{8,10},{9,11},{10,... | collective-permute-start | bytes 6291464 | tf_op jit(solution)/shard_map/ppermute | solution.py:401
  9.6 2.2 %copy-start = (bf16[1,2,4096,256]{3,2,1,0:T(8,128)(2,1)S(1)}, bf16[1,2,4096,256]{3,2,1,0:T(8,128)(2,1)}, u32[]{:S(2)}) copy-start(bf16[1,2,4096,256]{3,2,1,0:T(8,128)(2,1)} %param.8) | copy-start | bytes 12582916
  11.8 2.0 %copy-start.1 = (bf16[2,1024,256]{2,1,0:T(8,128)(2,1)S(1)}, bf16[2,1024,256]{2,1,0:T(8,128)(2,1)}, u32[]{:S(2)}) copy-start(bf16[2,1024,256]{2,1,0:T(8,128)(2,1)} %g_ref.13) | copy-start | bytes 3145732
  14.1 4.4 %collective-permute-start.5 = (f32[64,256]{1,0:T(8,128)S(1)}, f32[64,256]{1,0:T(8,128)S(1)}, u32[]{:S(2)}, u32[]{:S(2)}) collective-permute-start(f32[64,256]{1,0:T(8,128)S(1)} %left.1), channel_id=1, source_target_pairs={{0,4},{4,0},{8,12},{12,8},{16,20},{20,16},{24,28},{28,24},{1,5},{5... | collective-permute-start | bytes 196616 | tf_op jit(solution)/shard_map/ppermute | solution.py:401
  18.5 4.4 %collective-permute-start.6 = (f32[64,256]{1,0:T(8,128)S(1)}, f32[64,256]{1,0:T(8,128)S(1)}, u32[]{:S(2)}, u32[]{:S(2)}) collective-permute-start(f32[64,256]{1,0:T(8,128)S(1)} %add.39), channel_id=1, source_target_pairs={{0,8},{4,12},{8,0},{12,4},{16,24},{20,28},{24,16},{28,20},{1,9},{5... | collective-permute-start | bytes 196616 | tf_op jit(solution)/shard_map/ppermute | solution.py:401
  22.9 5.4 %collective-permute-start.7 = (f32[64,256]{1,0:T(8,128)S(1)}, f32[64,256]{1,0:T(8,128)S(1)}, u32[]{:S(2)}, u32[]{:S(2)}) collective-permute-start(f32[64,256]{1,0:T(8,128)S(1)} %add.40), channel_id=1, source_target_pairs={{0,16},{4,20},{8,24},{12,28},{16,0},{20,4},{24,8},{28,12},{1,17},{... | collective-permute-start | bytes 196616 | tf_op jit(solution)/shard_map/ppermute | solution.py:401
  29.6 5.6 %collective-permute-start.8 = (f32[160,256]{1,0:T(8,128)}, f32[160,256]{1,0:T(8,128)}, u32[]{:S(2)}, u32[]{:S(2)}) collective-permute-start(f32[160,256]{1,0:T(8,128)} %get-tuple-element.8), channel_id=1, source_target_pairs={{0,1},{1,0},{2,3},{3,2},{4,5},{5,4},{6,7},{7,6},{8,9},{9,8},{10,11... | collective-permute-start | bytes 491528 | tf_op jit(solution)/shard_map/ppermute | solution.py:401
  34.6 63.5 %collective-permute-start.18 = (bf16[256,4096]{1,0:T(8,128)(2,1)}, bf16[256,4096]{1,0:T(8,128)(2,1)S(1)}, u32[]{:S(2)}, u32[]{:S(2)}) collective-permute-start(bf16[256,4096]{1,0:T(8,128)(2,1)} %grad_block.5), channel_id=1, source_target_pairs={{0,1},{1,0},{2,3},{3,2},{4,5},{5,4},{6,7},{7,6},{8,9},{9,8},{10,11... | collective-permute-start | bytes 6291464 | tf_op jit(solution)/shard_map/ppermute | solution.py:401
  36.1 24.3 %collective-permute-start.9 = (f32[96,256]{1,0:T(8,128)S(1)}, f32[96,256]{1,0:T(8,128)S(1)}, u32[]{:S(2)}, u32[]{:S(2)}) collective-permute-start(f32[96,256]{1,0:T(8,128)S(1)} %slice.25), channel_id=1, source_target_pairs={{0,2},{1,3},{2,0},{3,1},{4,6},{5,7},{6,4},{7,5},{8,10},{9,11},{10,... | collective-permute-start | bytes 294920 | tf_op jit(solution)/shard_map/ppermute | solution.py:401
  67.6 3.3 %collective-permute-start.10 = (f32[64,2048]{1,0:T(8,128)}, f32[64,2048]{1,0:T(8,128)}, u32[]{:S(2)}, u32[]{:S(2)}) collective-permute-start(f32[64,2048]{1,0:T(8,128)} %right.3), channel_id=1, source_target_pairs={{0,1},{1,0},{2,3},{3,2},{4,5},{5,4},{6,7},{7,6},{8,9},{9,8},{10,11... | collective-permute-start | bytes 1572872 | tf_op jit(solution)/shard_map/ppermute | solution.py:401
  72.9 6.0 %collective-permute-start.11 = (bf16[64,1024]{1,0:T(8,128)(2,1)S(1)}, bf16[64,1024]{1,0:T(8,128)(2,1)S(1)}, u32[]{:S(2)}, u32[]{:S(2)}) collective-permute-start(bf16[64,1024]{1,0:T(8,128)(2,1)S(1)} %dynamic-slice_convert_fusion), channel_id=1, source_target_pairs={{0,2},{1,3},{2,0},{3,1},{4,6},{5,7},{6,4},{7,5},{8,10},{9,11},{10,... | collective-permute-start | bytes 393224 | tf_op jit(solution)/shard_map/ppermute | solution.py:401
  79.9 5.2 %collective-permute-start.12 = (bf16[64,1024]{1,0:T(8,128)(2,1)S(1)}, bf16[64,1024]{1,0:T(8,128)(2,1)S(1)}, u32[]{:S(2)}, u32[]{:S(2)}) collective-permute-start(bf16[64,1024]{1,0:T(8,128)(2,1)S(1)} %add_convert_fusion.2), channel_id=1, source_target_pairs={{0,4},{4,0},{8,12},{12,8},{16,20},{20,16},{24,28},{28,24},{1,5},{5... | collective-permute-start | bytes 393224 | tf_op jit(solution)/shard_map/ppermute | solution.py:401
  85.1 5.0 %collective-permute-start.13 = (bf16[64,1024]{1,0:T(8,128)(2,1)S(1)}, bf16[64,1024]{1,0:T(8,128)(2,1)S(1)}, u32[]{:S(2)}, u32[]{:S(2)}) collective-permute-start(bf16[64,1024]{1,0:T(8,128)(2,1)S(1)} %add_convert_fusion.1), channel_id=1, source_target_pairs={{0,8},{4,12},{8,0},{12,4},{16,24},{20,28},{24,16},{28,20},{1,9},{5... | collective-permute-start | bytes 393224 | tf_op jit(solution)/shard_map/ppermute | solution.py:401
  87.0 73.4 %collective-permute-start = (bf16[256,4096]{1,0:T(8,128)(2,1)}, bf16[256,4096]{1,0:T(8,128)(2,1)}, u32[]{:S(2)}, u32[]{:S(2)}) collective-permute-start(bf16[256,4096]{1,0:T(8,128)(2,1)} %x_ref.5), channel_id=1, source_target_pairs={{0,1},{1,0},{2,3},{3,2},{4,5},{5,4},{6,7},{7,6},{8,9},{9,8},{10,11... | collective-permute-start | bytes 6291464 | tf_op jit(solution)/shard_map/ppermute | solution.py:401
  87.0 73.4 %collective-permute-start.2 = (bf16[256,4096]{1,0:T(8,128)(2,1)}, bf16[256,4096]{1,0:T(8,128)(2,1)}, u32[]{:S(2)}, u32[]{:S(2)}) collective-permute-start(bf16[256,4096]{1,0:T(8,128)(2,1)} %collective-permute-done.1.x2), channel_id=1, source_target_pairs={{0,1},{1,0},{2,3},{3,2},{4,5},{5,4},{6,7},{7,6},{8,9},{9,8},{10,11... | collective-permute-start | bytes 6291464 | tf_op jit(solution)/shard_map/ppermute | solution.py:401
  90.2 14.6 %collective-permute-start.14 = (bf16[64,1024]{1,0:T(8,128)(2,1)S(1)}, bf16[64,1024]{1,0:T(8,128)(2,1)S(1)}, u32[]{:S(2)}, u32[]{:S(2)}) collective-permute-start(bf16[64,1024]{1,0:T(8,128)(2,1)S(1)} %add_convert_fusion), channel_id=1, source_target_pairs={{0,16},{4,20},{8,24},{12,28},{16,0},{20,4},{24,8},{28,12},{1,17},{... | collective-permute-start | bytes 393224 | tf_op jit(solution)/shard_map/ppermute | solution.py:401
  98.1 84.2 %collective-permute-start.17 = (bf16[256,4096]{1,0:T(8,128)(2,1)}, bf16[256,4096]{1,0:T(8,128)(2,1)}, u32[]{:S(2)}, u32[]{:S(2)}) collective-permute-start(bf16[256,4096]{1,0:T(8,128)(2,1)} %grad_block.4), channel_id=1, source_target_pairs={{0,1},{1,0},{2,3},{3,2},{4,5},{5,4},{6,7},{7,6},{8,9},{9,8},{10,11... | collective-permute-start | bytes 6291464 | tf_op jit(solution)/shard_map/ppermute | solution.py:401
  103.2 79.1 %collective-permute-start.19 = (bf16[256,4096]{1,0:T(8,128)(2,1)}, bf16[256,4096]{1,0:T(8,128)(2,1)S(1)}, u32[]{:S(2)}, u32[]{:S(2)}) collective-permute-start(bf16[256,4096]{1,0:T(8,128)(2,1)} %grad_block.6), channel_id=1, source_target_pairs={{0,2},{1,3},{2,0},{3,1},{4,6},{5,7},{6,4},{7,5},{8,10},{9,11},{10,... | collective-permute-start | bytes 6291464 | tf_op jit(solution)/shard_map/ppermute | solution.py:401
  104.8 49.5 %collective-permute-start.15 = (bf16[64,1024]{1,0:T(8,128)(2,1)S(1)}, bf16[64,1024]{1,0:T(8,128)(2,1)S(1)}, u32[]{:S(2)}, u32[]{:S(2)}) collective-permute-start(bf16[64,1024]{1,0:T(8,128)(2,1)S(1)} %multiply_convert_fusion), channel_id=1, source_target_pairs={{0,2},{1,3},{2,0},{3,1},{4,6},{5,7},{6,4},{7,5},{8,10},{9,11},{10,... | collective-permute-start | bytes 393224 | tf_op jit(solution)/shard_map/ppermute | solution.py:401
  155.1 1.9 collective-permute-start.16
  (1 other events, 0.8 us)

commit v2 on v1

v2 whole, which is shorter than its diff:
```python
from functools import partial

import jax
import jax.numpy as jnp
from jax import lax
from jax.experimental import pallas as pl
from jax.experimental.pallas import tpu as pltpu
from jax.sharding import PartitionSpec as P

TOKENS = 1024
SCALE = TOKENS ** (-0.5)
F32, BF16 = jnp.float32, jnp.bfloat16
WEIGHT = 4096
SECOND_PIECES = (1, 3)
VMEM_LIMIT = 20 * 1024 * 1024
NN = (((1,), (0,)), ((), ()))
NT = (((1,), (1,)), ((), ()))
TN = (((0,), (0,)), ((), ()))
HIGHEST = lax.Precision.HIGHEST


def mm(a, b, dims, precision=None):
    return lax.dot_general(a, b, dims, precision=precision, preferred_element_type=F32)


def split(value, terms):
    parts, rest = [], value
    for _ in range(terms):
        part = rest.astype(BF16)
        parts.append(part)
        rest = rest - part.astype(F32)
    return jnp.concatenate(parts, axis=0)


def split_mm(a, b, dims, terms):
    rows = a.shape[0]
    product = mm(split(a, terms), b, dims)
    total = product[:rows]
    for k in range(1, terms):
        total = total + product[k * rows : (k + 1) * rows]
    return total


def params(*semantics):
    return pltpu.CompilerParams(
        vmem_limit_bytes=VMEM_LIMIT,
        dimension_semantics=semantics if semantics else None,
    )


SMEM = pl.BlockSpec(memory_space=pltpu.SMEM)
VMEM = pl.BlockSpec(memory_space=pltpu.VMEM)


def hbm(value):
    return pltpu.with_memory_space_constraint(value, pltpu.HBM)


def cost(flops, nbytes):
    return pl.CostEstimate(flops=int(flops) // WEIGHT, bytes_accessed=int(nbytes) // WEIGHT, transcendentals=0)


def project_kernel(x_ref, r_ref, y_ref):
    modes, rank, chunk = r_ref.shape
    term = split_mm(r_ref[...].reshape(modes * rank, chunk), x_ref[...], NT, 3)

    @pl.when(pl.program_id(0) == 0)
    def _():
        y_ref[...] = term

    @pl.when(pl.program_id(0) > 0)
    def _():
        y_ref[...] += term


def project(x, r, chunk=2048):
    rows, depth = x.shape
    modes, rank, _ = r.shape
    return pl.pallas_call(
        project_kernel,
        grid=(depth // chunk,),
        in_specs=[
            pl.BlockSpec((rows, chunk), lambda i: (0, i)),
            pl.BlockSpec((modes, rank, chunk), lambda i: (0, 0, i)),
        ],
        out_specs=pl.BlockSpec((modes * rank, rows), lambda i: (0, 0)),
        out_shape=jax.ShapeDtypeStruct((modes * rank, rows), F32),
        compiler_params=params("arbitrary"),
        cost_estimate=cost(6 * rows * depth * modes * rank, x.nbytes + r.nbytes),
        name="project",
    )(hbm(x), hbm(r))


def feedback_kernel(r_ref, e_ref, out_ref):
    term = split_mm(r_ref[0], e_ref[0], NN, 3)

    @pl.when(pl.program_id(1) == 0)
    def _():
        out_ref[...] = term

    @pl.when(pl.program_id(1) > 0)
    def _():
        out_ref[...] += term


def feedback(r, e, chunk=2048):
    modes, rank, depth = r.shape
    cols = e.shape[-1]
    return pl.pallas_call(
        feedback_kernel,
        grid=(modes, depth // chunk),
        in_specs=[
            pl.BlockSpec((1, rank, chunk), lambda m, i: (m, 0, i)),
            pl.BlockSpec((1, chunk, cols), lambda m, i: (m, i, 0)),
        ],
        out_specs=pl.BlockSpec((rank, cols), lambda m, i: (m, 0)),
        out_shape=jax.ShapeDtypeStruct((modes * rank, cols), F32),
        compiler_params=params("arbitrary", "arbitrary"),
        cost_estimate=cost(6 * modes * rank * depth * cols, r.nbytes + e.nbytes),
        name="feedback",
    )(hbm(r), hbm(e))


def rows_of(t_ref, j, rows):
    return pl.ds(pl.multiple_of((t_ref[0] ^ j) * rows, rows), rows)


def by_core(t_ref, on_core0, on_core1):
    return jnp.where(t_ref[0] % 2 == 0, on_core0, on_core1)


def left_kernel(t_ref, own, near, far0, far1, g_ref, e_ref, out_ref):
    modes = g_ref.shape[0]
    rank, rows = own.shape[0] // modes, own.shape[1]
    n = modes * rank
    far = by_core(t_ref, far0[...], far1[...])
    same = by_core(t_ref, far[n:], far[:n])
    other = by_core(t_ref, far[:n], far[n:])
    for m in range(modes):
        at = slice(m * rank, (m + 1) * rank)
        total = 0.0
        for j, y in enumerate((own[...], near[...], same, other)):
            total = total + split_mm(y[at], g_ref[m, rows_of(t_ref, j, rows), :], NN, 3)
        out_ref[at, :] = total * SCALE + e_ref[at, :]


def left_local(t, ys, g, e):
    return pl.pallas_call(
        left_kernel,
        in_specs=[SMEM] + [VMEM] * 6,
        out_specs=VMEM,
        out_shape=jax.ShapeDtypeStruct(e.shape, F32),
        compiler_params=params(),
        cost_estimate=cost(6 * e.size * g.shape[1], g.nbytes),
        name="left",
    )(t, *ys, g, e)


def spread_kernel(t_ref, left_ref, g_ref, own_ref, near_ref, far_ref):
    modes = g_ref.shape[0]
    rank = left_ref.shape[0] // modes
    rows = own_ref.shape[1]
    n = modes * rank
    low = 2 + t_ref[0] % 2
    for j, (ref, top) in ((0, (own_ref, 0)), (1, (near_ref, 0)), (low, (far_ref, 0)), (low ^ 1, (far_ref, n))):
        for m in range(modes):
            ref[top + m * rank : top + (m + 1) * rank, :] = split_mm(
                left_ref[m * rank : (m + 1) * rank, :], g_ref[m, rows_of(t_ref, j, rows), :], NT, 3
            )
    zero = jnp.zeros((rank, left_ref.shape[1]), F32)
    a, b = left_ref[0:rank, :], left_ref[rank : 2 * rank, :]
    gram = mm(a, jnp.concatenate([a, zero, zero, zero], axis=0), NT, HIGHEST)
    gram = gram + mm(b, jnp.concatenate([zero, zero, b, zero], axis=0), NT, HIGHEST)
    far_ref[2 * n :, 0:128] = gram
    far_ref[2 * n :, 128:] = jnp.zeros((rank, rows - 128), F32)


def spread(t, left, g):
    rows = g.shape[1] // 4
    n = left.shape[0]
    small = jax.ShapeDtypeStruct((n, rows), F32)
    return pl.pallas_call(
        spread_kernel,
        in_specs=[SMEM, VMEM, VMEM],
        out_specs=[VMEM, VMEM, VMEM],
        out_shape=[small, small, jax.ShapeDtypeStruct((2 * n + n // 2, rows), F32)],
        compiler_params=params(),
        cost_estimate=cost(6 * left.size * g.shape[1], g.nbytes),
        name="spread",
    )(t, left, g)


def solve_kernel(t_ref, own_ref, near_ref, chip_ref, got0, got1, left_ref, z_ref, b_ref):
    modes = 2
    rank = left_ref.shape[0] // modes
    n = modes * rank
    got = by_core(t_ref, got0[...], got1[...])
    gram = chip_ref[2 * n :, 0:128] + got[2 * n :, 0:128]
    row = lax.broadcasted_iota(jnp.int32, (rank, 128), 0)
    lane = lax.broadcasted_iota(jnp.int32, (rank, 128), 1)
    ones = jnp.where((lane == row + rank) | (lane == row + 3 * rank), 1.0, 0.0)
    a = jnp.where((lane // rank) % 2 == 0, gram, ones)
    low = lane < 2 * rank
    scale = jnp.zeros((rank, 128), F32)
    for k in range(rank):
        pivot_row = a[k : k + 1, :]
        column = jnp.where(low, a[:, k : k + 1], a[:, 2 * rank + k : 2 * rank + k + 1])
        pivot = column[k : k + 1, :]
        inverse = 1.0 / pivot
        scale = jnp.where(row == k, lax.rsqrt(pivot), scale)
        a = jnp.where(row > k, a - column * (inverse * pivot_row), a)
    a = a * scale
    zero = jnp.zeros((rank, left_ref.shape[1]), F32)
    z = (own_ref[...] + near_ref[...] + by_core(t_ref, got[0:n], got[n : 2 * n])) * SCALE
    for m in range(modes):
        part = jnp.where(lane // rank == 2 * m + 1, a, 0.0)
        at = slice(m * rank, (m + 1) * rank)
        for value, ref in ((z[at], z_ref), (left_ref[at, :], b_ref)):
            stacked = [zero] * 4
            stacked[2 * m + 1] = value
            ref[at, :] = mm(part, jnp.concatenate(stacked, axis=0), NN, HIGHEST)


def solve(t, own, near, chip, got0, got1, left):
    shape = jax.ShapeDtypeStruct(left.shape, F32)
    return pl.pallas_call(
        solve_kernel,
        in_specs=[SMEM] + [VMEM] * 6,
        out_specs=[VMEM, VMEM],
        out_shape=[shape, shape],
        compiler_params=params(),
        cost_estimate=cost(10**7, 10**7),
        name="solve",
    )(t, own, near, chip, got0, got1, left)


def right_kernel(h_ref, z_ref, b_ref, x_ref, e_ref, near_ref, own_ref):
    modes = e_ref.shape[0]
    rank = z_ref.shape[0] // modes
    product = split_mm(z_ref[...], x_ref[...], NN, 2)
    parts = []
    for m in range(modes):
        at = slice(m * rank, (m + 1) * rank)
        parts.append(product[at] + split_mm(b_ref[at, :], e_ref[m], NT, 2))
    i = pl.program_id(0)

    @pl.when(i < 2)
    def _():
        near_ref[...] = jnp.concatenate(parts, axis=0)

    @pl.when(i >= 2)
    def _():
        own_ref[...] = jnp.concatenate(parts, axis=0)


def right_halves(core, bit, bit_near, z, b, x, e):
    rows, depth = x.shape
    modes, _, cols = e.shape
    chunk = depth // 4
    at, at_near = core * 2 + bit, (1 - core) * 2 + bit_near
    place = jnp.stack([at_near ^ 1, at_near, at ^ 1, at])
    shape = jax.ShapeDtypeStruct((z.shape[0], depth // 2), F32)
    return pl.pallas_call(
        right_kernel,
        grid_spec=pltpu.PrefetchScalarGridSpec(
            num_scalar_prefetch=1,
            grid=(4,),
            in_specs=[
                pl.BlockSpec(z.shape, lambda i, h: (0, 0)),
                pl.BlockSpec(b.shape, lambda i, h: (0, 0)),
                pl.BlockSpec((rows, chunk), lambda i, h: (0, h[i])),
                pl.BlockSpec((modes, chunk, cols), lambda i, h: (0, h[i], 0)),
            ],
            out_specs=[
                pl.BlockSpec((z.shape[0], chunk), lambda i, h: (0, jnp.minimum(i, 1))),
                pl.BlockSpec((z.shape[0], chunk), lambda i, h: (0, jnp.maximum(i - 2, 0))),
            ],
        ),
        out_shape=[shape, shape],
        compiler_params=params("arbitrary"),
        cost_estimate=cost(8 * depth * rows * 128, x.nbytes + e.nbytes),
        name="right",
    )(place, z, b, hbm(x), hbm(e))


def moment_kernel(t_ref, x0, x1, a0, a1, b0, b1, g_ref, e_ref, *refs):
    out_ref = refs[-1]
    modes = g_ref.shape[0]
    rows = x0.shape[0]
    low = 2 + t_ref[0] % 2
    terms = ((0, x0[...]), (1, x1[...]), (low, by_core(t_ref, a0[...], a1[...])), (low ^ 1, by_core(t_ref, b0[...], b1[...])))
    for m in range(modes):
        total = 0.0
        for j, x in terms:
            total = total + mm(x, g_ref[m, rows_of(t_ref, j, rows), :], TN)
        out_ref[m] = total * SCALE + e_ref[m].astype(F32)


def moment_quarter(quarter, t, xs, g, e, so_far=()):
    rows, depth = xs[0].shape
    modes, tokens, cols = g.shape
    chunk = depth // 8
    first = 2 * quarter
    both = pl.BlockSpec((rows, chunk), lambda i, t: (0, first + i))
    on0 = pl.BlockSpec((rows, chunk), lambda i, t: (0, (first + i) * (1 - t[0] % 2)))
    on1 = pl.BlockSpec((rows, chunk), lambda i, t: (0, (first + i) * (t[0] % 2)))
    return pl.pallas_call(
        moment_kernel,
        grid_spec=pltpu.PrefetchScalarGridSpec(
            num_scalar_prefetch=1,
            grid=(2,),
            in_specs=[
                both,
                both,
                on0,
                on1,
                on0,
                on1,
                pl.BlockSpec(g.shape, lambda i, t: (0, 0, 0)),
                pl.BlockSpec((modes, chunk, cols), lambda i, t: (0, first + i, 0)),
            ]
            + [pl.BlockSpec(memory_space=pl.ANY)] * len(so_far),
            out_specs=pl.BlockSpec((modes, chunk, cols), lambda i, t: (0, first + i, 0)),
        ),
        out_shape=pltpu.HBM((modes, depth, cols), F32),
        input_output_aliases={9: 0} if so_far else {},
        compiler_params=params("arbitrary"),
        cost_estimate=cost(2 * depth * modes * cols * tokens // 4, 8 * 2**20),
        name="moment",
    )(t, hbm(xs[0]), *xs[1:], g, hbm(e), *so_far)


def error_kernel(q_ref, m_ref, r0, r1, b_ref, *refs):
    out_ref, right_ref = refs[-2:]
    modes = out_ref.shape[0]
    rank = b_ref.shape[0] // modes
    right = jnp.where(pl.program_id(0) == 0, r0[...], r1[...])
    right_ref[...] = right.astype(F32)
    for m in range(modes):
        at = slice(m * rank, (m + 1) * rank)
        stacked = jnp.concatenate([right[at], right[at]], axis=0)
        out_ref[m] = m_ref[m] - mm(stacked, split(b_ref[at, :], 2), TN)


def error_quarters(places, moments, rights, b, so_far=(), pieces=1):
    modes, depth, cols = moments.shape
    ranks, width = rights[0].shape
    width //= pieces
    spec = pl.BlockSpec((modes, width, cols), lambda i, j, q: (0, q[i] * pieces + j, 0))
    half = pl.BlockSpec((ranks, width), lambda i, j, q: (0, j))
    return pl.pallas_call(
        error_kernel,
        grid_spec=pltpu.PrefetchScalarGridSpec(
            num_scalar_prefetch=1,
            grid=(2, pieces),
            in_specs=[spec, half, half, pl.BlockSpec(b.shape, lambda i, j, q: (0, 0))]
            + [pl.BlockSpec(memory_space=pl.ANY)] * len(so_far),
            out_specs=[spec, pl.BlockSpec((ranks, width), lambda i, j, q: (0, q[i] * pieces + j))],
        ),
        out_shape=[
            pltpu.HBM(moments.shape, F32),
            pltpu.HBM((ranks, depth), F32),
        ],
        input_output_aliases={1: 0, 5: 1} if so_far else {1: 0},
        compiler_params=params("arbitrary", "arbitrary"),
        cost_estimate=cost(10**6, 8 * 2**20),
        name="error",
    )(jnp.stack(places), moments, *rights, b, *so_far)


def grad_kernel(t_ref, g_ref, w_ref, keep_ref, send_ref):
    rows = keep_ref.shape[0] // 2
    w = jnp.concatenate([w_ref[0], w_ref[1]], axis=1)
    for j, (ref, top) in enumerate(((keep_ref, 0), (send_ref, 0), (keep_ref, rows), (send_ref, rows))):
        at = rows_of(t_ref, j, rows)
        g = jnp.concatenate([g_ref[0, at, :], g_ref[1, at, :]], axis=1)
        ref[top : top + rows, :] = mm(g, w, NT).astype(BF16)


def grad_half(half, t, g, w, chunk=1024):
    modes, depth, cols = w.shape
    rows = g.shape[1] // 2
    steps = depth // 2 // chunk
    first = half * steps
    shape = jax.ShapeDtypeStruct((rows, depth // 2), BF16)
    return pl.pallas_call(
        grad_kernel,
        grid=(steps,),
        in_specs=[
            SMEM,
            pl.BlockSpec(g.shape, lambda i: (0, 0, 0)),
            pl.BlockSpec((modes, chunk, cols), lambda i: (0, first + i, 0)),
        ],
        out_specs=[pl.BlockSpec((rows, chunk), lambda i: (0, i))] * 2,
        out_shape=[shape, shape],
        compiler_params=params("arbitrary"),
        cost_estimate=cost(4 * rows * depth * modes * cols, w.nbytes),
        name="grad",
    )(t, g, hbm(w))


def pair_kernel(sizes, a_ref, b_ref, *outs):
    total = (a_ref[...].astype(F32) + b_ref[...].astype(F32)).astype(BF16)
    chunk = total.shape[1]
    i = pl.program_id(0)
    first = 0
    for size, out in zip(sizes, outs):
        for u in range(size):

            @pl.when(i == first + u)
            def _(out=out, u=u):
                out[:, u * chunk : (u + 1) * chunk] = total

        first += size


def pair_sum(a, b, sizes):
    rows, width = a.shape
    rows //= 2
    chunk = width // sum(sizes)
    spec = pl.BlockSpec((rows, chunk), lambda i: (1, i))
    shapes = [(rows, size * chunk) for size in sizes]
    return pl.pallas_call(
        partial(pair_kernel, sizes),
        grid=(sum(sizes),),
        in_specs=[spec, spec],
        out_specs=[pl.BlockSpec(shape, lambda i: (0, 0)) for shape in shapes],
        out_shape=[jax.ShapeDtypeStruct(shape, BF16) for shape in shapes],
        compiler_params=params("arbitrary"),
        cost_estimate=cost(rows * width, 6 * rows * width),
        name="pair_sum",
    )(a, b)


def finish_kernel(a_ref, b_ref, c_ref, *refs):
    total = a_ref[...].astype(F32) + b_ref[...].astype(F32)
    refs[-1][...] = (total + c_ref[...].astype(F32)).astype(BF16)


def finish_grad(place, depth, keep, near, first, far, so_far=()):
    rows, width = far.shape
    chunk = depth // 8
    if width % (2 * chunk) == 0 and place % 2 == 0 and first % 2 == 0:
        chunk, place, first = 2 * chunk, place // 2, first // 2
    mine = pl.BlockSpec((rows, chunk), lambda i: (0, first + i))
    return pl.pallas_call(
        finish_kernel,
        grid=(width // chunk,),
        in_specs=[mine, mine, pl.BlockSpec((rows, chunk), lambda i: (0, i))]
        + [pl.BlockSpec(memory_space=pl.ANY)] * len(so_far),
        out_specs=pl.BlockSpec((rows, chunk), lambda i: (0, place + i)),
        out_shape=pltpu.HBM((rows, depth), BF16),
        input_output_aliases={3: 0} if so_far else {},
        compiler_params=params("arbitrary"),
        cost_estimate=cost(far.size, 3 * far.nbytes),
        name="finish_grad",
    )(keep, near, far, *so_far)


def compress(moments, right_prev):
    highest = lax.Precision.HIGHEST
    replicas = lax.axis_size("dp")
    projected = jnp.einsum("mdc,mrd->mrc", moments, right_prev, precision=highest)
    left_sum = lax.psum(projected, "dp")
    gram_matrix = lax.psum(
        jnp.einsum("mrc,msc->mrs", left_sum, left_sum, precision=highest), "tensor"
    )
    factor = jnp.linalg.cholesky(gram_matrix)
    ortho_basis = jax.vmap(partial(jax.scipy.linalg.solve_triangular, lower=True))(factor, left_sum)
    right_local = jnp.einsum("mdc,mrc->mrd", moments, ortho_basis, precision=highest)
    right_total = lax.psum(right_local, "tensor")
    right_total = lax.psum(right_total, "dp")
    right_mean = right_total / replicas
    approximation = jnp.einsum("mrd,mrc->mdc", right_mean, ortho_basis, precision=highest)
    return (moments - approximation, right_mean)


def any_mesh(layer_input, kv_weight, kv_cotangent, error_before, right_factor):
    portion = kv_cotangent
    weight_grad = jnp.einsum(
        "td,mtc->mdc",
        lax.all_gather(layer_input, "tensor", axis=0, tiled=True),
        portion,
        preferred_element_type=jnp.float32,
    )
    moments = weight_grad * TOKENS ** (-0.5) + error_before[0].astype(jnp.float32)
    portion = kv_cotangent
    input_sum = lax.psum_scatter(
        jnp.einsum("mtc,mdc->td", portion, kv_weight, preferred_element_type=jnp.float32).astype(
            jnp.bfloat16
        ),
        "tensor",
        scatter_dimension=0,
        tiled=True,
    )
    leading = compress(moments[0:1], right_factor[0:1])
    second = compress(moments[1:2], right_factor[1:2])
    errors = jnp.concatenate([leading[0], second[0]], axis=0)
    right_next = jnp.concatenate([leading[1], second[1]], axis=0)
    return (errors[None], right_next, input_sum)


def tie(value, *others):
    return lax.optimization_barrier((value, *others))[0]


def per_device(layer_input, kv_weight, kv_cotangent, error_before, right_factor):
    tensor, replicas = lax.axis_size("tensor"), lax.axis_size("dp")
    t = lax.axis_index("tensor").astype(jnp.int32)
    d = lax.axis_index("dp").astype(jnp.int32)
    core = t & 1
    place = t.reshape(1)
    errors = error_before[0]
    depth = layer_input.shape[1]
    n = 2 * right_factor.shape[1]
    bits = replicas.bit_length() - 1

    def swap(value):
        return lax.ppermute(value, "tensor", [(i, i ^ 1) for i in range(tensor)])

    def cross(value, carrier=None):
        cores = range(tensor) if carrier is None else range(carrier, tensor, 2)
        return lax.ppermute(value, "tensor", [(i, i ^ 2) for i in cores])

    def hop(value, step):
        pairs = []
        for i in range(replicas):
            for k in range(tensor):
                bit = (step + 1 - k % 2) % bits
                pairs.append((i * tensor + k, (i ^ (1 << bit)) * tensor + k))
        return lax.ppermute(value, ("dp", "tensor"), pairs)

    bit0, bit1 = (d >> (1 % bits)) & 1, d & 1
    bit, bit_near = jnp.where(core == 1, bit1, bit0), jnp.where(core == 1, bit0, bit1)
    at, at_near = core * 2 + bit, (1 - core) * 2 + bit_near
    places = (at, at_near, at ^ 1, at_near ^ 1)
    always = d + t < replicas + tensor

    def together(steps, *args):
        def skipped(*args):
            shapes = jax.eval_shape(steps, *args)
            return jax.tree.map(lambda v: jnp.zeros(v.shape, v.dtype), shapes)

        return lax.cond(always, steps, skipped, *args)

    xa0 = cross(layer_input, 0)

    def project_rows(x, r, errors):
        y = project(x, r)
        y_near = swap(y)
        y_far = cross(jnp.concatenate([y, y_near], axis=0), 1)
        x_near = swap(tie(x, y_near))
        e = feedback(tie(r, y_near), errors)
        y_far = tie(y_far, e, x_near)
        return (y, y_near, swap(y_far), y_far), e, x_near

    ys, e, x_near = together(project_rows, layer_input, right_factor, errors)
    xb0 = cross(x_near, 0)

    def left_factors(ys, e):
        left = left_local(place, ys, kv_cotangent, e)
        grads = []
        for k in range(bits):
            arrived = hop(left, k)
            if k < 2:
                grads.append(grad_half(k, place, kv_cotangent, tie(kv_weight, left)))
                arrived = tie(arrived, grads[k][0])
            if k == 1:
                got0 = swap(tie(grads[0][1], left))
                arrived = tie(arrived, got0)
            elif k == 2:
                got1 = swap(tie(grads[1][1], left))
                (first,) = pair_sum(grads[0][0], tie(got0, left), (2,))
                arrived = tie(arrived, first, got1)
            left = left + arrived
        return left, grads, got0, got1, first

    left, grads, got0, got1, first = together(left_factors, ys, e)
    (keep0, _), (keep1, _) = grads
    left, xa0 = lax.optimization_barrier((left, xa0))

    def spread_out(left, keep1, got1):
        own, send, far = spread(place, left, kv_cotangent)
        near = swap(jnp.concatenate([send, far], axis=0))
        chip = far + near[n:]
        got = cross(chip, 1)
        pieces = pair_sum(tie(keep1, chip), got1, SECOND_PIECES)
        got = tie(got, *pieces)
        return own, near[:n], chip, swap(got), got, pieces

    own, near, chip, *gots, (second, third) = together(spread_out, left, keep1, got1)
    chip, xb0, first = lax.optimization_barrier((chip, xb0, first))
    first = cross(first)

    def right_halves_of(own, near, chip, got0, got, left, xa0, xb0):
        xa1 = swap(xa0)
        z, b = solve(place, own, near, chip, got0, got, left)
        xb1 = swap(tie(xb0, z))
        half_near, half = right_halves(core, bit, bit_near, z, b, layer_input, errors)
        half_near = swap(tie(half_near, xa1, xb1))
        quarter = half.shape[1] // 2
        give = (half[:, :quarter] + half_near[:, :quarter]).astype(BF16)
        return b, give, half[:, quarter:] + half_near[:, quarter:], xa1, xb1

    args = (own, near, chip, *gots, left, xa0, xb0)
    b, give, own, xa1, xb1 = together(right_halves_of, *args)
    second = cross(tie(second, give))

    def moments_of(j, xs, after, *so_far):
        return moment_quarter(j, place, xs, tie(kv_cotangent, after), errors, so_far)

    xs = (layer_input, x_near, xa0, xa1, xb0, xb1)

    def right_sums(give, own, xs):
        moments = moments_of(0, xs, give)
        own = own + tie(hop(give, 0), moments).astype(F32)
        for k in range(1, bits):
            rounded = lax.optimization_barrier(own.astype(BF16))
            moments = moments_of(k, xs, rounded, moments)
            own = rounded.astype(F32) + tie(hop(rounded, k), moments).astype(F32)
        return own.astype(BF16), moments

    own, moments = together(right_sums, give, own, xs)
    own, first, second = lax.optimization_barrier((own, first, second))

    def over_x(own, keep0, got0, first, keep1, got1, second):
        arrived = cross(own)
        grad = finish_grad(0, depth, keep0, got0, 0, tie(first, own))
        grad = finish_grad(4, depth, keep1, got1, 0, second, (grad,))
        own = own.astype(F32) + tie(arrived, grad).astype(F32)
        return (own * (1.0 / replicas)).astype(BF16), grad

    own, grad = together(over_x, own, keep0, got0, first, keep1, got1, second)
    third = cross(tie(third, own))

    def first_errors(own, b, moments, xs):
        other = hop(own, 0)
        near = swap(own)
        moments = moments_of(3, xs, own, moments)
        other = tie(other, moments)
        other_near = swap(other)
        after, right = error_quarters(places[:2], moments, (own, near), b)
        return after, right, other, tie(other_near, right)

    after, right, other, other_near = together(first_errors, own, b, moments, xs)
    after, right = error_quarters(places[2:], after, (other, other_near), b, (right,))
    done = SECOND_PIECES[0]
    grad = finish_grad(4 + done, depth, keep1, got1, done, tie(third, other_near), (grad,))
    return (after[None], right.reshape(right_factor.shape), grad)


def solution(mesh):
    sizes = mesh.shape
    fits = sizes["tensor"] == 4 and sizes["dp"] == 8
    return jax.shard_map(
        per_device if fits else any_mesh,
        mesh=mesh,
        in_specs=(
            P(("dp", "tensor"), None),
            P(None, None, "tensor"),
            P(None, "dp", "tensor"),
            P("dp", None, None, "tensor"),
            P(),
        ),
        out_specs=(P("dp", None, None, "tensor"), P(), P(("dp", "tensor"), None)),
        check_vma=False,
    )
```

time: 189 us -> 120 us (0.63)
  waiting for transfers between devices: 91.6 us -> 12.4 us
  starting transfers between devices: 24.2 us -> 32.7 us
  Pallas kernels: 59.5 us -> 67.2 us
  other arithmetic: 7.44 us -> 2.71 us
    ppermute x20 -> x27, waiting for transfers between devices: 91.6 us -> 12.4 us  [the longest x12 9.1 us: swap(): return lax.ppermute(value, 'tensor', [(i, i ^ 1) for i in range(tensor)])]
    ppermute x20 -> x27, starting transfers between devices: 24.2 us -> 32.7 us  [the longest x8 13.9 us: cross(): return lax.ppermute(value, 'tensor', [(i, i ^ 2) for i in cores])]
    pallas_call x9 -> x15, Pallas kernels: 53.3 us -> 58.3 us  [the longest x4 16.4 us: moment_quarter(): pl.pallas_call(moment_kernel, grid_spec=pltpu.PrefetchScalarGridSpec(num_...]
    convert_element_type x6 -> x4, other arithmetic: 4.51 us -> 0.14 us  [the longest x2 0.06 us: right_sums(): rounded = lax.optimization_barrier(own.astype(BF16))]
    unnamed x10 -> x8, local copies, waits for them, and re-layouts: 4.2 us -> 1.64 us
    pallas_call x1, Pallas kernels: 1.38 us -> 3.76 us  [feedback(): pl.pallas_call(feedback_kernel, grid=(modes, depth // chunk), in_specs=[p...]
  transfers between devices with their start and end apart: 20 -> 27, of which waited for: 11 -> 9; matrix products, arithmetic and copies ran while one was open for 4% -> 2% of each run, Pallas kernels for 27% -> 54%
where the time goes in v2:
time: 120 us; the launch traced here: 119 us
  Pallas kernels  67.2 us (56%)
  starting transfers between devices  32.7 us (27%)
  waiting for transfers between devices  12.4 us (10%)
  local copies, waits for them, and re-layouts  3.54 us (3%)
  other arithmetic  2.71 us (2%)
    pallas_call x4, Pallas kernels, moment_quarter(): pl.pallas_call(moment_kernel, grid_spec=pltpu.PrefetchScalarGridSpec(num_...  16.4 us
    ppermute x8, starting transfers between devices, cross(): return lax.ppermute(value, 'tensor', [(i, i ^ 2) for i in cores])  13.9 us
    ppermute x7, starting transfers between devices, hop(): return lax.ppermute(value, ('dp', 'tensor'), pairs)  11.2 us
    pallas_call x2, Pallas kernels, error_quarters(): pl.pallas_call(error_kernel, grid_spec=pltpu.PrefetchScalarGridSpec(num_s...  9.64 us
    pallas_call x2, Pallas kernels, grad_half(): pl.pallas_call(grad_kernel, grid=(steps,), in_specs=[SMEM, pl.BlockSpec(g...  9.41 us
    ppermute x12, waiting for transfers between devices, swap(): return lax.ppermute(value, 'tensor', [(i, i ^ 1) for i in range(tensor)])  9.1 us
    pallas_call x3, Pallas kernels, finish_grad(): pl.pallas_call(finish_kernel, grid=(width // chunk,), in_specs=[mine, min...  7.9 us
    ppermute x12, starting transfers between devices, swap(): return lax.ppermute(value, 'tensor', [(i, i ^ 1) for i in range(tensor)])  7.61 us
  transfers between devices with their start and end apart: 27, of which 9 were waited for; matrix products, arithmetic and copies ran while one was open for 2% of the time, Pallas kernels for 54%

profile of v2, /device:TPU:0, one launch (start us, length us, event | category | flops | bytes accessed | tf_op | source)
XLA Modules:
  0.0 119.5 jit_solution(11249792196874626900)
XLA Ops:
  0.6 4.8 %collective-permute-start.22 = (bf16[256,4096]{1,0:T(8,128)(2,1)}, bf16[256,4096]{1,0:T(8,128)(2,1)S(1)}, u32[]{:S(2)}, u32[]{:S(2)}) collective-permute-start(bf16[256,4096]{1,0:T(8,128)(2,1)} %param.19), channel_id=1, source_target_pairs={{0,2},{2,0},{4,6},{6,4},{8,10},{10,8},{12,14},{14,12},{16,18},{18,... | collective-permute-start | bytes 6291464 | tf_op jit(solution)/shard_map/ppermute | solution.py:523
  5.5 15.0 %conditional.7 = (f32[64,256]{1,0:T(8,128)}, f32[64,256]{1,0:T(8,128)}, f32[128,256]{1,0:T(8,128)}, f32[128,256]{1,0:T(8,128)}, f32[64,256]{1,0:T(8,128)S(1)}, /*index=5*/bf16[256,4096]{1,0:T(8,128)(2,1)}) conditional(s32[]{:T(128)} %convert_element_type.45, () %tuple.103, (bf16[256,4096]{1,0:T(8,128)(2,1)}, f32[2,32,4096]{2,1,0:T(8,128)}, ...), branch_computations={%region_0.1_spmd, %region_1.2_spmd} | conditional | flops 229376 | bytes 18352364 | solution.py:544
  5.5 3.2 %project.1 = f32[64,256]{1,0:T(8,128)} custom-call(bf16[256,4096]{1,0:T(8,128)(2,1)} %get-tuple-element.128.x_ref, f32[2,32,4096]{2,1,0:T(8,128)} %get-tuple-element.126.r_ref), custom_call_target="tpu_custom_call" | custom-call | flops 98304 | bytes 768 | tf_op jit(solution)/shard_map/cond/branch_1_fun/project/pallas_call | solution.py:79
  12.7 3.8 %feedback.1 = f32[64,256]{1,0:T(8,128)S(1)} custom-call(f32[2,32,4096]{2,1,0:T(8,128)} %get-tuple-element.126.r_ref, bf16[2,4096,256]{2,1,0:T(8,128)(2,1)} %get-tuple-element.127.e_ref), custom_call_target="tpu_custom_call" | custom-call | flops 98304 | bytes 1280 | tf_op jit(solution)/shard_map/cond/branch_1_fun/feedback/pallas_call | solution.py:109
  22.7 19.9 %conditional.8 = (f32[64,256]{1,0:T(8,128)S(1)}, bf16[512,2048]{1,0:T(8,128)(2,1)}, bf16[512,2048]{1,0:T(8,128)(2,1)}, bf16[512,2048]{1,0:T(8,128)(2,1)}, bf16[5...) conditional(s32[]{:T(128)} %convert_element_type.45, () %tuple.102, (s32[1]{0:T(128)}, f32[64,256]{1,0:T(8,128)}, ...), branch_computations={%region_2.3_spmd, %region_3.4_spmd} | conditional | flops 2171008 | bytes 18156792 | solution.py:544
  26.0 4.7 %grad.2 = (bf16[512,2048]{1,0:T(8,128)(2,1)}, bf16[512,2048]{1,0:T(8,128)(2,1)S(1)}) custom-call(s32[1]{0:T(128)} %get-tuple-element.130.t_ref, bf16[2,1024,256]{2,1,0:T(8,128)(2,1)S(1)} %get-tuple-element.135.g_ref, bf16[2,4096,256]{2,1,0:T(8,128)(2,1)} %get-tuple-element.141.w_ref), custom_call_target="tpu_custom_call" | custom-call | flops 1048576 | bytes 1024 | tf_op jit(solution)/shard_map/cond/branch_1_fun/grad/pallas_call | solution.py:386
  33.5 4.7 %grad.3 = (bf16[512,2048]{1,0:T(8,128)(2,1)}, bf16[512,2048]{1,0:T(8,128)(2,1)S(1)}) custom-call(s32[1]{0:T(128)} %get-tuple-element.130.t_ref, bf16[2,1024,256]{2,1,0:T(8,128)(2,1)S(1)} %get-tuple-element.135.g_ref, bf16[2,4096,256]{2,1,0:T(8,128)(2,1)} %get-tuple-element.141.w_ref), custom_call_target="tpu_custom_call" | custom-call | flops 1048576 | bytes 1024 | tf_op jit(solution)/shard_map/cond/branch_1_fun/grad/pallas_call | solution.py:386
  44.3 12.4 %conditional.9 = (f32[64,256]{1,0:T(8,128)S(1)}, f32[64,256]{1,0:T(8,128)S(1)}, f32[160,256]{1,0:T(8,128)}, f32[160,256]{1,0:T(8,128)}, f32[160,256]{1,0:T(8,128...) conditional(s32[]{:T(128)} %convert_element_type.45, () %tuple.101, (s32[1]{0:T(128)}, ...), branch_computations={%region_4.5_spmd, %region_5.6_spmd} | conditional | flops 123008 | bytes 3310768 | solution.py:544
  48.9 3.5 %pair_sum.3 = (bf16[256,512]{1,0:T(8,128)(2,1)}, bf16[256,1536]{1,0:T(8,128)(2,1)}) custom-call(bf16[512,2048]{1,0:T(8,128)(2,1)} %get-tuple-element.158.a_ref, bf16[512,2048]{1,0:T(8,128)(2,1)} %get-tuple-element.159.b_ref), custom_call_target="tpu_custom_call" | custom-call | flops 128 | bytes 768 | tf_op jit(solution)/shard_map/cond/branch_1_fun/pair_sum/pallas_call | solution.py:423
  52.4 2.8 %collective-permute-start.11 = (f32[160,256]{1,0:T(8,128)}, f32[160,256]{1,0:T(8,128)}, u32[]{:S(2)}, u32[]{:S(2)}) collective-permute-start(f32[160,256]{1,0:T(8,128)} %collective-permute-done.10), channel_id=1, source_target_pairs={{0,1},{1,0},{2,3},{3,2},{4,5},{5,4},{6,7},{7,6},{8,9},{9,8},{10,11... | collective-permute-start | bytes 491528 | tf_op jit(solution)/shard_map/cond/branch_1_fun/ppermute | solution.py:519
  58.7 15.5 %conditional.10 = (f32[64,256]{1,0:T(8,128)}, bf16[64,1024]{1,0:T(8,128)(2,1)}, f32[64,1024]{1,0:T(8,128)S(1)}, bf16[256,4096]{1,0:T(8,128)(2,1)}, bf16[256,4096]{1,0:T(8,128)(2,1)}) conditional(s32[]{:T(128)} %convert_element_type.45, () %tuple.100, (s32[1]{0:T(128)}, f32[64,256]{1,0:T(8,128)S(1)}, f32[64,256]{1,0:T(8,128)S(1)}, ...), branch_computations={%region_6.7_spmd, %region_7.8_spmd} | conditional | flops 461212 | bytes 20582584 | solution.py:544
  59.3 4.7 %solve.1 = (f32[64,256]{1,0:T(8,128)S(1)}, f32[64,256]{1,0:T(8,128)}) custom-call(s32[1]{0:T(128)} %get-tuple-element.163.t_ref, f32[64,256]{1,0:T(8,128)S(1)} %get-tuple-element.164.own_ref, f32[64,256]{1,0:T(8,128)} %copy-done.7, f32[160,256]{1,0:T(8,128)} %get-tuple-element.166.chip_ref, f32[160,256]{1,0:T(8,128)} %get-tuple-element.167.got0, ...), custom_call_target="tpu_custom_call" | custom-call | flops 2441 | bytes 2441 | tf_op jit(solution)/shard_map/cond/branch_1_fun/solve/pallas_call | solution.py:226
  64.6 5.0 %right.1 = (f32[64,2048]{1,0:T(8,128)S(1)}, f32[64,2048]{1,0:T(8,128)S(1)}) custom-call(s32[4]{0:T(128)S(1)} %pad_add_fusion.h_ref, f32[64,256]{1,0:T(8,128)S(1)} %get-tuple-element.174.z_ref, f32[64,256]{1,0:T(8,128)} %get-tuple-element.370.b_ref, bf16[256,4096]{1,0:T(8,128)(2,1)S(1)} %get-tuple-element.175.x_ref, ...), custom_call_target="tpu_custom_call" | custom-call | flops 262144 | bytes 1536 | tf_op jit(solution)/shard_map/cond/branch_1_fun/right/pallas_call | solution.py:263
  74.2 18.6 %conditional.11 = (bf16[64,1024]{1,0:T(8,128)(2,1)S(1)}, f32[2,4096,256]{2,1,0:T(8,128)}) conditional(s32[]{:T(128)} %convert_element_type.45, () %tuple.99, (bf16[64,1024]{1,0:T(8,128)(2,1)}, bf16[2,1024,256]{2,1,0:T(8,128)(2,1)S(1)}, s32[1]{0:T(128)}, bf16[256,4096]{1,0:T(8,128)(2,1)S(1)}, bf16[256,4096]{1,0:T(8,128)(2,1)}, ...), branch_computations={%region_8.9_spmd, %region_9.10_spmd} | conditional | flops 1507328 | bytes 11278500 | solution.py:544
  75.8 4.1 %moment.4.refs_0_ = f32[2,4096,256]{2,1,0:T(8,128)} custom-call(s32[1]{0:T(128)} %get-tuple-element.185.t_ref, bf16[256,4096]{1,0:T(8,128)(2,1)S(1)} %get-tuple-element.186.x0, bf16[256,4096]{1,0:T(8,128)(2,1)} %get-tuple-element.187.x1, bf16[256,4096]{1,0:T(8,128)(2,1)} %get-tuple-element.188.a0, bf16[256,4096]{1,0:T(8,128)(2,1)} %get-tuple-element.189.a1, ...), custom_call_target="tpu_custom_call" | custom-call | flops 262144 | bytes 2048 | tf_op jit(solution)/shard_map/cond/branch_1_fun/moment/pallas_call | solution.py:307
  81.8 3.9 %moment.5.refs_0_ = f32[2,4096,256]{2,1,0:T(8,128)} custom-call(s32[1]{0:T(128)} %get-tuple-element.185.t_ref, bf16[256,4096]{1,0:T(8,128)(2,1)S(1)} %get-tuple-element.186.x0, bf16[256,4096]{1,0:T(8,128)(2,1)} %get-tuple-element.187.x1, bf16[256,4096]{1,0:T(8,128)(2,1)S(1)} %copy-done.5, ...), custom_call_target="tpu_custom_call", output_to_operand_aliasing={{}: (9, {})} | custom-call | flops 262144 | bytes 2048 | tf_op jit(solution)/shard_map/cond/branch_1_fun/moment/pallas_call | solution.py:307
  88.9 3.9 %moment.6 = f32[2,4096,256]{2,1,0:T(8,128)} custom-call(s32[1]{0:T(128)} %get-tuple-element.185.t_ref, bf16[256,4096]{1,0:T(8,128)(2,1)S(1)} %get-tuple-element.186.x0, bf16[256,4096]{1,0:T(8,128)(2,1)} %get-tuple-element.187.x1, bf16[256,4096]{1,0:T(8,128)(2,1)S(1)} %copy-done.5, ...), custom_call_target="tpu_custom_call", output_to_operand_aliasing={{}: (9, {})} | custom-call | flops 262144 | bytes 2048 | tf_op jit(solution)/shard_map/cond/branch_1_fun/moment/pallas_call | solution.py:307
  92.8 6.6 %conditional.12 = (bf16[64,1024]{1,0:T(8,128)(2,1)S(1)}, bf16[256,4096]{1,0:T(8,128)(2,1)}) conditional(s32[]{:T(128)} %convert_element_type.45, () %tuple.98, (bf16[64,1024]{1,0:T(8,128)(2,1)S(1)}, bf16[256,2048]{1,0:T(8,128)(2,1)}, bf16[512,2048]{1,0:T(8,128)(2,1)}, bf16[512,2048]{1,0:T(8,128)(2,1)}, bf16[512,2048]{1,0:T(8,128)(2,1)}, ...), branch_computations={%region_10.11_spmd, %region_11.12_spmd} | conditional | flops 327840 | bytes 2228244 | solution.py:544
  94.7 2.8 %finish_grad.3.refs_0_ = bf16[256,4096]{1,0:T(8,128)(2,1)} custom-call(bf16[512,2048]{1,0:T(8,128)(2,1)} %get-tuple-element.204.a_ref, bf16[512,2048]{1,0:T(8,128)(2,1)} %get-tuple-element.205.b_ref, bf16[256,2048]{1,0:T(8,128)(2,1)} %get-tuple-element.207.c_ref), custom_call_target="tpu_custom_call" | custom-call | flops 128 | bytes 768 | tf_op jit(solution)/shard_map/cond/branch_1_fun/finish_grad/pallas_call | solution.py:446
  99.9 10.8 %conditional.13 = (f32[2,4096,256]{2,1,0:T(8,128)}, f32[64,4096]{1,0:T(8,128)}, bf16[64,1024]{1,0:T(8,128)(2,1)}, bf16[64,1024]{1,0:T(8,128)(2,1)}) conditional(s32[]{:T(128)} %convert_element_type.45, () %tuple.97, (s32[]{:T(128)}, s32[]{:T(128)}, bf16[2,1024,256]{2,1,0:T(8,128)(2,1)}, bf16[64,1024]{1,0:T(8,128)(2,1)S(1)}, s32[1]{0:T(128)}, ...), branch_computations={%region_12.13_spmd, %region_13.14_spmd} | conditional | flops 262390 | bytes 9965764 | solution.py:544
  101.2 4.4 %moment.7.m_ref = f32[2,4096,256]{2,1,0:T(8,128)} custom-call(s32[1]{0:T(128)} %get-tuple-element.211.t_ref, bf16[256,4096]{1,0:T(8,128)(2,1)} %copy-done.2, bf16[256,4096]{1,0:T(8,128)(2,1)} %get-tuple-element.213.x1, bf16[256,4096]{1,0:T(8,128)(2,1)} %get-tuple-element.214.a0, ...), custom_call_target="tpu_custom_call", output_to_operand_aliasing={{}: (9, {})} | custom-call | flops 262144 | bytes 2048 | tf_op jit(solution)/shard_map/cond/branch_1_fun/moment/pallas_call | solution.py:307
  105.8 4.8 %error.2 = (f32[2,4096,256]{2,1,0:T(8,128)}, f32[64,4096]{1,0:T(8,128)}) custom-call(s32[2]{0:T(128)S(1)} %pad_add_fusion.1.q_ref, f32[2,4096,256]{2,1,0:T(8,128)} %moment.7.m_ref, bf16[64,1024]{1,0:T(8,128)(2,1)S(1)} %get-tuple-element.219.r0, bf16[64,1024]{1,0:T(8,128)(2,1)S(1)} %collective-permute-done.19.r1, ...), custom_call_target="tpu_custom_call", output_to_operand_aliasing={{0}: (1, {})} | custom-call | flops 244 | bytes 2048 | tf_op jit(solution)/shard_map/cond/branch_1_fun/error/pallas_call | solution.py:351
  110.6 4.8 %error.3 = (f32[2,4096,256]{2,1,0:T(8,128)}, f32[64,4096]{1,0:T(8,128)}) custom-call(s32[2]{0:T(128)S(1)} %pad_add_fusion.2.q_ref, f32[2,4096,256]{2,1,0:T(8,128)} %get-tuple-element.311.m_ref, bf16[64,1024]{1,0:T(8,128)(2,1)} %get-tuple-element.312.r0, bf16[64,1024]{1,0:T(8,128)(2,1)} %get-tuple-element.313.r1, ...), custom_call_target="tpu_custom_call", output_to_operand_aliasing={{0}: (1, {}), {1}: (5, {})} | custom-call | flops 244 | bytes 2048 | tf_op jit(solution)/shard_map/error/pallas_call | solution.py:351
  116.3 3.2 %finish_grad.5 = bf16[256,4096]{1,0:T(8,128)(2,1)} custom-call(bf16[512,2048]{1,0:T(8,128)(2,1)} %get-tuple-element.283.a_ref, bf16[512,2048]{1,0:T(8,128)(2,1)} %get-tuple-element.284.b_ref, bf16[256,1536]{1,0:T(8,128)(2,1)S(1)} %collective-permute-done.26.c_ref, bf16[256,4096]{1,0:T(8,128)(2,1)} %get-tuple-element.320.refs_0_), custom_call_target="tpu_custom_call", output_to_operand_aliasing={{}: (3, {})} | custom-call | flops 96 | bytes 576 | tf_op jit(solution)/shard_map/finish_grad/pallas_call | solution.py:446
  (87 shorter events, 49.3 us)
Async XLA Ops:
  0.6 42.0 %collective-permute-start.22 = (bf16[256,4096]{1,0:T(8,128)(2,1)}, bf16[256,4096]{1,0:T(8,128)(2,1)S(1)}, u32[]{:S(2)}, u32[]{:S(2)}) collective-permute-start(bf16[256,4096]{1,0:T(8,128)(2,1)} %param.19), channel_id=1, source_target_pairs={{0,2},{2,0},{4,6},{6,4},{8,10},{10,8},{12,14},{14,12},{16,18},{18,... | collective-permute-start | bytes 6291464 | tf_op jit(solution)/shard_map/ppermute | solution.py:523
  10.3 6.1 %collective-permute-start.7 = (bf16[256,4096]{1,0:T(8,128)(2,1)S(1)}, bf16[256,4096]{1,0:T(8,128)(2,1)}, u32[]{:S(2)}, u32[]{:S(2)}) collective-permute-start(bf16[256,4096]{1,0:T(8,128)(2,1)S(1)} %copy-done.1), channel_id=1, source_target_pairs={{0,1},{1,0},{2,3},{3,2},{4,5},{5,4},{6,7},{7,6},{8,9},{9,8},{10,11... | collective-permute-start | bytes 6291464 | tf_op jit(solution)/shard_map/cond/branch_1_fun/ppermute | solution.py:519
  11.4 5.1 %collective-permute-start.6 = (f32[128,256]{1,0:T(8,128)S(1)}, f32[128,256]{1,0:T(8,128)}, u32[]{:S(2)}, u32[]{:S(2)}) collective-permute-start(f32[128,256]{1,0:T(8,128)S(1)} %pad_maximum_fusion), channel_id=1, source_target_pairs={{1,3},{3,1},{5,7},{7,5},{9,11},{11,9},{13,15},{15,13},{17,19},{19,... | collective-permute-start | bytes 393224 | tf_op jit(solution)/shard_map/cond/branch_1_fun/ppermute | solution.py:523
  16.5 4.1 %collective-permute-start.8 = (f32[128,256]{1,0:T(8,128)}, f32[128,256]{1,0:T(8,128)}, u32[]{:S(2)}, u32[]{:S(2)}) collective-permute-start(f32[128,256]{1,0:T(8,128)} %collective-permute-done.6), channel_id=1, source_target_pairs={{0,1},{1,0},{2,3},{3,2},{4,5},{5,4},{6,7},{7,6},{8,9},{9,8},{10,11... | collective-permute-start | bytes 393224 | tf_op jit(solution)/shard_map/cond/branch_1_fun/ppermute | solution.py:519
  20.5 36.1 %collective-permute-start.23 = (bf16[256,4096]{1,0:T(8,128)(2,1)}, bf16[256,4096]{1,0:T(8,128)(2,1)}, u32[]{:S(2)}, u32[]{:S(2)}) collective-permute-start(bf16[256,4096]{1,0:T(8,128)(2,1)} %get-tuple-element.288), channel_id=1, source_target_pairs={{0,2},{2,0},{4,6},{6,4},{8,10},{10,8},{12,14},{14,12},{16,18},{18,... | collective-permute-start | bytes 6291464 | tf_op jit(solution)/shard_map/ppermute | solution.py:523
  24.1 6.6 %collective-permute-start = (f32[64,256]{1,0:T(8,128)S(1)}, f32[64,256]{1,0:T(8,128)S(1)}, u32[]{:S(2)}, u32[]{:S(2)}) collective-permute-start(f32[64,256]{1,0:T(8,128)S(1)} %left.1), channel_id=1, source_target_pairs={{0,8},{1,5},{2,10},{3,7},{4,12},{5,1},{6,14},{7,3},{8,0},{9,13},{1... | collective-permute-start | bytes 196616 | tf_op jit(solution)/shard_map/cond/branch_1_fun/ppermute | solution.py:531
  30.7 7.4 %collective-permute-start.2 = (bf16[512,2048]{1,0:T(8,128)(2,1)S(1)}, bf16[512,2048]{1,0:T(8,128)(2,1)}, u32[]{:S(2)}, u32[]{:S(2)}) collective-permute-start(bf16[512,2048]{1,0:T(8,128)(2,1)S(1)} %get-tuple-element.145), channel_id=1, source_target_pairs={{0,1},{1,0},{2,3},{3,2},{4,5},{5,4},{6,7},{7,6},{8,9},{9,8},{10,11... | collective-permute-start | bytes 6291464 | tf_op jit(solution)/shard_map/cond/branch_1_fun/ppermute | solution.py:519
  30.8 7.4 %collective-permute-start.1 = (f32[64,256]{1,0:T(8,128)S(1)}, f32[64,256]{1,0:T(8,128)S(1)}, u32[]{:S(2)}, u32[]{:S(2)}) collective-permute-start(f32[64,256]{1,0:T(8,128)S(1)} %add.30), channel_id=1, source_target_pairs={{0,16},{1,9},{2,18},{3,11},{4,20},{5,13},{6,22},{7,15},{8,24},{9,1... | collective-permute-start | bytes 196616 | tf_op jit(solution)/shard_map/cond/branch_1_fun/ppermute | solution.py:531
  38.2 4.4 %collective-permute-start.4 = (bf16[512,2048]{1,0:T(8,128)(2,1)S(1)}, bf16[512,2048]{1,0:T(8,128)(2,1)}, u32[]{:S(2)}, u32[]{:S(2)}) collective-permute-start(bf16[512,2048]{1,0:T(8,128)(2,1)S(1)} %get-tuple-element.149), channel_id=1, source_target_pairs={{0,1},{1,0},{2,3},{3,2},{4,5},{5,4},{6,7},{7,6},{8,9},{9,8},{10,11... | collective-permute-start | bytes 6291464 | tf_op jit(solution)/shard_map/cond/branch_1_fun/ppermute | solution.py:519
  38.2 4.3 %collective-permute-start.3 = (f32[64,256]{1,0:T(8,128)S(1)}, f32[64,256]{1,0:T(8,128)S(1)}, u32[]{:S(2)}, u32[]{:S(2)}) collective-permute-start(f32[64,256]{1,0:T(8,128)S(1)} %add.31), channel_id=1, source_target_pairs={{0,4},{1,17},{2,6},{3,19},{4,0},{5,21},{6,2},{7,23},{8,12},{9,25},... | collective-permute-start | bytes 196616 | tf_op jit(solution)/shard_map/cond/branch_1_fun/ppermute | solution.py:531
  47.6 4.8 %collective-permute-start.10 = (f32[160,256]{1,0:T(8,128)}, f32[160,256]{1,0:T(8,128)}, u32[]{:S(2)}, u32[]{:S(2)}) collective-permute-start(f32[160,256]{1,0:T(8,128)} %slice_add_fusion), channel_id=1, source_target_pairs={{1,3},{3,1},{5,7},{7,5},{9,11},{11,9},{13,15},{15,13},{17,19},{19,... | collective-permute-start | bytes 491528 | tf_op jit(solution)/shard_map/cond/branch_1_fun/ppermute | solution.py:523
  52.4 4.2 %collective-permute-start.11 = (f32[160,256]{1,0:T(8,128)}, f32[160,256]{1,0:T(8,128)}, u32[]{:S(2)}, u32[]{:S(2)}) collective-permute-start(f32[160,256]{1,0:T(8,128)} %collective-permute-done.10), channel_id=1, source_target_pairs={{0,1},{1,0},{2,3},{3,2},{4,5},{5,4},{6,7},{7,6},{8,9},{9,8},{10,11... | collective-permute-start | bytes 491528 | tf_op jit(solution)/shard_map/cond/branch_1_fun/ppermute | solution.py:519
  56.6 36.2 %collective-permute-start.24 = (bf16[256,2048]{1,0:T(8,128)(2,1)}, bf16[256,2048]{1,0:T(8,128)(2,1)}, u32[]{:S(2)}, u32[]{:S(2)}) collective-permute-start(bf16[256,2048]{1,0:T(8,128)(2,1)} %copy-done.6), channel_id=1, source_target_pairs={{0,2},{1,3},{2,0},{3,1},{4,6},{5,7},{6,4},{7,5},{8,10},{9,11},{10,... | collective-permute-start | bytes 3145736 | tf_op jit(solution)/shard_map/ppermute | solution.py:523
  64.0 5.6 %collective-permute-start.13 = (bf16[256,4096]{1,0:T(8,128)(2,1)}, bf16[256,4096]{1,0:T(8,128)(2,1)}, u32[]{:S(2)}, u32[]{:S(2)}) collective-permute-start(bf16[256,4096]{1,0:T(8,128)(2,1)} %get-tuple-element.181), channel_id=1, source_target_pairs={{0,1},{1,0},{2,3},{3,2},{4,5},{5,4},{6,7},{7,6},{8,9},{9,8},{10,11... | collective-permute-start | bytes 6291464 | tf_op jit(solution)/shard_map/cond/branch_1_fun/ppermute | solution.py:519
  64.1 7.4 %collective-permute-start.12 = (bf16[256,4096]{1,0:T(8,128)(2,1)}, bf16[256,4096]{1,0:T(8,128)(2,1)}, u32[]{:S(2)}, u32[]{:S(2)}) collective-permute-start(bf16[256,4096]{1,0:T(8,128)(2,1)} %get-tuple-element.179), channel_id=1, source_target_pairs={{0,1},{1,0},{2,3},{3,2},{4,5},{5,4},{6,7},{7,6},{8,9},{9,8},{10,11... | collective-permute-start | bytes 6291464 | tf_op jit(solution)/shard_map/cond/branch_1_fun/ppermute | solution.py:519
  74.2 18.7 %collective-permute-start.25 = (bf16[256,512]{1,0:T(8,128)(2,1)}, bf16[256,512]{1,0:T(8,128)(2,1)}, u32[]{:S(2)}, u32[]{:S(2)}) collective-permute-start(bf16[256,512]{1,0:T(8,128)(2,1)} %get-tuple-element.302), channel_id=1, source_target_pairs={{0,2},{1,3},{2,0},{3,1},{4,6},{5,7},{6,4},{7,5},{8,10},{9,11},{10,... | collective-permute-start | bytes 786440 | tf_op jit(solution)/shard_map/ppermute | solution.py:523
  74.2 5.7 %collective-permute-start.15 = (bf16[64,1024]{1,0:T(8,128)(2,1)}, bf16[64,1024]{1,0:T(8,128)(2,1)S(1)}, u32[]{:S(2)}, u32[]{:S(2)}) collective-permute-start(bf16[64,1024]{1,0:T(8,128)(2,1)} %get-tuple-element.184), channel_id=1, source_target_pairs={{0,8},{1,5},{2,10},{3,7},{4,12},{5,1},{6,14},{7,3},{8,0},{9,13},{1... | collective-permute-start | bytes 393224 | tf_op jit(solution)/shard_map/cond/branch_1_fun/ppermute | solution.py:531
  79.9 7.3 %collective-permute-start.16 = (bf16[64,1024]{1,0:T(8,128)(2,1)S(1)}, bf16[64,1024]{1,0:T(8,128)(2,1)S(1)}, u32[]{:S(2)}, u32[]{:S(2)}) collective-permute-start(bf16[64,1024]{1,0:T(8,128)(2,1)S(1)} %add_convert_fusion.2), channel_id=1, source_target_pairs={{0,16},{1,9},{2,18},{3,11},{4,20},{5,13},{6,22},{7,15},{8,24},{9,1... | collective-permute-start | bytes 393224 | tf_op jit(solution)/shard_map/cond/branch_1_fun/ppermute | solution.py:531
  87.3 5.5 %collective-permute-start.17 = (bf16[64,1024]{1,0:T(8,128)(2,1)S(1)}, bf16[64,1024]{1,0:T(8,128)(2,1)S(1)}, u32[]{:S(2)}, u32[]{:S(2)}) collective-permute-start(bf16[64,1024]{1,0:T(8,128)(2,1)S(1)} %add_convert_fusion.1), channel_id=1, source_target_pairs={{0,4},{1,17},{2,6},{3,19},{4,0},{5,21},{6,2},{7,23},{8,12},{9,25},... | collective-permute-start | bytes 393224 | tf_op jit(solution)/shard_map/cond/branch_1_fun/ppermute | solution.py:531
  92.8 6.6 %collective-permute-start.18 = (bf16[64,1024]{1,0:T(8,128)(2,1)S(1)}, bf16[64,1024]{1,0:T(8,128)(2,1)S(1)}, u32[]{:S(2)}, u32[]{:S(2)}) collective-permute-start(bf16[64,1024]{1,0:T(8,128)(2,1)S(1)} %get-tuple-element.200), channel_id=1, source_target_pairs={{0,2},{1,3},{2,0},{3,1},{4,6},{5,7},{6,4},{7,5},{8,10},{9,11},{10,... | collective-permute-start | bytes 393224 | tf_op jit(solution)/shard_map/cond/branch_1_fun/ppermute | solution.py:523
  99.5 16.9 %collective-permute-start.26 = (bf16[256,1536]{1,0:T(8,128)(2,1)}, bf16[256,1536]{1,0:T(8,128)(2,1)S(1)}, u32[]{:S(2)}, u32[]{:S(2)}) collective-permute-start(bf16[256,1536]{1,0:T(8,128)(2,1)} %get-tuple-element.318), channel_id=1, source_target_pairs={{0,2},{1,3},{2,0},{3,1},{4,6},{5,7},{6,4},{7,5},{8,10},{9,11},{10,... | collective-permute-start | bytes 2359304 | tf_op jit(solution)/shard_map/ppermute | solution.py:523
  99.9 5.8 %collective-permute-start.20 = (bf16[64,1024]{1,0:T(8,128)(2,1)S(1)}, bf16[64,1024]{1,0:T(8,128)(2,1)}, u32[]{:S(2)}, u32[]{:S(2)}) collective-permute-start(bf16[64,1024]{1,0:T(8,128)(2,1)S(1)} %get-tuple-element.219.r0), channel_id=1, source_target_pairs={{0,8},{1,5},{2,10},{3,7},{4,12},{5,1},{6,14},{7,3},{8,0},{9,13},{1... | collective-permute-start | bytes 393224 | tf_op jit(solution)/shard_map/cond/branch_1_fun/ppermute | solution.py:531
  99.9 5.9 %collective-permute-start.19 = (bf16[64,1024]{1,0:T(8,128)(2,1)S(1)}, bf16[64,1024]{1,0:T(8,128)(2,1)S(1)}, u32[]{:S(2)}, u32[]{:S(2)}) collective-permute-start(bf16[64,1024]{1,0:T(8,128)(2,1)S(1)} %get-tuple-element.219.r0), channel_id=1, source_target_pairs={{0,1},{1,0},{2,3},{3,2},{4,5},{5,4},{6,7},{7,6},{8,9},{9,8},{10,11... | collective-permute-start | bytes 393224 | tf_op jit(solution)/shard_map/cond/branch_1_fun/ppermute | solution.py:519
  105.7 5.0 %collective-permute-start.21 = (bf16[64,1024]{1,0:T(8,128)(2,1)}, bf16[64,1024]{1,0:T(8,128)(2,1)}, u32[]{:S(2)}, u32[]{:S(2)}) collective-permute-start(bf16[64,1024]{1,0:T(8,128)(2,1)} %collective-permute-done.20), channel_id=1, source_target_pairs={{0,1},{1,0},{2,3},{3,2},{4,5},{5,4},{6,7},{7,6},{8,9},{9,8},{10,11... | collective-permute-start | bytes 393224 | tf_op jit(solution)/shard_map/cond/branch_1_fun/ppermute | solution.py:519
  (11 other events, 53.4 us)

commit v3 on v2

--- a/solution.py
+++ b/solution.py
@@ -11,8 +11,9 @@
 SCALE = TOKENS ** (-0.5)
 F32, BF16 = jnp.float32, jnp.bfloat16
 WEIGHT = 4096
-SECOND_PIECES = (1, 3)
-VMEM_LIMIT = 20 * 1024 * 1024
+MOMENT_STEPS = 2
+SECOND_PIECES = (6, 10)
+VMEM_LIMIT = 12 * 1024 * 1024
 NN = (((1,), (0,)), ((), ()))
 NT = (((1,), (1,)), ((), ()))
 TN = (((0,), (0,)), ((), ()))
@@ -235,52 +236,52 @@
 
 
 def right_kernel(h_ref, z_ref, b_ref, x_ref, e_ref, near_ref, own_ref):
-    modes = e_ref.shape[0]
+    modes, width, _ = e_ref.shape
     rank = z_ref.shape[0] // modes
     product = split_mm(z_ref[...], x_ref[...], NN, 2)
     parts = []
     for m in range(modes):
         at = slice(m * rank, (m + 1) * rank)
         parts.append(product[at] + split_mm(b_ref[at, :], e_ref[m], NT, 2))
+    whole = jnp.concatenate(parts, axis=0)
+    low, high = whole[:, : width // 2], whole[:, width // 2 :]
     i = pl.program_id(0)
-
-    @pl.when(i < 2)
+    keep_high = h_ref[2 + i] == 1
+    ordered = jnp.concatenate([jnp.where(keep_high, low, high), jnp.where(keep_high, high, low)], axis=1)
+
+    @pl.when(i == 0)
     def _():
-        near_ref[...] = jnp.concatenate(parts, axis=0)
-
-    @pl.when(i >= 2)
+        near_ref[...] = ordered
+
+    @pl.when(i == 1)
     def _():
-        own_ref[...] = jnp.concatenate(parts, axis=0)
+        own_ref[...] = ordered
 
 
 def right_halves(core, bit, bit_near, z, b, x, e):
     rows, depth = x.shape
     modes, _, cols = e.shape
-    chunk = depth // 4
-    at, at_near = core * 2 + bit, (1 - core) * 2 + bit_near
-    place = jnp.stack([at_near ^ 1, at_near, at ^ 1, at])
-    shape = jax.ShapeDtypeStruct((z.shape[0], depth // 2), F32)
+    width = depth // 2
+    shape = jax.ShapeDtypeStruct((z.shape[0], width), F32)
+    whole = pl.BlockSpec(shape.shape, lambda i, h: (0, 0))
     return pl.pallas_call(
         right_kernel,
         grid_spec=pltpu.PrefetchScalarGridSpec(
             num_scalar_prefetch=1,
-            grid=(4,),
+            grid=(2,),
             in_specs=[
                 pl.BlockSpec(z.shape, lambda i, h: (0, 0)),
                 pl.BlockSpec(b.shape, lambda i, h: (0, 0)),
-                pl.BlockSpec((rows, chunk), lambda i, h: (0, h[i])),
-                pl.BlockSpec((modes, chunk, cols), lambda i, h: (0, h[i], 0)),
+                pl.BlockSpec((rows, width), lambda i, h: (0, h[i])),
+                pl.BlockSpec((modes, width, cols), lambda i, h: (0, h[i], 0)),
             ],
-            out_specs=[
-                pl.BlockSpec((z.shape[0], chunk), lambda i, h: (0, jnp.minimum(i, 1))),
-                pl.BlockSpec((z.shape[0], chunk), lambda i, h: (0, jnp.maximum(i - 2, 0))),
-            ],
+            out_specs=[whole, whole],
         ),
         out_shape=[shape, shape],
         compiler_params=params("arbitrary"),
         cost_estimate=cost(8 * depth * rows * 128, x.nbytes + e.nbytes),
         name="right",
-    )(place, z, b, hbm(x), hbm(e))
+    )(jnp.stack([1 - core, core, bit_near, bit]), z, b, hbm(x), hbm(e))
 
 
 def moment_kernel(t_ref, x0, x1, a0, a1, b0, b1, g_ref, e_ref, *refs):
@@ -299,8 +300,9 @@
 def moment_quarter(quarter, t, xs, g, e, so_far=()):
     rows, depth = xs[0].shape
     modes, tokens, cols = g.shape
-    chunk = depth // 8
-    first = 2 * quarter
+    steps = MOMENT_STEPS
+    chunk = depth // 4 // steps
+    first = steps * quarter
     both = pl.BlockSpec((rows, chunk), lambda i, t: (0, first + i))
     on0 = pl.BlockSpec((rows, chunk), lambda i, t: (0, (first + i) * (1 - t[0] % 2)))
     on1 = pl.BlockSpec((rows, chunk), lambda i, t: (0, (first + i) * (t[0] % 2)))
@@ -308,7 +310,7 @@
         moment_kernel,
         grid_spec=pltpu.PrefetchScalarGridSpec(
             num_scalar_prefetch=1,
-            grid=(2,),
+            grid=(steps,),
             in_specs=[
                 both,
                 both,
@@ -327,7 +329,7 @@
         compiler_params=params("arbitrary"),
         cost_estimate=cost(2 * depth * modes * cols * tokens // 4, 8 * 2**20),
         name="moment",
-    )(t, hbm(xs[0]), *xs[1:], g, hbm(e), *so_far)
+    )(t, *xs, g, hbm(e), *so_far)
 
 
 def error_kernel(q_ref, m_ref, r0, r1, b_ref, *refs):
@@ -399,62 +401,57 @@
     )(t, g, hbm(w))
 
 
-def pair_kernel(sizes, a_ref, b_ref, *outs):
-    total = (a_ref[...].astype(F32) + b_ref[...].astype(F32)).astype(BF16)
-    chunk = total.shape[1]
-    i = pl.program_id(0)
+def pair_kernel(a0, b0, a1, b1, own_ref, *outs):
+    own_ref[...] = (a0[...].astype(F32) + b0[...].astype(F32)).astype(BF16)
+    total = (a1[...].astype(F32) + b1[...].astype(F32)).astype(BF16)
     first = 0
-    for size, out in zip(sizes, outs):
-        for u in range(size):
-
-            @pl.when(i == first + u)
-            def _(out=out, u=u):
-                out[:, u * chunk : (u + 1) * chunk] = total
-
-        first += size
-
-
-def pair_sum(a, b, sizes):
+    for out in outs:
+        out[...] = total[:, first : first + out.shape[1]]
+        first += out.shape[1]
+
+
+def pair_sum(a, b, sizes, steps=2):
     rows, width = a.shape
     rows //= 2
-    chunk = width // sum(sizes)
-    spec = pl.BlockSpec((rows, chunk), lambda i: (1, i))
-    shapes = [(rows, size * chunk) for size in sizes]
-    return pl.pallas_call(
-        partial(pair_kernel, sizes),
-        grid=(sum(sizes),),
-        in_specs=[spec, spec],
-        out_specs=[pl.BlockSpec(shape, lambda i: (0, 0)) for shape in shapes],
-        out_shape=[jax.ShapeDtypeStruct(shape, BF16) for shape in shapes],
+    widths = [width] + [width * size // sum(sizes) for size in sizes]
+    own = pl.BlockSpec((rows // steps, width), lambda i: (i, 0))
+    far = pl.BlockSpec((rows // steps, width), lambda i: (steps + i, 0))
+    return pl.pallas_call(
+        pair_kernel,
+        grid=(steps,),
+        in_specs=[own, own, far, far],
+        out_specs=[pl.BlockSpec((rows // steps, w), lambda i: (i, 0)) for w in widths],
+        out_shape=[jax.ShapeDtypeStruct((rows, w), BF16) for w in widths],
         compiler_params=params("arbitrary"),
-        cost_estimate=cost(rows * width, 6 * rows * width),
+        cost_estimate=cost(2 * rows * width, 12 * rows * width),
         name="pair_sum",
-    )(a, b)
-
-
-def finish_kernel(a_ref, b_ref, c_ref, *refs):
-    total = a_ref[...].astype(F32) + b_ref[...].astype(F32)
-    refs[-1][...] = (total + c_ref[...].astype(F32)).astype(BF16)
-
-
-def finish_grad(place, depth, keep, near, first, far, so_far=()):
-    rows, width = far.shape
-    chunk = depth // 8
-    if width % (2 * chunk) == 0 and place % 2 == 0 and first % 2 == 0:
-        chunk, place, first = 2 * chunk, place // 2, first // 2
-    mine = pl.BlockSpec((rows, chunk), lambda i: (0, first + i))
-    return pl.pallas_call(
-        finish_kernel,
-        grid=(width // chunk,),
-        in_specs=[mine, mine, pl.BlockSpec((rows, chunk), lambda i: (0, i))]
+    )(a, b, a, b)
+
+
+def finish_kernel(count, own_ref, *refs):
+    out_ref = refs[-1]
+    first = 0
+    for far_ref in refs[:count]:
+        at = slice(first, first + far_ref.shape[1])
+        out_ref[:, at] = (own_ref[:, at].astype(F32) + far_ref[...].astype(F32)).astype(BF16)
+        first = at.stop
+
+
+def finish_grad(half, own, fars, so_far=(), steps=2):
+    rows, width = own.shape
+    return pl.pallas_call(
+        partial(finish_kernel, len(fars)),
+        grid=(steps,),
+        in_specs=[pl.BlockSpec((rows // steps, width), lambda i: (i, 0))]
+        + [pl.BlockSpec((rows // steps, far.shape[1]), lambda i: (i, 0)) for far in fars]
         + [pl.BlockSpec(memory_space=pl.ANY)] * len(so_far),
-        out_specs=pl.BlockSpec((rows, chunk), lambda i: (0, place + i)),
-        out_shape=pltpu.HBM((rows, depth), BF16),
-        input_output_aliases={3: 0} if so_far else {},
+        out_specs=pl.BlockSpec((rows // steps, width), lambda i: (i, half)),
+        out_shape=pltpu.HBM((rows, 2 * width), BF16),
+        input_output_aliases={1 + len(fars): 0} if so_far else {},
         compiler_params=params("arbitrary"),
-        cost_estimate=cost(far.size, 3 * far.nbytes),
+        cost_estimate=cost(3 * rows * width, 8 * rows * width),
         name="finish_grad",
-    )(keep, near, far, *so_far)
+    )(own, *fars, *so_far)
 
 
 def compress(moments, right_prev):
@@ -545,20 +542,24 @@
 
     xa0 = cross(layer_input, 0)
 
-    def project_rows(x, r, errors):
-        y = project(x, r)
+    def project_rows(x, r):
+        x_near = swap(x)
+        y = project(tie(x, r), r)
         y_near = swap(y)
-        y_far = cross(jnp.concatenate([y, y_near], axis=0), 1)
-        x_near = swap(tie(x, y_near))
-        e = feedback(tie(r, y_near), errors)
-        y_far = tie(y_far, e, x_near)
-        return (y, y_near, swap(y_far), y_far), e, x_near
-
-    ys, e, x_near = together(project_rows, layer_input, right_factor, errors)
-    xb0 = cross(x_near, 0)
-
-    def left_factors(ys, e):
-        left = left_local(place, ys, kv_cotangent, e)
+        return x_near, y, y_near, jnp.concatenate([y, y_near], axis=0)
+
+    x_near, y, y_near, pair = together(project_rows, layer_input, right_factor)
+
+    def exchange(pair, r, errors):
+        y_far = cross(pair, 1)
+        e = feedback(tie(r, pair), errors)
+        return tie(y_far, e), e
+
+    y_far, e = together(exchange, pair, right_factor, errors)
+    xb0 = cross(tie(x_near, y_far), 0)
+
+    def left_factors(y, y_near, y_far, e):
+        left = left_local(place, (y, y_near, swap(y_far), y_far), kv_cotangent, e)
         grads = []
         for k in range(bits):
             arrived = hop(left, k)
@@ -570,40 +571,39 @@
                 arrived = tie(arrived, got0)
             elif k == 2:
                 got1 = swap(tie(grads[1][1], left))
-                (first,) = pair_sum(grads[0][0], tie(got0, left), (2,))
+                own0, first = pair_sum(grads[0][0], tie(got0, left), (1,))
                 arrived = tie(arrived, first, got1)
             left = left + arrived
-        return left, grads, got0, got1, first
-
-    left, grads, got0, got1, first = together(left_factors, ys, e)
-    (keep0, _), (keep1, _) = grads
+        return left, grads[1][0], got1, own0, first
+
+    left, keep1, got1, own0, first = together(left_factors, y, y_near, y_far, e)
     left, xa0 = lax.optimization_barrier((left, xa0))
 
-    def spread_out(left, keep1, got1):
+    def spread_out(left, keep1, got1, xa0):
         own, send, far = spread(place, left, kv_cotangent)
         near = swap(jnp.concatenate([send, far], axis=0))
         chip = far + near[n:]
         got = cross(chip, 1)
-        pieces = pair_sum(tie(keep1, chip), got1, SECOND_PIECES)
-        got = tie(got, *pieces)
-        return own, near[:n], chip, swap(got), got, pieces
-
-    own, near, chip, *gots, (second, third) = together(spread_out, left, keep1, got1)
-    chip, xb0, first = lax.optimization_barrier((chip, xb0, first))
-    first = cross(first)
-
-    def right_halves_of(own, near, chip, got0, got, left, xa0, xb0):
-        xa1 = swap(xa0)
+        xa1 = swap(tie(xa0, chip))
+        own1, *pieces = pair_sum(tie(keep1, chip), got1, SECOND_PIECES)
+        got = tie(got, xa1, own1, *pieces)
+        return own, near[:n], chip, swap(got), got, own1, pieces, xa1
+
+    own, near, chip, *gots, own1, (second, third), xa1 = together(spread_out, left, keep1, got1, xa0)
+    first = cross(tie(first, chip))
+    chip, xb0 = lax.optimization_barrier((chip, xb0))
+
+    def right_halves_of(own, near, chip, got0, got, left, xb0):
+        xb1 = swap(xb0)
         z, b = solve(place, own, near, chip, got0, got, left)
-        xb1 = swap(tie(xb0, z))
         half_near, half = right_halves(core, bit, bit_near, z, b, layer_input, errors)
-        half_near = swap(tie(half_near, xa1, xb1))
+        half_near = swap(tie(half_near, xb1))
         quarter = half.shape[1] // 2
         give = (half[:, :quarter] + half_near[:, :quarter]).astype(BF16)
-        return b, give, half[:, quarter:] + half_near[:, quarter:], xa1, xb1
-
-    args = (own, near, chip, *gots, left, xa0, xb0)
-    b, give, own, xa1, xb1 = together(right_halves_of, *args)
+        return b, give, half[:, quarter:] + half_near[:, quarter:], xb1
+
+    args = (own, near, chip, *gots, left, xb0)
+    b, give, own, xb1 = together(right_halves_of, *args)
     second = cross(tie(second, give))
 
     def moments_of(j, xs, after, *so_far):
@@ -623,29 +623,23 @@
     own, moments = together(right_sums, give, own, xs)
     own, first, second = lax.optimization_barrier((own, first, second))
 
-    def over_x(own, keep0, got0, first, keep1, got1, second):
+    def last_quarters(own, third, b, moments, xs, own0, first):
         arrived = cross(own)
-        grad = finish_grad(0, depth, keep0, got0, 0, tie(first, own))
-        grad = finish_grad(4, depth, keep1, got1, 0, second, (grad,))
-        own = own.astype(F32) + tie(arrived, grad).astype(F32)
-        return (own * (1.0 / replicas)).astype(BF16), grad
-
-    own, grad = together(over_x, own, keep0, got0, first, keep1, got1, second)
-    third = cross(tie(third, own))
-
-    def first_errors(own, b, moments, xs):
+        moments = moments_of(3, xs, own, moments)
+        own = own.astype(F32) + tie(arrived, moments).astype(F32)
+        own = lax.optimization_barrier((own * (1.0 / replicas)).astype(BF16))
+        third = cross(tie(third, own))
         other = hop(own, 0)
         near = swap(own)
-        moments = moments_of(3, xs, own, moments)
-        other = tie(other, moments)
+        after, right = error_quarters(places[:2], moments, (own, near), b)
+        other = tie(other, right)
         other_near = swap(other)
-        after, right = error_quarters(places[:2], moments, (own, near), b)
-        return after, right, other, tie(other_near, right)
-
-    after, right, other, other_near = together(first_errors, own, b, moments, xs)
-    after, right = error_quarters(places[2:], after, (other, other_near), b, (right,))
-    done = SECOND_PIECES[0]
-    grad = finish_grad(4 + done, depth, keep1, got1, done, tie(third, other_near), (grad,))
+        grad = finish_grad(0, own0, (tie(first, other),))
+        other_near = tie(other_near, grad)
+        return *error_quarters(places[2:], after, (other, other_near), b, (right,)), grad, third
+
+    after, right, grad, third = together(last_quarters, own, third, b, moments, xs, own0, first)
+    grad = finish_grad(1, own1, (second, third), (grad,))
     return (after[None], right.reshape(right_factor.shape), grad)
 
 

time: 120 us -> 112 us (0.933)
  Pallas kernels: 67.2 us -> 60.4 us
  starting transfers between devices: 32.7 us -> 36.7 us
  local copies, waits for them, and re-layouts: 3.54 us -> 1.35 us
  waiting for transfers between devices: 12.4 us -> 10.3 us
    pallas_call x5 -> x4, Pallas kernels: 13.2 us -> 8.63 us  [the longest x2 4.43 us: finish_grad(): pl.pallas_call(partial(finish_kernel, len(fars)), grid=(steps,), in_specs...]
    ppermute x12, waiting for transfers between devices: 9.1 us -> 6.49 us  [swap(): return lax.ppermute(value, 'tensor', [(i, i ^ 1) for i in range(tensor)])]
    ppermute x7, starting transfers between devices: 11.2 us -> 13.7 us  [hop(): return lax.ppermute(value, ('dp', 'tensor'), pairs)]
    ppermute x12, starting transfers between devices: 7.61 us -> 9.62 us  [swap(): return lax.ppermute(value, 'tensor', [(i, i ^ 1) for i in range(tensor)])]
    cond x8 -> x4, local copies, waits for them, and re-layouts: 1.89 us -> 0.01 us
    pallas_call x2, Pallas kernels: 9.41 us -> 8.15 us  [grad_half(): pl.pallas_call(grad_kernel, grid=(steps,), in_specs=[SMEM, pl.BlockSpec(g...]
  transfers between devices with their start and end apart: 27 -> 27, of which waited for: 9 -> 12; matrix products, arithmetic and copies ran while one was open for 2% -> 2% of each run, Pallas kernels for 54% -> 52%
where the time goes in v3:
time: 112 us
  Pallas kernels  60.4 us (54%)
  starting transfers between devices  36.7 us (33%)
  waiting for transfers between devices  10.3 us (9%)
  other arithmetic  2.04 us (2%)
  local copies, waits for them, and re-layouts  1.35 us (1%)
    pallas_call x4, Pallas kernels, moment_quarter(): pl.pallas_call(moment_kernel, grid_spec=pltpu.PrefetchScalarGridSpec(num_...  16 us
    ppermute x7, starting transfers between devices, hop(): return lax.ppermute(value, ('dp', 'tensor'), pairs)  13.7 us
    ppermute x8, starting transfers between devices, cross(): return lax.ppermute(value, 'tensor', [(i, i ^ 2) for i in cores])  13.4 us
    pallas_call x2, Pallas kernels, error_quarters(): pl.pallas_call(error_kernel, grid_spec=pltpu.PrefetchScalarGridSpec(num_s...  9.64 us
    ppermute x12, starting transfers between devices, swap(): return lax.ppermute(value, 'tensor', [(i, i ^ 1) for i in range(tensor)])  9.62 us
    pallas_call x2, Pallas kernels, grad_half(): pl.pallas_call(grad_kernel, grid=(steps,), in_specs=[SMEM, pl.BlockSpec(g...  8.15 us
    ppermute x12, waiting for transfers between devices, swap(): return lax.ppermute(value, 'tensor', [(i, i ^ 1) for i in range(tensor)])  6.49 us
    pallas_call x1, Pallas kernels, solve(): pl.pallas_call(solve_kernel, in_specs=[SMEM] + [VMEM] * 6, out_specs=[VME...  4.74 us
  transfers between devices with their start and end apart: 27, of which 12 were waited for; matrix products, arithmetic and copies ran while one was open for 2% of the time, Pallas kernels for 52%

profile of v3, /device:TPU:0, one launch (start us, length us, event | category | flops | bytes accessed | tf_op | source)
XLA Modules:
  0.0 111.7 jit_solution(1670019637298825955)
XLA Ops:
  0.6 4.8 %collective-permute-start.23 = (bf16[256,4096]{1,0:T(8,128)(2,1)}, bf16[256,4096]{1,0:T(8,128)(2,1)}, u32[]{:S(2)}, u32[]{:S(2)}) collective-permute-start(bf16[256,4096]{1,0:T(8,128)(2,1)} %param.19), channel_id=1, source_target_pairs={{0,2},{2,0},{4,6},{6,4},{8,10},{10,8},{12,14},{14,12},{16,18},{18,... | collective-permute-start | bytes 6291464 | tf_op jit(solution)/shard_map/ppermute | solution.py:520
  5.5 5.7 %conditional.7 = (bf16[256,4096]{1,0:T(8,128)(2,1)}, f32[64,256]{1,0:T(8,128)}, f32[64,256]{1,0:T(8,128)}, f32[128,256]{1,0:T(8,128)S(1)}) conditional(s32[]{:T(128)} %convert_element_type.45, () %tuple.110, (bf16[256,4096]{1,0:T(8,128)(2,1)}, f32[2,32,4096]{2,1,0:T(8,128)}) %tuple.111), branch_computations={%region_0.1_spmd, %region_1.2_spmd} | conditional | flops 131072 | bytes 8913776 | solution.py:541
  5.6 3.0 %project.1 = f32[64,256]{1,0:T(8,128)} custom-call(bf16[256,4096]{1,0:T(8,128)(2,1)} %get-tuple-element.138.x_ref, f32[2,32,4096]{2,1,0:T(8,128)} %get-tuple-element.139.r_ref), custom_call_target="tpu_custom_call" | custom-call | flops 98304 | bytes 768 | tf_op jit(solution)/shard_map/cond/branch_1_fun/project/pallas_call | solution.py:80
  11.3 5.2 %conditional.8 = (f32[128,256]{1,0:T(8,128)}, f32[64,256]{1,0:T(8,128)S(1)}) conditional(s32[]{:T(128)} %convert_element_type.45, () %tuple.109, (f32[128,256]{1,0:T(8,128)S(1)}, f32[2,32,4096]{2,1,0:T(8,128)}, bf16[2,4096,256]{2,1,0:T(8,128)(2,1)}) %tuple.141), branch_computations={%region_2.3_spmd, %region_3.4_spmd} | conditional | flops 98304 | bytes 525624 | solution.py:541
  12.7 3.8 %feedback.1 = f32[64,256]{1,0:T(8,128)S(1)} custom-call(f32[2,32,4096]{2,1,0:T(8,128)} %get-tuple-element.142.r_ref, bf16[2,4096,256]{2,1,0:T(8,128)(2,1)} %get-tuple-element.143.e_ref), custom_call_target="tpu_custom_call" | custom-call | flops 98304 | bytes 1280 | tf_op jit(solution)/shard_map/cond/branch_1_fun/feedback/pallas_call | solution.py:110
  18.4 22.4 %conditional.9 = (f32[64,256]{1,0:T(8,128)S(1)}, bf16[512,2048]{1,0:T(8,128)(2,1)S(1)}, bf16[512,2048]{1,0:T(8,128)(2,1)}, bf16[256,2048]{1,0:T(8,128)(2,1)}, bf16[256,2048]{1,0:T(8,128)(2,1)}) conditional(s32[]{:T(128)} %convert_element_type.45, () %tuple.108, (f32[128,256]{1,0:T(8,128)}, s32[1]{0:T(128)}, f32[64,256]{1,0:T(8,128)}, ...), branch_computations={%region_4.5_spmd, %region_5.6_spmd} | conditional | flops 2171136 | bytes 18681880 | solution.py:541
  18.5 2.9 %collective-permute-start.1 = (f32[128,256]{1,0:T(8,128)}, f32[128,256]{1,0:T(8,128)S(1)}, u32[]{:S(2)}, u32[]{:S(2)}) collective-permute-start(f32[128,256]{1,0:T(8,128)} %get-tuple-element.148.far1), channel_id=1, source_target_pairs={{0,1},{1,0},{2,3},{3,2},{4,5},{5,4},{6,7},{7,6},{8,9},{9,8},{10,11... | collective-permute-start | bytes 393224 | tf_op jit(solution)/shard_map/cond/branch_1_fun/ppermute | solution.py:516
  25.5 4.1 %grad.2 = (bf16[512,2048]{1,0:T(8,128)(2,1)S(1)}, bf16[512,2048]{1,0:T(8,128)(2,1)S(1)}) custom-call(s32[1]{0:T(128)} %get-tuple-element.145.t_ref, bf16[2,1024,256]{2,1,0:T(8,128)(2,1)S(1)} %get-tuple-element.149.g_ref, bf16[2,4096,256]{2,1,0:T(8,128)(2,1)} %get-tuple-element.155.w_ref), custom_call_target="tpu_custom_call" | custom-call | flops 1048576 | bytes 1024 | tf_op jit(solution)/shard_map/cond/branch_1_fun/grad/pallas_call | solution.py:388
  32.3 4.1 %grad.3 = (bf16[512,2048]{1,0:T(8,128)(2,1)S(1)}, bf16[512,2048]{1,0:T(8,128)(2,1)S(1)}) custom-call(s32[1]{0:T(128)} %get-tuple-element.145.t_ref, bf16[2,1024,256]{2,1,0:T(8,128)(2,1)S(1)} %get-tuple-element.149.g_ref, bf16[2,4096,256]{2,1,0:T(8,128)(2,1)} %get-tuple-element.155.w_ref), custom_call_target="tpu_custom_call" | custom-call | flops 1048576 | bytes 1024 | tf_op jit(solution)/shard_map/cond/branch_1_fun/grad/pallas_call | solution.py:388
  40.9 13.6 %conditional.10 = (f32[64,256]{1,0:T(8,128)}, f32[64,256]{1,0:T(8,128)}, f32[160,256]{1,0:T(8,128)}, f32[160,256]{1,0:T(8,128)}, f32[160,256]{1,0:T(8,128)}, /*i...) conditional(s32[]{:T(128)} %convert_element_type.45, () %tuple.107, ...), branch_computations={%region_6.7_spmd, %region_7.8_spmd} | conditional | flops 123136 | bytes 11700200 | solution.py:541
  45.6 2.7 %pair_sum.3 = (bf16[256,2048]{1,0:T(8,128)(2,1)}, bf16[256,768]{1,0:T(8,128)(2,1)}, bf16[256,1280]{1,0:T(8,128)(2,1)}) custom-call(bf16[512,2048]{1,0:T(8,128)(2,1)S(1)} %get-tuple-element.176.a0.a1, bf16[512,2048]{1,0:T(8,128)(2,1)} %get-tuple-element.177.b0.b1, bf16[512,2048]{1,0:T(8,128)(2,1)S(1)} %get-tuple-element.176.a0.a1, ...), custom_call_target="tpu_custom_call" | custom-call | flops 256 | bytes 1536 | tf_op jit(solution)/shard_map/cond/branch_1_fun/pair_sum/pallas_call | solution.py:419
  48.6 4.5 %collective-permute-start.12 = (f32[160,256]{1,0:T(8,128)}, f32[160,256]{1,0:T(8,128)}, u32[]{:S(2)}, u32[]{:S(2)}) collective-permute-start(f32[160,256]{1,0:T(8,128)} %collective-permute-done.10), channel_id=1, source_target_pairs={{0,1},{1,0},{2,3},{3,2},{4,5},{5,4},{6,7},{7,6},{8,9},{9,8},{10,11... | collective-permute-start | bytes 491528 | tf_op jit(solution)/shard_map/cond/branch_1_fun/ppermute | solution.py:516
  55.4 11.2 %conditional.11 = (f32[64,256]{1,0:T(8,128)}, bf16[64,1024]{1,0:T(8,128)(2,1)S(1)}, f32[64,1024]{1,0:T(8,128)S(1)}, bf16[256,4096]{1,0:T(8,128)(2,1)}) conditional(s32[]{:T(128)} %convert_element_type.45, () %tuple.106, (s32[1]{0:T(128)}, f32[64,256]{1,0:T(8,128)}, f32[64,256]{1,0:T(8,128)}, f32[160,256]{1,0:T(8,128)}, f32[160,256]{1,0:T(8,128)}, ...), branch_computations={%region_8.9_spmd, %region_9.10_spmd} | conditional | flops 461206 | bytes 11931685 | solution.py:541
  55.4 4.7 %solve.1 = (f32[64,256]{1,0:T(8,128)S(1)}, f32[64,256]{1,0:T(8,128)}) custom-call(s32[1]{0:T(128)} %get-tuple-element.182.t_ref, f32[64,256]{1,0:T(8,128)} %get-tuple-element.183.own_ref, f32[64,256]{1,0:T(8,128)} %get-tuple-element.184.near_ref, f32[160,256]{1,0:T(8,128)} %get-tuple-element.185.chip_ref, f32[160,256]{1,0:T(8,128)} %get-tuple-element.186.got0, ...), custom_call_target="tpu_custom_call" | custom-call | flops 2441 | bytes 2441 | tf_op jit(solution)/shard_map/cond/branch_1_fun/solve/pallas_call | solution.py:227
  60.3 4.2 %right.1 = (f32[64,2048]{1,0:T(8,128)S(1)}, f32[64,2048]{1,0:T(8,128)S(1)}) custom-call(s32[4]{0:T(128)S(1)} %pad_add_fusion.h_ref, f32[64,256]{1,0:T(8,128)S(1)} %get-tuple-element.193.z_ref, f32[64,256]{1,0:T(8,128)} %get-tuple-element.376.b_ref, bf16[256,4096]{1,0:T(8,128)(2,1)S(1)} %get-tuple-element.194.x_ref, ...), custom_call_target="tpu_custom_call" | custom-call | flops 262144 | bytes 1536 | tf_op jit(solution)/shard_map/cond/branch_1_fun/right/pallas_call | solution.py:267
  69.4 19.5 %conditional.12 = (bf16[64,1024]{1,0:T(8,128)(2,1)S(1)}, f32[2,4096,256]{2,1,0:T(8,128)}) conditional(s32[]{:T(128)} %convert_element_type.45, () %tuple.105, (bf16[64,1024]{1,0:T(8,128)(2,1)S(1)}, bf16[2,1024,256]{2,1,0:T(8,128)(2,1)S(1)}, s32[1]{0:T(128)}, bf16[256,4096]{1,0:T(8,128)(2,1)S(1)}, bf16[256,4096]{1,0:T(8,128)(2,1)}, ...), branch_computations={%region_10.11_spmd, %region_11.12_spmd} | conditional | flops 1507328 | bytes 8519702 | solution.py:541
  71.0 4.0 %moment.4.refs_0_ = f32[2,4096,256]{2,1,0:T(8,128)} custom-call(s32[1]{0:T(128)} %get-tuple-element.202.t_ref, bf16[256,4096]{1,0:T(8,128)(2,1)S(1)} %get-tuple-element.203.x0, bf16[256,4096]{1,0:T(8,128)(2,1)} %get-tuple-element.204.x1, bf16[256,4096]{1,0:T(8,128)(2,1)} %get-tuple-element.205.a0, bf16[256,4096]{1,0:T(8,128)(2,1)} %get-tuple-element.206.a1, ...), custom_call_target="tpu_custom_call" | custom-call | flops 262144 | bytes 2048 | tf_op jit(solution)/shard_map/cond/branch_1_fun/moment/pallas_call | solution.py:309
  75.0 2.7 %collective-permute-start.16 = (bf16[64,1024]{1,0:T(8,128)(2,1)S(1)}, bf16[64,1024]{1,0:T(8,128)(2,1)S(1)}, u32[]{:S(2)}, u32[]{:S(2)}) collective-permute-start(bf16[64,1024]{1,0:T(8,128)(2,1)S(1)} %add_convert_fusion.2), channel_id=1, source_target_pairs={{0,16},{1,9},{2,18},{3,11},{4,20},{5,13},{6,22},{7,15},{8,24},{9,1... | collective-permute-start | bytes 393224 | tf_op jit(solution)/shard_map/cond/branch_1_fun/ppermute | solution.py:528
  77.7 4.0 %moment.5.refs_0_ = f32[2,4096,256]{2,1,0:T(8,128)} custom-call(s32[1]{0:T(128)} %get-tuple-element.202.t_ref, bf16[256,4096]{1,0:T(8,128)(2,1)S(1)} %get-tuple-element.203.x0, bf16[256,4096]{1,0:T(8,128)(2,1)} %get-tuple-element.204.x1, bf16[256,4096]{1,0:T(8,128)(2,1)} %get-tuple-element.205.a0, ...), custom_call_target="tpu_custom_call", output_to_operand_aliasing={{}: (9, {})} | custom-call | flops 262144 | bytes 2048 | tf_op jit(solution)/shard_map/cond/branch_1_fun/moment/pallas_call | solution.py:309
  84.8 4.0 %moment.6 = f32[2,4096,256]{2,1,0:T(8,128)} custom-call(s32[1]{0:T(128)} %get-tuple-element.202.t_ref, bf16[256,4096]{1,0:T(8,128)(2,1)S(1)} %get-tuple-element.203.x0, bf16[256,4096]{1,0:T(8,128)(2,1)} %get-tuple-element.204.x1, bf16[256,4096]{1,0:T(8,128)(2,1)} %get-tuple-element.205.a0, ...), custom_call_target="tpu_custom_call", output_to_operand_aliasing={{}: (9, {})} | custom-call | flops 262144 | bytes 2048 | tf_op jit(solution)/shard_map/cond/branch_1_fun/moment/pallas_call | solution.py:309
  88.9 20.6 %conditional.13 = (bf16[256,4096]{1,0:T(8,128)(2,1)}, bf16[256,1280]{1,0:T(8,128)(2,1)}, f32[1,2,4096,256]{3,2,1,0:T(8,128)}, f32[2,32,4096]{2,1,0:T(8,128)}) conditional(s32[]{:T(128)} %convert_element_type.45, () %tuple.104, (bf16[64,1024]{1,0:T(8,128)(2,1)S(1)}, bf16[2,1024,256]{2,1,0:T(8,128)(2,1)S(1)}, s32[1]{0:T(128)}, ...), branch_computations={%region_12.13_spmd, %region_13.14_spmd} | conditional | flops 590707 | bytes 12189740 | solution.py:541
  89.1 4.0 %moment.7.m_ref = f32[2,4096,256]{2,1,0:T(8,128)} custom-call(s32[1]{0:T(128)} %get-tuple-element.220.t_ref, bf16[256,4096]{1,0:T(8,128)(2,1)S(1)} %get-tuple-element.221.x0, bf16[256,4096]{1,0:T(8,128)(2,1)} %get-tuple-element.222.x1, bf16[256,4096]{1,0:T(8,128)(2,1)} %get-tuple-element.223.a0, ...), custom_call_target="tpu_custom_call", output_to_operand_aliasing={{}: (9, {})} | custom-call | flops 262144 | bytes 2048 | tf_op jit(solution)/shard_map/cond/branch_1_fun/moment/pallas_call | solution.py:309
  96.4 4.8 %error.2 = (f32[2,4096,256]{2,1,0:T(8,128)}, f32[64,4096]{1,0:T(8,128)}) custom-call(s32[2]{0:T(128)S(1)} %pad_add_fusion.1.q_ref, f32[2,4096,256]{2,1,0:T(8,128)} %moment.7.m_ref, bf16[64,1024]{1,0:T(8,128)(2,1)S(1)} %multiply_convert_fusion.r0, bf16[64,1024]{1,0:T(8,128)(2,1)S(1)} %collective-permute-done.20.r1, ...), custom_call_target="tpu_custom_call", output_to_operand_aliasing={{0}: (1, {})} | custom-call | flops 244 | bytes 2048 | tf_op jit(solution)/shard_map/cond/branch_1_fun/error/pallas_call | solution.py:353
  104.0 4.8 %error.3 = (f32[2,4096,256]{2,1,0:T(8,128)}, f32[64,4096]{1,0:T(8,128)}) custom-call(s32[2]{0:T(128)S(1)} %pad_add_fusion.2.q_ref, f32[2,4096,256]{2,1,0:T(8,128)} %get-tuple-element.241.m_ref, bf16[64,1024]{1,0:T(8,128)(2,1)S(1)} %collective-permute-done.19.r0, ...), custom_call_target="tpu_custom_call", output_to_operand_aliasing={{0}: (1, {}), {1}: (5, {})} | custom-call | flops 244 | bytes 2048 | tf_op jit(solution)/shard_map/cond/branch_1_fun/error/pallas_call | solution.py:353
  (80 shorter events, 43.6 us)
Async XLA Ops:
  0.6 40.3 %collective-permute-start.23 = (bf16[256,4096]{1,0:T(8,128)(2,1)}, bf16[256,4096]{1,0:T(8,128)(2,1)}, u32[]{:S(2)}, u32[]{:S(2)}) collective-permute-start(bf16[256,4096]{1,0:T(8,128)(2,1)} %param.19), channel_id=1, source_target_pairs={{0,2},{2,0},{4,6},{6,4},{8,10},{10,8},{12,14},{14,12},{16,18},{18,... | collective-permute-start | bytes 6291464 | tf_op jit(solution)/shard_map/ppermute | solution.py:520
  5.5 5.7 %collective-permute-start.7 = (bf16[256,4096]{1,0:T(8,128)(2,1)}, bf16[256,4096]{1,0:T(8,128)(2,1)}, u32[]{:S(2)}, u32[]{:S(2)}) collective-permute-start(bf16[256,4096]{1,0:T(8,128)(2,1)} %get-tuple-element.138.x_ref), channel_id=1, source_target_pairs={{0,1},{1,0},{2,3},{3,2},{4,5},{5,4},{6,7},{7,6},{8,9},{9,8},{10,11... | collective-permute-start | bytes 6291464 | tf_op jit(solution)/shard_map/cond/branch_1_fun/ppermute | solution.py:516
  11.3 5.2 %collective-permute-start = (f32[128,256]{1,0:T(8,128)S(1)}, f32[128,256]{1,0:T(8,128)}, u32[]{:S(2)}, u32[]{:S(2)}) collective-permute-start(f32[128,256]{1,0:T(8,128)S(1)} %get-tuple-element.140), channel_id=1, source_target_pairs={{1,3},{3,1},{5,7},{7,5},{9,11},{11,9},{13,15},{15,13},{17,19},{19,... | collective-permute-start | bytes 393224 | tf_op jit(solution)/shard_map/cond/branch_1_fun/ppermute | solution.py:520
  16.5 38.9 %collective-permute-start.24 = (bf16[256,4096]{1,0:T(8,128)(2,1)}, bf16[256,4096]{1,0:T(8,128)(2,1)}, u32[]{:S(2)}, u32[]{:S(2)}) collective-permute-start(bf16[256,4096]{1,0:T(8,128)(2,1)} %get-tuple-element.302), channel_id=1, source_target_pairs={{0,2},{2,0},{4,6},{6,4},{8,10},{10,8},{12,14},{14,12},{16,18},{18,... | collective-permute-start | bytes 6291464 | tf_op jit(solution)/shard_map/ppermute | solution.py:520
  18.5 4.1 %collective-permute-start.1 = (f32[128,256]{1,0:T(8,128)}, f32[128,256]{1,0:T(8,128)S(1)}, u32[]{:S(2)}, u32[]{:S(2)}) collective-permute-start(f32[128,256]{1,0:T(8,128)} %get-tuple-element.148.far1), channel_id=1, source_target_pairs={{0,1},{1,0},{2,3},{3,2},{4,5},{5,4},{6,7},{7,6},{8,9},{9,8},{10,11... | collective-permute-start | bytes 393224 | tf_op jit(solution)/shard_map/cond/branch_1_fun/ppermute | solution.py:516
  23.8 5.7 %collective-permute-start.2 = (f32[64,256]{1,0:T(8,128)S(1)}, f32[64,256]{1,0:T(8,128)S(1)}, u32[]{:S(2)}, u32[]{:S(2)}) collective-permute-start(f32[64,256]{1,0:T(8,128)S(1)} %left.1), channel_id=1, source_target_pairs={{0,8},{1,5},{2,10},{3,7},{4,12},{5,1},{6,14},{7,3},{8,0},{9,13},{1... | collective-permute-start | bytes 196616 | tf_op jit(solution)/shard_map/cond/branch_1_fun/ppermute | solution.py:528
  29.6 6.8 %collective-permute-start.4 = (bf16[512,2048]{1,0:T(8,128)(2,1)S(1)}, bf16[512,2048]{1,0:T(8,128)(2,1)S(1)}, u32[]{:S(2)}, u32[]{:S(2)}) collective-permute-start(bf16[512,2048]{1,0:T(8,128)(2,1)S(1)} %get-tuple-element.159), channel_id=1, source_target_pairs={{0,1},{1,0},{2,3},{3,2},{4,5},{5,4},{6,7},{7,6},{8,9},{9,8},{10,11... | collective-permute-start | bytes 6291464 | tf_op jit(solution)/shard_map/cond/branch_1_fun/ppermute | solution.py:516
  29.7 6.7 %collective-permute-start.3 = (f32[64,256]{1,0:T(8,128)S(1)}, f32[64,256]{1,0:T(8,128)S(1)}, u32[]{:S(2)}, u32[]{:S(2)}) collective-permute-start(f32[64,256]{1,0:T(8,128)S(1)} %add.28), channel_id=1, source_target_pairs={{0,16},{1,9},{2,18},{3,11},{4,20},{5,13},{6,22},{7,15},{8,24},{9,1... | collective-permute-start | bytes 196616 | tf_op jit(solution)/shard_map/cond/branch_1_fun/ppermute | solution.py:528
  36.4 4.4 %collective-permute-start.6 = (bf16[512,2048]{1,0:T(8,128)(2,1)S(1)}, bf16[512,2048]{1,0:T(8,128)(2,1)}, u32[]{:S(2)}, u32[]{:S(2)}) collective-permute-start(bf16[512,2048]{1,0:T(8,128)(2,1)S(1)} %get-tuple-element.164), channel_id=1, source_target_pairs={{0,1},{1,0},{2,3},{3,2},{4,5},{5,4},{6,7},{7,6},{8,9},{9,8},{10,11... | collective-permute-start | bytes 6291464 | tf_op jit(solution)/shard_map/cond/branch_1_fun/ppermute | solution.py:516
  36.5 4.3 %collective-permute-start.5 = (f32[64,256]{1,0:T(8,128)S(1)}, f32[64,256]{1,0:T(8,128)S(1)}, u32[]{:S(2)}, u32[]{:S(2)}) collective-permute-start(f32[64,256]{1,0:T(8,128)S(1)} %add.29), channel_id=1, source_target_pairs={{0,4},{1,17},{2,6},{3,19},{4,0},{5,21},{6,2},{7,23},{8,12},{9,25},... | collective-permute-start | bytes 196616 | tf_op jit(solution)/shard_map/cond/branch_1_fun/ppermute | solution.py:528
  44.1 4.5 %collective-permute-start.11 = (bf16[256,4096]{1,0:T(8,128)(2,1)}, bf16[256,4096]{1,0:T(8,128)(2,1)}, u32[]{:S(2)}, u32[]{:S(2)}) collective-permute-start(bf16[256,4096]{1,0:T(8,128)(2,1)} %get-tuple-element.174), channel_id=1, source_target_pairs={{0,1},{1,0},{2,3},{3,2},{4,5},{5,4},{6,7},{7,6},{8,9},{9,8},{10,11... | collective-permute-start | bytes 6291464 | tf_op jit(solution)/shard_map/cond/branch_1_fun/ppermute | solution.py:516
  44.3 4.0 %collective-permute-start.10 = (f32[160,256]{1,0:T(8,128)}, f32[160,256]{1,0:T(8,128)}, u32[]{:S(2)}, u32[]{:S(2)}) collective-permute-start(f32[160,256]{1,0:T(8,128)} %slice_add_fusion), channel_id=1, source_target_pairs={{1,3},{3,1},{5,7},{7,5},{9,11},{11,9},{13,15},{15,13},{17,19},{19,... | collective-permute-start | bytes 491528 | tf_op jit(solution)/shard_map/cond/branch_1_fun/ppermute | solution.py:520
  48.6 5.9 %collective-permute-start.12 = (f32[160,256]{1,0:T(8,128)}, f32[160,256]{1,0:T(8,128)}, u32[]{:S(2)}, u32[]{:S(2)}) collective-permute-start(f32[160,256]{1,0:T(8,128)} %collective-permute-done.10), channel_id=1, source_target_pairs={{0,1},{1,0},{2,3},{3,2},{4,5},{5,4},{6,7},{7,6},{8,9},{9,8},{10,11... | collective-permute-start | bytes 491528 | tf_op jit(solution)/shard_map/cond/branch_1_fun/ppermute | solution.py:516
  54.5 34.4 %collective-permute-start.25 = (bf16[256,2048]{1,0:T(8,128)(2,1)}, bf16[256,2048]{1,0:T(8,128)(2,1)}, u32[]{:S(2)}, u32[]{:S(2)}) collective-permute-start(bf16[256,2048]{1,0:T(8,128)(2,1)} %get-tuple-element.313), channel_id=1, source_target_pairs={{0,2},{1,3},{2,0},{3,1},{4,6},{5,7},{6,4},{7,5},{8,10},{9,11},{10,... | collective-permute-start | bytes 3145736 | tf_op jit(solution)/shard_map/ppermute | solution.py:520
  55.4 9.0 %collective-permute-start.13 = (bf16[256,4096]{1,0:T(8,128)(2,1)}, bf16[256,4096]{1,0:T(8,128)(2,1)}, u32[]{:S(2)}, u32[]{:S(2)}) collective-permute-start(bf16[256,4096]{1,0:T(8,128)(2,1)} %get-tuple-element.198), channel_id=1, source_target_pairs={{0,1},{1,0},{2,3},{3,2},{4,5},{5,4},{6,7},{7,6},{8,9},{9,8},{10,11... | collective-permute-start | bytes 6291464 | tf_op jit(solution)/shard_map/cond/branch_1_fun/ppermute | solution.py:516
  64.5 2.1 %collective-permute-start.14 = (f32[64,2048]{1,0:T(8,128)S(1)}, f32[64,2048]{1,0:T(8,128)S(1)}, u32[]{:S(2)}, u32[]{:S(2)}) collective-permute-start(f32[64,2048]{1,0:T(8,128)S(1)} %get-tuple-element.199), channel_id=1, source_target_pairs={{0,1},{1,0},{2,3},{3,2},{4,5},{5,4},{6,7},{7,6},{8,9},{9,8},{10,11... | collective-permute-start | bytes 1572872 | tf_op jit(solution)/shard_map/cond/branch_1_fun/ppermute | solution.py:516
  67.3 21.5 %collective-permute-start.26 = (bf16[256,768]{1,0:T(8,128)(2,1)}, bf16[256,768]{1,0:T(8,128)(2,1)S(1)}, u32[]{:S(2)}, u32[]{:S(2)}) collective-permute-start(bf16[256,768]{1,0:T(8,128)(2,1)} %get-tuple-element.315), channel_id=1, source_target_pairs={{0,2},{1,3},{2,0},{3,1},{4,6},{5,7},{6,4},{7,5},{8,10},{9,11},{10,... | collective-permute-start | bytes 1179656 | tf_op jit(solution)/shard_map/ppermute | solution.py:520
  69.4 5.6 %collective-permute-start.15 = (bf16[64,1024]{1,0:T(8,128)(2,1)S(1)}, bf16[64,1024]{1,0:T(8,128)(2,1)S(1)}, u32[]{:S(2)}, u32[]{:S(2)}) collective-permute-start(bf16[64,1024]{1,0:T(8,128)(2,1)S(1)} %get-tuple-element.201), channel_id=1, source_target_pairs={{0,8},{1,5},{2,10},{3,7},{4,12},{5,1},{6,14},{7,3},{8,0},{9,13},{1... | collective-permute-start | bytes 393224 | tf_op jit(solution)/shard_map/cond/branch_1_fun/ppermute | solution.py:528
  75.0 7.3 %collective-permute-start.16 = (bf16[64,1024]{1,0:T(8,128)(2,1)S(1)}, bf16[64,1024]{1,0:T(8,128)(2,1)S(1)}, u32[]{:S(2)}, u32[]{:S(2)}) collective-permute-start(bf16[64,1024]{1,0:T(8,128)(2,1)S(1)} %add_convert_fusion.2), channel_id=1, source_target_pairs={{0,16},{1,9},{2,18},{3,11},{4,20},{5,13},{6,22},{7,15},{8,24},{9,1... | collective-permute-start | bytes 393224 | tf_op jit(solution)/shard_map/cond/branch_1_fun/ppermute | solution.py:528
  82.4 6.4 %collective-permute-start.17 = (bf16[64,1024]{1,0:T(8,128)(2,1)S(1)}, bf16[64,1024]{1,0:T(8,128)(2,1)S(1)}, u32[]{:S(2)}, u32[]{:S(2)}) collective-permute-start(bf16[64,1024]{1,0:T(8,128)(2,1)S(1)} %add_convert_fusion.1), channel_id=1, source_target_pairs={{0,4},{1,17},{2,6},{3,19},{4,0},{5,21},{6,2},{7,23},{8,12},{9,25},... | collective-permute-start | bytes 393224 | tf_op jit(solution)/shard_map/cond/branch_1_fun/ppermute | solution.py:528
  88.9 5.0 %collective-permute-start.18 = (bf16[64,1024]{1,0:T(8,128)(2,1)S(1)}, bf16[64,1024]{1,0:T(8,128)(2,1)S(1)}, u32[]{:S(2)}, u32[]{:S(2)}) collective-permute-start(bf16[64,1024]{1,0:T(8,128)(2,1)S(1)} %get-tuple-element.219), channel_id=1, source_target_pairs={{0,2},{1,3},{2,0},{3,1},{4,6},{5,7},{6,4},{7,5},{8,10},{9,11},{10,... | collective-permute-start | bytes 393224 | tf_op jit(solution)/shard_map/cond/branch_1_fun/ppermute | solution.py:520
  94.0 15.5 %collective-permute-start.21 = (bf16[256,1280]{1,0:T(8,128)(2,1)}, bf16[256,1280]{1,0:T(8,128)(2,1)}, u32[]{:S(2)}, u32[]{:S(2)}) collective-permute-start(bf16[256,1280]{1,0:T(8,128)(2,1)} %get-tuple-element.240), channel_id=1, source_target_pairs={{0,2},{1,3},{2,0},{3,1},{4,6},{5,7},{6,4},{7,5},{8,10},{9,11},{10,... | collective-permute-start | bytes 1966088 | tf_op jit(solution)/shard_map/cond/branch_1_fun/ppermute | solution.py:520
  95.1 6.2 %collective-permute-start.19 = (bf16[64,1024]{1,0:T(8,128)(2,1)S(1)}, bf16[64,1024]{1,0:T(8,128)(2,1)S(1)}, u32[]{:S(2)}, u32[]{:S(2)}) collective-permute-start(bf16[64,1024]{1,0:T(8,128)(2,1)S(1)} %multiply_convert_fusion.r0), channel_id=1, source_target_pairs={{0,8},{1,5},{2,10},{3,7},{4,12},{5,1},{6,14},{7,3},{8,0},{9,13},{1... | collective-permute-start | bytes 393224 | tf_op jit(solution)/shard_map/cond/branch_1_fun/ppermute | solution.py:528
  101.3 2.7 %collective-permute-start.22 = (bf16[64,1024]{1,0:T(8,128)(2,1)S(1)}, bf16[64,1024]{1,0:T(8,128)(2,1)S(1)}, u32[]{:S(2)}, u32[]{:S(2)}) collective-permute-start(bf16[64,1024]{1,0:T(8,128)(2,1)S(1)} %collective-permute-done.19.r0), channel_id=1, source_target_pairs={{0,1},{1,0},{2,3},{3,2},{4,5},{5,4},{6,7},{7,6},{8,9},{9,8},{10,11... | collective-permute-start | bytes 393224 | tf_op jit(solution)/shard_map/cond/branch_1_fun/ppermute | solution.py:516
  (8 other events, 36.5 us)

commit v4 on v3

--- a/solution.py
+++ b/solution.py
@@ -51,6 +51,10 @@
 
 SMEM = pl.BlockSpec(memory_space=pltpu.SMEM)
 VMEM = pl.BlockSpec(memory_space=pltpu.VMEM)
+
+
+def vmem(value):
+    return pltpu.with_memory_space_constraint(value, pltpu.VMEM)
 
 
 def hbm(value):
@@ -212,7 +216,7 @@
         a = jnp.where(row > k, a - column * (inverse * pivot_row), a)
     a = a * scale
     zero = jnp.zeros((rank, left_ref.shape[1]), F32)
-    z = (own_ref[...] + near_ref[...] + by_core(t_ref, got[0:n], got[n : 2 * n])) * SCALE
+    z = (own_ref[...] + near_ref[0:n, :] + by_core(t_ref, got[0:n], got[n : 2 * n])) * SCALE
     for m in range(modes):
         part = jnp.where(lane // rank == 2 * m + 1, a, 0.0)
         at = slice(m * rank, (m + 1) * rank)
@@ -591,36 +595,31 @@
 
     own, near, chip, *gots, own1, (second, third), xa1 = together(spread_out, left, keep1, got1, xa0)
     first = cross(tie(first, chip))
+    second = cross(tie(second, chip))
     chip, xb0 = lax.optimization_barrier((chip, xb0))
 
-    def right_halves_of(own, near, chip, got0, got, left, xb0):
+    def moments_of(j, xs, after, *so_far):
+        return moment_quarter(j, place, xs, tie(kv_cotangent, after), errors, so_far)
+
+    def right_sums(own, near, chip, got0, got, left, x_near, xa0, xa1, xb0):
         xb1 = swap(xb0)
         z, b = solve(place, own, near, chip, got0, got, left)
         half_near, half = right_halves(core, bit, bit_near, z, b, layer_input, errors)
         half_near = swap(tie(half_near, xb1))
         quarter = half.shape[1] // 2
         give = (half[:, :quarter] + half_near[:, :quarter]).astype(BF16)
-        return b, give, half[:, quarter:] + half_near[:, quarter:], xb1
-
-    args = (own, near, chip, *gots, left, xb0)
-    b, give, own, xb1 = together(right_halves_of, *args)
-    second = cross(tie(second, give))
-
-    def moments_of(j, xs, after, *so_far):
-        return moment_quarter(j, place, xs, tie(kv_cotangent, after), errors, so_far)
-
-    xs = (layer_input, x_near, xa0, xa1, xb0, xb1)
-
-    def right_sums(give, own, xs):
+        xs = (layer_input, x_near, xa0, xa1, xb0, xb1)
         moments = moments_of(0, xs, give)
-        own = own + tie(hop(give, 0), moments).astype(F32)
+        own = half[:, quarter:] + half_near[:, quarter:] + tie(hop(give, 0), moments).astype(F32)
         for k in range(1, bits):
             rounded = lax.optimization_barrier(own.astype(BF16))
             moments = moments_of(k, xs, rounded, moments)
             own = rounded.astype(F32) + tie(hop(rounded, k), moments).astype(F32)
-        return own.astype(BF16), moments
-
-    own, moments = together(right_sums, give, own, xs)
+        return own.astype(BF16), b, moments, xb1
+
+    args = (own, near, chip, *gots, left, x_near, xa0, xa1, xb0)
+    own, b, moments, xb1 = together(right_sums, *args)
+    xs = (layer_input, x_near, xa0, xa1, xb0, xb1)
     own, first, second = lax.optimization_barrier((own, first, second))
 
     def last_quarters(own, third, b, moments, xs, own0, first):
@@ -639,7 +638,7 @@
         return *error_quarters(places[2:], after, (other, other_near), b, (right,)), grad, third
 
     after, right, grad, third = together(last_quarters, own, third, b, moments, xs, own0, first)
-    grad = finish_grad(1, own1, (second, third), (grad,))
+    grad = finish_grad(1, vmem(own1), (vmem(second), third), (grad,))
     return (after[None], right.reshape(right_factor.shape), grad)
 
 

time: 112 us -> 112 us (level)
  waiting for transfers between devices: 10.3 us -> 12.2 us
  local copies, waits for them, and re-layouts: 1.35 us -> 0.02 us
    ppermute x8, waiting for transfers between devices: 1.88 us -> 3.08 us  [cross(): return lax.ppermute(value, 'tensor', [(i, i ^ 2) for i in cores])]
  transfers between devices with their start and end apart: 27 -> 27, of which waited for: 12 -> 11; matrix products, arithmetic and copies ran while one was open for 2% -> 2% of each run, Pallas kernels for 52% -> 52%
where the time goes in v4:
time: 112 us; the launch traced here: 111 us
  Pallas kernels  59.4 us (53%)
  starting transfers between devices  36.5 us (33%)
  waiting for transfers between devices  12.2 us (11%)
  other arithmetic  2.03 us (2%)
    pallas_call x4, Pallas kernels, moment_quarter(): pl.pallas_call(moment_kernel, grid_spec=pltpu.PrefetchScalarGridSpec(num_...  16.1 us
    ppermute x7, starting transfers between devices, hop(): return lax.ppermute(value, ('dp', 'tensor'), pairs)  13.5 us
    ppermute x8, starting transfers between devices, cross(): return lax.ppermute(value, 'tensor', [(i, i ^ 2) for i in cores])  13.3 us
    ppermute x12, starting transfers between devices, swap(): return lax.ppermute(value, 'tensor', [(i, i ^ 1) for i in range(tensor)])  9.79 us
    pallas_call x2, Pallas kernels, error_quarters(): pl.pallas_call(error_kernel, grid_spec=pltpu.PrefetchScalarGridSpec(num_s...  9.61 us
    pallas_call x2, Pallas kernels, grad_half(): pl.pallas_call(grad_kernel, grid=(steps,), in_specs=[SMEM, pl.BlockSpec(g...  8.15 us
    ppermute x12, waiting for transfers between devices, swap(): return lax.ppermute(value, 'tensor', [(i, i ^ 1) for i in range(tensor)])  7.26 us
    pallas_call x1, Pallas kernels, right_halves(): pl.pallas_call(right_kernel, grid_spec=pltpu.PrefetchScalarGridSpec(num_s...  4.5 us
  transfers between devices with their start and end apart: 27, of which 11 were waited for; matrix products, arithmetic and copies ran while one was open for 2% of the time, Pallas kernels for 52%

profile of v4, /device:TPU:0, one launch (start us, length us, event | category | flops | bytes accessed | tf_op | source)
XLA Modules:
  0.0 111.1 jit_solution(8153209778777290820)
XLA Ops:
  0.6 4.8 %collective-permute-start.23 = (bf16[256,4096]{1,0:T(8,128)(2,1)}, bf16[256,4096]{1,0:T(8,128)(2,1)}, u32[]{:S(2)}, u32[]{:S(2)}) collective-permute-start(bf16[256,4096]{1,0:T(8,128)(2,1)} %param.17), channel_id=1, source_target_pairs={{0,2},{2,0},{4,6},{6,4},{8,10},{10,8},{12,14},{14,12},{16,18},{18,... | collective-permute-start | bytes 6291464 | tf_op jit(solution)/shard_map/ppermute | solution.py:524
  5.5 5.7 %conditional.6 = (bf16[256,4096]{1,0:T(8,128)(2,1)}, f32[64,256]{1,0:T(8,128)}, f32[64,256]{1,0:T(8,128)}, f32[128,256]{1,0:T(8,128)S(1)}) conditional(s32[]{:T(128)} %convert_element_type.44, () %tuple.101, (bf16[256,4096]{1,0:T(8,128)(2,1)}, f32[2,32,4096]{2,1,0:T(8,128)}) %tuple.102), branch_computations={%region_0.1_spmd, %region_1.2_spmd} | conditional | flops 131072 | bytes 8913776 | solution.py:545
  5.6 3.0 %project.1 = f32[64,256]{1,0:T(8,128)} custom-call(bf16[256,4096]{1,0:T(8,128)(2,1)} %get-tuple-element.124.x_ref, f32[2,32,4096]{2,1,0:T(8,128)} %get-tuple-element.125.r_ref), custom_call_target="tpu_custom_call" | custom-call | flops 98304 | bytes 768 | tf_op jit(solution)/shard_map/cond/branch_1_fun/project/pallas_call | solution.py:84
  11.3 5.2 %conditional.7 = (f32[128,256]{1,0:T(8,128)}, f32[64,256]{1,0:T(8,128)S(1)}) conditional(s32[]{:T(128)} %convert_element_type.44, () %tuple.100, (f32[128,256]{1,0:T(8,128)S(1)}, f32[2,32,4096]{2,1,0:T(8,128)}, bf16[2,4096,256]{2,1,0:T(8,128)(2,1)}) %tuple.128), branch_computations={%region_2.3_spmd, %region_3.4_spmd} | conditional | flops 98304 | bytes 525624 | solution.py:545
  12.7 3.8 %feedback.1 = f32[64,256]{1,0:T(8,128)S(1)} custom-call(f32[2,32,4096]{2,1,0:T(8,128)} %get-tuple-element.128.r_ref, bf16[2,4096,256]{2,1,0:T(8,128)(2,1)} %get-tuple-element.129.e_ref), custom_call_target="tpu_custom_call" | custom-call | flops 98304 | bytes 1280 | tf_op jit(solution)/shard_map/cond/branch_1_fun/feedback/pallas_call | solution.py:114
  18.4 22.4 %conditional.8 = (f32[64,256]{1,0:T(8,128)S(1)}, bf16[512,2048]{1,0:T(8,128)(2,1)S(1)}, bf16[512,2048]{1,0:T(8,128)(2,1)}, bf16[256,2048]{1,0:T(8,128)(2,1)}, bf16[256,2048]{1,0:T(8,128)(2,1)}) conditional(s32[]{:T(128)} %convert_element_type.44, () %tuple.99, (f32[128,256]{1,0:T(8,128)}, s32[1]{0:T(128)}, f32[64,256]{1,0:T(8,128)}, ...), branch_computations={%region_4.5_spmd, %region_5.6_spmd} | conditional | flops 2171136 | bytes 18681880 | solution.py:545
  18.5 2.9 %collective-permute-start.1 = (f32[128,256]{1,0:T(8,128)}, f32[128,256]{1,0:T(8,128)S(1)}, u32[]{:S(2)}, u32[]{:S(2)}) collective-permute-start(f32[128,256]{1,0:T(8,128)} %get-tuple-element.134.far1), channel_id=1, source_target_pairs={{0,1},{1,0},{2,3},{3,2},{4,5},{5,4},{6,7},{7,6},{8,9},{9,8},{10,11... | collective-permute-start | bytes 393224 | tf_op jit(solution)/shard_map/cond/branch_1_fun/ppermute | solution.py:520
  25.5 4.1 %grad.2 = (bf16[512,2048]{1,0:T(8,128)(2,1)S(1)}, bf16[512,2048]{1,0:T(8,128)(2,1)S(1)}) custom-call(s32[1]{0:T(128)} %get-tuple-element.131.t_ref, bf16[2,1024,256]{2,1,0:T(8,128)(2,1)S(1)} %get-tuple-element.135.g_ref, bf16[2,4096,256]{2,1,0:T(8,128)(2,1)} %get-tuple-element.141.w_ref), custom_call_target="tpu_custom_call" | custom-call | flops 1048576 | bytes 1024 | tf_op jit(solution)/shard_map/cond/branch_1_fun/grad/pallas_call | solution.py:392
  29.7 2.7 %collective-permute-start.3 = (f32[64,256]{1,0:T(8,128)S(1)}, f32[64,256]{1,0:T(8,128)S(1)}, u32[]{:S(2)}, u32[]{:S(2)}) collective-permute-start(f32[64,256]{1,0:T(8,128)S(1)} %add.28), channel_id=1, source_target_pairs={{0,16},{1,9},{2,18},{3,11},{4,20},{5,13},{6,22},{7,15},{8,24},{9,1... | collective-permute-start | bytes 196616 | tf_op jit(solution)/shard_map/cond/branch_1_fun/ppermute | solution.py:532
  32.3 4.1 %grad.3 = (bf16[512,2048]{1,0:T(8,128)(2,1)S(1)}, bf16[512,2048]{1,0:T(8,128)(2,1)S(1)}) custom-call(s32[1]{0:T(128)} %get-tuple-element.131.t_ref, bf16[2,1024,256]{2,1,0:T(8,128)(2,1)S(1)} %get-tuple-element.135.g_ref, bf16[2,4096,256]{2,1,0:T(8,128)(2,1)} %get-tuple-element.141.w_ref), custom_call_target="tpu_custom_call" | custom-call | flops 1048576 | bytes 1024 | tf_op jit(solution)/shard_map/cond/branch_1_fun/grad/pallas_call | solution.py:392
  40.9 13.2 %conditional.9 = (f32[64,256]{1,0:T(8,128)S(1)}, f32[64,256]{1,0:T(8,128)S(1)}, f32[160,256]{1,0:T(8,128)}, f32[160,256]{1,0:T(8,128)}, f32[160,256]{1,0:T(8,128...) conditional(s32[]{:T(128)} %convert_element_type.44, () %tuple.98, ...), branch_computations={%region_6.7_spmd, %region_7.8_spmd} | conditional | flops 123136 | bytes 11700200 | solution.py:545
  48.2 4.5 %collective-permute-start.12 = (f32[160,256]{1,0:T(8,128)}, f32[160,256]{1,0:T(8,128)}, u32[]{:S(2)}, u32[]{:S(2)}) collective-permute-start(f32[160,256]{1,0:T(8,128)} %collective-permute-done.10), channel_id=1, source_target_pairs={{0,1},{1,0},{2,3},{3,2},{4,5},{5,4},{6,7},{7,6},{8,9},{9,8},{10,11... | collective-permute-start | bytes 491528 | tf_op jit(solution)/shard_map/cond/branch_1_fun/ppermute | solution.py:520
  56.1 29.7 %conditional.10 = (bf16[64,1024]{1,0:T(8,128)(2,1)S(1)}, f32[64,256]{1,0:T(8,128)S(1)}, f32[2,4096,256]{2,1,0:T(8,128)}, bf16[256,4096]{1,0:T(8,128)(2,1)}) conditional(s32[]{:T(128)} %convert_element_type.44, () %tuple.97, (s32[]{:T(128)}, s32[]{:T(128)}, s32[]{:T(128)}, s32[1]{0:T(128)}, f32[64,256]{1,0:T(8,128)S(1)}, ...), branch_computations={%region_8.9_spmd, %region_9.10_spmd} | conditional | flops 1968534 | bytes 23210224 | solution.py:545
  56.1 4.0 %solve.1 = (f32[64,256]{1,0:T(8,128)S(1)}, f32[64,256]{1,0:T(8,128)S(1)}) custom-call(s32[1]{0:T(128)} %get-tuple-element.171.t_ref, f32[64,256]{1,0:T(8,128)S(1)} %get-tuple-element.172.own_ref, f32[64,256]{1,0:T(8,128)S(1)} %get-tuple-element.173.near_ref, f32[160,256]{1,0:T(8,128)} %get-tuple-element.174.chip_ref, f32[160,256]{1,0:T(8,128)} %get-tuple-element.175.got0, ...), custom_call_target="tpu_custom_call" | custom-call | flops 2441 | bytes 2441 | tf_op jit(solution)/shard_map/cond/branch_1_fun/solve/pallas_call | solution.py:231
  60.3 4.5 %right.1 = (f32[64,2048]{1,0:T(8,128)S(1)}, f32[64,2048]{1,0:T(8,128)S(1)}) custom-call(s32[4]{0:T(128)S(1)} %pad_add_fusion.h_ref, f32[64,256]{1,0:T(8,128)S(1)} %get-tuple-element.178.z_ref, f32[64,256]{1,0:T(8,128)S(1)} %get-tuple-element.350.b_ref, bf16[256,4096]{1,0:T(8,128)(2,1)} %get-tuple-element.180.x_ref.x0, ...), custom_call_target="tpu_custom_call" | custom-call | flops 262144 | bytes 1536 | tf_op jit(solution)/shard_map/cond/branch_1_fun/right/pallas_call | solution.py:271
  68.5 4.0 %moment.4.refs_0_ = f32[2,4096,256]{2,1,0:T(8,128)} custom-call(s32[1]{0:T(128)} %get-tuple-element.171.t_ref, bf16[256,4096]{1,0:T(8,128)(2,1)S(1)} %copy-done, bf16[256,4096]{1,0:T(8,128)(2,1)} %get-tuple-element.186.x1, bf16[256,4096]{1,0:T(8,128)(2,1)} %get-tuple-element.187.a0, bf16[256,4096]{1,0:T(8,128)(2,1)} %get-tuple-element.188.a1, ...), custom_call_target="tpu_custom_call" | custom-call | flops 262144 | bytes 2048 | tf_op jit(solution)/shard_map/cond/branch_1_fun/moment/pallas_call | solution.py:313
  72.6 2.5 %collective-permute-start.16 = (bf16[64,1024]{1,0:T(8,128)(2,1)S(1)}, bf16[64,1024]{1,0:T(8,128)(2,1)S(1)}, u32[]{:S(2)}, u32[]{:S(2)}) collective-permute-start(bf16[64,1024]{1,0:T(8,128)(2,1)S(1)} %fusion.2), channel_id=1, source_target_pairs={{0,16},{1,9},{2,18},{3,11},{4,20},{5,13},{6,22},{7,15},{8,24},{9,1... | collective-permute-start | bytes 393224 | tf_op jit(solution)/shard_map/cond/branch_1_fun/ppermute | solution.py:532
  75.1 4.0 %moment.5.refs_0_ = f32[2,4096,256]{2,1,0:T(8,128)} custom-call(s32[1]{0:T(128)} %get-tuple-element.171.t_ref, bf16[256,4096]{1,0:T(8,128)(2,1)S(1)} %copy-done, bf16[256,4096]{1,0:T(8,128)(2,1)} %get-tuple-element.186.x1, bf16[256,4096]{1,0:T(8,128)(2,1)} %get-tuple-element.187.a0, ...), custom_call_target="tpu_custom_call", output_to_operand_aliasing={{}: (9, {})} | custom-call | flops 262144 | bytes 2048 | tf_op jit(solution)/shard_map/cond/branch_1_fun/moment/pallas_call | solution.py:313
  81.7 4.0 %moment.6 = f32[2,4096,256]{2,1,0:T(8,128)} custom-call(s32[1]{0:T(128)} %get-tuple-element.171.t_ref, bf16[256,4096]{1,0:T(8,128)(2,1)S(1)} %copy-done, bf16[256,4096]{1,0:T(8,128)(2,1)} %get-tuple-element.186.x1, bf16[256,4096]{1,0:T(8,128)(2,1)} %get-tuple-element.187.a0, ...), custom_call_target="tpu_custom_call", output_to_operand_aliasing={{}: (9, {})} | custom-call | flops 262144 | bytes 2048 | tf_op jit(solution)/shard_map/cond/branch_1_fun/moment/pallas_call | solution.py:313
  88.1 20.9 %conditional.11 = (bf16[256,4096]{1,0:T(8,128)(2,1)}, bf16[256,1280]{1,0:T(8,128)(2,1)}, f32[1,2,4096,256]{3,2,1,0:T(8,128)}, f32[2,32,4096]{2,1,0:T(8,128)}) conditional(s32[]{:T(128)} %convert_element_type.44, () %tuple.96, (bf16[64,1024]{1,0:T(8,128)(2,1)S(1)}, bf16[2,1024,256]{2,1,0:T(8,128)(2,1)S(1)}, s32[1]{0:T(128)}, ...), branch_computations={%region_10.11_spmd, %region_11.12_spmd} | conditional | flops 590707 | bytes 12189740 | solution.py:545
  88.7 4.1 %moment.7.m_ref = f32[2,4096,256]{2,1,0:T(8,128)} custom-call(s32[1]{0:T(128)} %get-tuple-element.199.t_ref, bf16[256,4096]{1,0:T(8,128)(2,1)} %get-tuple-element.200.x0, bf16[256,4096]{1,0:T(8,128)(2,1)} %get-tuple-element.201.x1, bf16[256,4096]{1,0:T(8,128)(2,1)} %get-tuple-element.202.a0, ...), custom_call_target="tpu_custom_call", output_to_operand_aliasing={{}: (9, {})} | custom-call | flops 262144 | bytes 2048 | tf_op jit(solution)/shard_map/cond/branch_1_fun/moment/pallas_call | solution.py:313
  95.9 4.8 %error.2 = (f32[2,4096,256]{2,1,0:T(8,128)}, f32[64,4096]{1,0:T(8,128)}) custom-call(s32[2]{0:T(128)S(1)} %pad_add_fusion.1.q_ref, f32[2,4096,256]{2,1,0:T(8,128)} %moment.7.m_ref, bf16[64,1024]{1,0:T(8,128)(2,1)S(1)} %multiply_convert_fusion.r0, bf16[64,1024]{1,0:T(8,128)(2,1)S(1)} %collective-permute-done.20.r1, ...), custom_call_target="tpu_custom_call", output_to_operand_aliasing={{0}: (1, {})} | custom-call | flops 244 | bytes 2048 | tf_op jit(solution)/shard_map/cond/branch_1_fun/error/pallas_call | solution.py:357
  101.5 2.4 %finish_grad.2 = bf16[256,4096]{1,0:T(8,128)(2,1)} custom-call(bf16[256,2048]{1,0:T(8,128)(2,1)} %get-tuple-element.196.own_ref, bf16[256,2048]{1,0:T(8,128)(2,1)} %get-tuple-element.217.refs_0_), custom_call_target="tpu_custom_call" | custom-call | flops 384 | bytes 1024 | tf_op jit(solution)/shard_map/cond/branch_1_fun/finish_grad/pallas_call | solution.py:446
  103.9 4.8 %error.3 = (f32[2,4096,256]{2,1,0:T(8,128)}, f32[64,4096]{1,0:T(8,128)}) custom-call(s32[2]{0:T(128)S(1)} %pad_add_fusion.2.q_ref, f32[2,4096,256]{2,1,0:T(8,128)} %get-tuple-element.220.m_ref, bf16[64,1024]{1,0:T(8,128)(2,1)S(1)} %collective-permute-done.19.r0, ...), custom_call_target="tpu_custom_call", output_to_operand_aliasing={{0}: (1, {}), {1}: (5, {})} | custom-call | flops 244 | bytes 2048 | tf_op jit(solution)/shard_map/cond/branch_1_fun/error/pallas_call | solution.py:357
  (77 shorter events, 41.2 us)
Async XLA Ops:
  0.6 40.2 %collective-permute-start.23 = (bf16[256,4096]{1,0:T(8,128)(2,1)}, bf16[256,4096]{1,0:T(8,128)(2,1)}, u32[]{:S(2)}, u32[]{:S(2)}) collective-permute-start(bf16[256,4096]{1,0:T(8,128)(2,1)} %param.17), channel_id=1, source_target_pairs={{0,2},{2,0},{4,6},{6,4},{8,10},{10,8},{12,14},{14,12},{16,18},{18,... | collective-permute-start | bytes 6291464 | tf_op jit(solution)/shard_map/ppermute | solution.py:524
  5.5 5.7 %collective-permute-start.7 = (bf16[256,4096]{1,0:T(8,128)(2,1)}, bf16[256,4096]{1,0:T(8,128)(2,1)}, u32[]{:S(2)}, u32[]{:S(2)}) collective-permute-start(bf16[256,4096]{1,0:T(8,128)(2,1)} %get-tuple-element.124.x_ref), channel_id=1, source_target_pairs={{0,1},{1,0},{2,3},{3,2},{4,5},{5,4},{6,7},{7,6},{8,9},{9,8},{10,11... | collective-permute-start | bytes 6291464 | tf_op jit(solution)/shard_map/cond/branch_1_fun/ppermute | solution.py:520
  11.3 5.2 %collective-permute-start = (f32[128,256]{1,0:T(8,128)S(1)}, f32[128,256]{1,0:T(8,128)}, u32[]{:S(2)}, u32[]{:S(2)}) collective-permute-start(f32[128,256]{1,0:T(8,128)S(1)} %get-tuple-element.126), channel_id=1, source_target_pairs={{1,3},{3,1},{5,7},{7,5},{9,11},{11,9},{13,15},{15,13},{17,19},{19,... | collective-permute-start | bytes 393224 | tf_op jit(solution)/shard_map/cond/branch_1_fun/ppermute | solution.py:524
  16.5 39.6 %collective-permute-start.24 = (bf16[256,4096]{1,0:T(8,128)(2,1)}, bf16[256,4096]{1,0:T(8,128)(2,1)}, u32[]{:S(2)}, u32[]{:S(2)}) collective-permute-start(bf16[256,4096]{1,0:T(8,128)(2,1)} %get-tuple-element.279), channel_id=1, source_target_pairs={{0,2},{2,0},{4,6},{6,4},{8,10},{10,8},{12,14},{14,12},{16,18},{18,... | collective-permute-start | bytes 6291464 | tf_op jit(solution)/shard_map/ppermute | solution.py:524
  18.5 4.1 %collective-permute-start.1 = (f32[128,256]{1,0:T(8,128)}, f32[128,256]{1,0:T(8,128)S(1)}, u32[]{:S(2)}, u32[]{:S(2)}) collective-permute-start(f32[128,256]{1,0:T(8,128)} %get-tuple-element.134.far1), channel_id=1, source_target_pairs={{0,1},{1,0},{2,3},{3,2},{4,5},{5,4},{6,7},{7,6},{8,9},{9,8},{10,11... | collective-permute-start | bytes 393224 | tf_op jit(solution)/shard_map/cond/branch_1_fun/ppermute | solution.py:520
  23.8 5.7 %collective-permute-start.2 = (f32[64,256]{1,0:T(8,128)S(1)}, f32[64,256]{1,0:T(8,128)S(1)}, u32[]{:S(2)}, u32[]{:S(2)}) collective-permute-start(f32[64,256]{1,0:T(8,128)S(1)} %left.1), channel_id=1, source_target_pairs={{0,8},{1,5},{2,10},{3,7},{4,12},{5,1},{6,14},{7,3},{8,0},{9,13},{1... | collective-permute-start | bytes 196616 | tf_op jit(solution)/shard_map/cond/branch_1_fun/ppermute | solution.py:532
  29.6 6.8 %collective-permute-start.4 = (bf16[512,2048]{1,0:T(8,128)(2,1)S(1)}, bf16[512,2048]{1,0:T(8,128)(2,1)S(1)}, u32[]{:S(2)}, u32[]{:S(2)}) collective-permute-start(bf16[512,2048]{1,0:T(8,128)(2,1)S(1)} %get-tuple-element.145), channel_id=1, source_target_pairs={{0,1},{1,0},{2,3},{3,2},{4,5},{5,4},{6,7},{7,6},{8,9},{9,8},{10,11... | collective-permute-start | bytes 6291464 | tf_op jit(solution)/shard_map/cond/branch_1_fun/ppermute | solution.py:520
  29.7 6.7 %collective-permute-start.3 = (f32[64,256]{1,0:T(8,128)S(1)}, f32[64,256]{1,0:T(8,128)S(1)}, u32[]{:S(2)}, u32[]{:S(2)}) collective-permute-start(f32[64,256]{1,0:T(8,128)S(1)} %add.28), channel_id=1, source_target_pairs={{0,16},{1,9},{2,18},{3,11},{4,20},{5,13},{6,22},{7,15},{8,24},{9,1... | collective-permute-start | bytes 196616 | tf_op jit(solution)/shard_map/cond/branch_1_fun/ppermute | solution.py:532
  36.4 4.4 %collective-permute-start.6 = (bf16[512,2048]{1,0:T(8,128)(2,1)S(1)}, bf16[512,2048]{1,0:T(8,128)(2,1)}, u32[]{:S(2)}, u32[]{:S(2)}) collective-permute-start(bf16[512,2048]{1,0:T(8,128)(2,1)S(1)} %get-tuple-element.150), channel_id=1, source_target_pairs={{0,1},{1,0},{2,3},{3,2},{4,5},{5,4},{6,7},{7,6},{8,9},{9,8},{10,11... | collective-permute-start | bytes 6291464 | tf_op jit(solution)/shard_map/cond/branch_1_fun/ppermute | solution.py:520
  36.5 4.3 %collective-permute-start.5 = (f32[64,256]{1,0:T(8,128)S(1)}, f32[64,256]{1,0:T(8,128)S(1)}, u32[]{:S(2)}, u32[]{:S(2)}) collective-permute-start(f32[64,256]{1,0:T(8,128)S(1)} %add.29), channel_id=1, source_target_pairs={{0,4},{1,17},{2,6},{3,19},{4,0},{5,21},{6,2},{7,23},{8,12},{9,25},... | collective-permute-start | bytes 196616 | tf_op jit(solution)/shard_map/cond/branch_1_fun/ppermute | solution.py:532
  43.7 4.5 %collective-permute-start.11 = (bf16[256,4096]{1,0:T(8,128)(2,1)}, bf16[256,4096]{1,0:T(8,128)(2,1)}, u32[]{:S(2)}, u32[]{:S(2)}) collective-permute-start(bf16[256,4096]{1,0:T(8,128)(2,1)} %get-tuple-element.160), channel_id=1, source_target_pairs={{0,1},{1,0},{2,3},{3,2},{4,5},{5,4},{6,7},{7,6},{8,9},{9,8},{10,11... | collective-permute-start | bytes 6291464 | tf_op jit(solution)/shard_map/cond/branch_1_fun/ppermute | solution.py:520
  43.9 3.7 %collective-permute-start.10 = (f32[160,256]{1,0:T(8,128)}, f32[160,256]{1,0:T(8,128)}, u32[]{:S(2)}, u32[]{:S(2)}) collective-permute-start(f32[160,256]{1,0:T(8,128)} %slice_add_fusion), channel_id=1, source_target_pairs={{1,3},{3,1},{5,7},{7,5},{9,11},{11,9},{13,15},{15,13},{17,19},{19,... | collective-permute-start | bytes 491528 | tf_op jit(solution)/shard_map/cond/branch_1_fun/ppermute | solution.py:524
  48.2 5.9 %collective-permute-start.12 = (f32[160,256]{1,0:T(8,128)}, f32[160,256]{1,0:T(8,128)}, u32[]{:S(2)}, u32[]{:S(2)}) collective-permute-start(f32[160,256]{1,0:T(8,128)} %collective-permute-done.10), channel_id=1, source_target_pairs={{0,1},{1,0},{2,3},{3,2},{4,5},{5,4},{6,7},{7,6},{8,9},{9,8},{10,11... | collective-permute-start | bytes 491528 | tf_op jit(solution)/shard_map/cond/branch_1_fun/ppermute | solution.py:520
  54.1 34.1 %collective-permute-start.25 = (bf16[256,2048]{1,0:T(8,128)(2,1)}, bf16[256,2048]{1,0:T(8,128)(2,1)}, u32[]{:S(2)}, u32[]{:S(2)}) collective-permute-start(bf16[256,2048]{1,0:T(8,128)(2,1)} %get-tuple-element.287), channel_id=1, source_target_pairs={{0,2},{1,3},{2,0},{3,1},{4,6},{5,7},{6,4},{7,5},{8,10},{9,11},{10,... | collective-permute-start | bytes 3145736 | tf_op jit(solution)/shard_map/ppermute | solution.py:524
  54.6 33.5 %collective-permute-start.26 = (bf16[256,768]{1,0:T(8,128)(2,1)S(1)}, bf16[256,768]{1,0:T(8,128)(2,1)S(1)}, u32[]{:S(2)}, u32[]{:S(2)}) collective-permute-start(bf16[256,768]{1,0:T(8,128)(2,1)S(1)} %get-tuple-element.289), channel_id=1, source_target_pairs={{0,2},{1,3},{2,0},{3,1},{4,6},{5,7},{6,4},{7,5},{8,10},{9,11},{10,... | collective-permute-start | bytes 1179656 | tf_op jit(solution)/shard_map/ppermute | solution.py:524
  56.1 8.7 %collective-permute-start.13 = (bf16[256,4096]{1,0:T(8,128)(2,1)}, bf16[256,4096]{1,0:T(8,128)(2,1)}, u32[]{:S(2)}, u32[]{:S(2)}) collective-permute-start(bf16[256,4096]{1,0:T(8,128)(2,1)} %get-tuple-element.184.b0), channel_id=1, source_target_pairs={{0,1},{1,0},{2,3},{3,2},{4,5},{5,4},{6,7},{7,6},{8,9},{9,8},{10,11... | collective-permute-start | bytes 6291464 | tf_op jit(solution)/shard_map/cond/branch_1_fun/ppermute | solution.py:520
  64.8 2.1 %collective-permute-start.14 = (f32[64,2048]{1,0:T(8,128)S(1)}, f32[64,2048]{1,0:T(8,128)S(1)}, u32[]{:S(2)}, u32[]{:S(2)}) collective-permute-start(f32[64,2048]{1,0:T(8,128)S(1)} %get-tuple-element.185), channel_id=1, source_target_pairs={{0,1},{1,0},{2,3},{3,2},{4,5},{5,4},{6,7},{7,6},{8,9},{9,8},{10,11... | collective-permute-start | bytes 1572872 | tf_op jit(solution)/shard_map/cond/branch_1_fun/ppermute | solution.py:520
  66.9 5.6 %collective-permute-start.15 = (bf16[64,1024]{1,0:T(8,128)(2,1)S(1)}, bf16[64,1024]{1,0:T(8,128)(2,1)S(1)}, u32[]{:S(2)}, u32[]{:S(2)}) collective-permute-start(bf16[64,1024]{1,0:T(8,128)(2,1)S(1)} %fusion), channel_id=1, source_target_pairs={{0,8},{1,5},{2,10},{3,7},{4,12},{5,1},{6,14},{7,3},{8,0},{9,13},{1... | collective-permute-start | bytes 393224 | tf_op jit(solution)/shard_map/cond/branch_1_fun/ppermute | solution.py:532
  72.6 7.1 %collective-permute-start.16 = (bf16[64,1024]{1,0:T(8,128)(2,1)S(1)}, bf16[64,1024]{1,0:T(8,128)(2,1)S(1)}, u32[]{:S(2)}, u32[]{:S(2)}) collective-permute-start(bf16[64,1024]{1,0:T(8,128)(2,1)S(1)} %fusion.2), channel_id=1, source_target_pairs={{0,16},{1,9},{2,18},{3,11},{4,20},{5,13},{6,22},{7,15},{8,24},{9,1... | collective-permute-start | bytes 393224 | tf_op jit(solution)/shard_map/cond/branch_1_fun/ppermute | solution.py:532
  79.8 6.0 %collective-permute-start.17 = (bf16[64,1024]{1,0:T(8,128)(2,1)S(1)}, bf16[64,1024]{1,0:T(8,128)(2,1)S(1)}, u32[]{:S(2)}, u32[]{:S(2)}) collective-permute-start(bf16[64,1024]{1,0:T(8,128)(2,1)S(1)} %add_convert_fusion.1), channel_id=1, source_target_pairs={{0,4},{1,17},{2,6},{3,19},{4,0},{5,21},{6,2},{7,23},{8,12},{9,25},... | collective-permute-start | bytes 393224 | tf_op jit(solution)/shard_map/cond/branch_1_fun/ppermute | solution.py:532
  88.1 5.0 %collective-permute-start.18 = (bf16[64,1024]{1,0:T(8,128)(2,1)S(1)}, bf16[64,1024]{1,0:T(8,128)(2,1)S(1)}, u32[]{:S(2)}, u32[]{:S(2)}) collective-permute-start(bf16[64,1024]{1,0:T(8,128)(2,1)S(1)} %get-tuple-element.198), channel_id=1, source_target_pairs={{0,2},{1,3},{2,0},{3,1},{4,6},{5,7},{6,4},{7,5},{8,10},{9,11},{10,... | collective-permute-start | bytes 393224 | tf_op jit(solution)/shard_map/cond/branch_1_fun/ppermute | solution.py:524
  93.2 15.9 %collective-permute-start.21 = (bf16[256,1280]{1,0:T(8,128)(2,1)}, bf16[256,1280]{1,0:T(8,128)(2,1)}, u32[]{:S(2)}, u32[]{:S(2)}) collective-permute-start(bf16[256,1280]{1,0:T(8,128)(2,1)} %get-tuple-element.219), channel_id=1, source_target_pairs={{0,2},{1,3},{2,0},{3,1},{4,6},{5,7},{6,4},{7,5},{8,10},{9,11},{10,... | collective-permute-start | bytes 1966088 | tf_op jit(solution)/shard_map/cond/branch_1_fun/ppermute | solution.py:524
  94.4 6.4 %collective-permute-start.19 = (bf16[64,1024]{1,0:T(8,128)(2,1)S(1)}, bf16[64,1024]{1,0:T(8,128)(2,1)S(1)}, u32[]{:S(2)}, u32[]{:S(2)}) collective-permute-start(bf16[64,1024]{1,0:T(8,128)(2,1)S(1)} %multiply_convert_fusion.r0), channel_id=1, source_target_pairs={{0,8},{1,5},{2,10},{3,7},{4,12},{5,1},{6,14},{7,3},{8,0},{9,13},{1... | collective-permute-start | bytes 393224 | tf_op jit(solution)/shard_map/cond/branch_1_fun/ppermute | solution.py:532
  100.8 3.2 %collective-permute-start.22 = (bf16[64,1024]{1,0:T(8,128)(2,1)S(1)}, bf16[64,1024]{1,0:T(8,128)(2,1)S(1)}, u32[]{:S(2)}, u32[]{:S(2)}) collective-permute-start(bf16[64,1024]{1,0:T(8,128)(2,1)S(1)} %collective-permute-done.19.r0), channel_id=1, source_target_pairs={{0,1},{1,0},{2,3},{3,2},{4,5},{5,4},{6,7},{7,6},{8,9},{9,8},{10,11... | collective-permute-start | bytes 393224 | tf_op jit(solution)/shard_map/cond/branch_1_fun/ppermute | solution.py:520
  (7 other events, 30.9 us)

commit v5 on v4

--- a/solution.py
+++ b/solution.py
@@ -176,8 +176,8 @@
     a, b = left_ref[0:rank, :], left_ref[rank : 2 * rank, :]
     gram = mm(a, jnp.concatenate([a, zero, zero, zero], axis=0), NT, HIGHEST)
     gram = gram + mm(b, jnp.concatenate([zero, zero, b, zero], axis=0), NT, HIGHEST)
-    far_ref[2 * n :, 0:128] = gram
-    far_ref[2 * n :, 128:] = jnp.zeros((rank, rows - 128), F32)
+    far_ref[2 * n :, 0:128] = gram[: rank // 2]
+    far_ref[2 * n :, 128:] = gram[rank // 2 :]
 
 
 def spread(t, left, g):
@@ -188,7 +188,7 @@
         spread_kernel,
         in_specs=[SMEM, VMEM, VMEM],
         out_specs=[VMEM, VMEM, VMEM],
-        out_shape=[small, small, jax.ShapeDtypeStruct((2 * n + n // 2, rows), F32)],
+        out_shape=[small, small, jax.ShapeDtypeStruct((2 * n + n // 4, rows), F32)],
         compiler_params=params(),
         cost_estimate=cost(6 * left.size * g.shape[1], g.nbytes),
         name="spread",
@@ -200,7 +200,8 @@
     rank = left_ref.shape[0] // modes
     n = modes * rank
     got = by_core(t_ref, got0[...], got1[...])
-    gram = chip_ref[2 * n :, 0:128] + got[2 * n :, 0:128]
+    gram = chip_ref[2 * n :, :] + got[2 * n :, :]
+    gram = jnp.concatenate([gram[:, 0:128], gram[:, 128:]], axis=0)
     row = lax.broadcasted_iota(jnp.int32, (rank, 128), 0)
     lane = lax.broadcasted_iota(jnp.int32, (rank, 128), 1)
     ones = jnp.where((lane == row + rank) | (lane == row + 3 * rank), 1.0, 0.0)

time: 112 us -> 111 us (level)
  no operation moved by 1% of the time
where the time goes in v5:
time: 111 us
  Pallas kernels  59.4 us (54%)
  starting transfers between devices  36.7 us (33%)
  waiting for transfers between devices  11.7 us (11%)
  other arithmetic  2.02 us (2%)
    pallas_call x4, Pallas kernels, moment_quarter(): pl.pallas_call(moment_kernel, grid_spec=pltpu.PrefetchScalarGridSpec(num_...  16.1 us
    ppermute x7, starting transfers between devices, hop(): return lax.ppermute(value, ('dp', 'tensor'), pairs)  13.8 us
    ppermute x8, starting transfers between devices, cross(): return lax.ppermute(value, 'tensor', [(i, i ^ 2) for i in cores])  13.4 us
    pallas_call x2, Pallas kernels, error_quarters(): pl.pallas_call(error_kernel, grid_spec=pltpu.PrefetchScalarGridSpec(num_s...  9.61 us
    ppermute x12, starting transfers between devices, swap(): return lax.ppermute(value, 'tensor', [(i, i ^ 1) for i in range(tensor)])  9.45 us
    pallas_call x2, Pallas kernels, grad_half(): pl.pallas_call(grad_kernel, grid=(steps,), in_specs=[SMEM, pl.BlockSpec(g...  8.15 us
    ppermute x12, waiting for transfers between devices, swap(): return lax.ppermute(value, 'tensor', [(i, i ^ 1) for i in range(tensor)])  7.22 us
    pallas_call x1, Pallas kernels, right_halves(): pl.pallas_call(right_kernel, grid_spec=pltpu.PrefetchScalarGridSpec(num_s...  4.5 us
  transfers between devices with their start and end apart: 27, of which 11 were waited for; matrix products, arithmetic and copies ran while one was open for 2% of the time, Pallas kernels for 52%

profile of v5, /device:TPU:0, one launch (start us, length us, event | category | flops | bytes accessed | tf_op | source)
XLA Modules:
  0.0 110.7 jit_solution(1458746386383048181)
XLA Ops:
  0.6 4.8 %collective-permute-start.23 = (bf16[256,4096]{1,0:T(8,128)(2,1)}, bf16[256,4096]{1,0:T(8,128)(2,1)}, u32[]{:S(2)}, u32[]{:S(2)}) collective-permute-start(bf16[256,4096]{1,0:T(8,128)(2,1)} %param.17), channel_id=1, source_target_pairs={{0,2},{2,0},{4,6},{6,4},{8,10},{10,8},{12,14},{14,12},{16,18},{18,... | collective-permute-start | bytes 6291464 | tf_op jit(solution)/shard_map/ppermute | solution.py:525
  5.5 5.7 %conditional.6 = (bf16[256,4096]{1,0:T(8,128)(2,1)}, f32[64,256]{1,0:T(8,128)}, f32[64,256]{1,0:T(8,128)}, f32[128,256]{1,0:T(8,128)S(1)}) conditional(s32[]{:T(128)} %convert_element_type.44, () %tuple.101, (bf16[256,4096]{1,0:T(8,128)(2,1)}, f32[2,32,4096]{2,1,0:T(8,128)}) %tuple.102), branch_computations={%region_0.1_spmd, %region_1.2_spmd} | conditional | flops 131072 | bytes 8913776 | solution.py:546
  5.6 3.0 %project.1 = f32[64,256]{1,0:T(8,128)} custom-call(bf16[256,4096]{1,0:T(8,128)(2,1)} %get-tuple-element.124.x_ref, f32[2,32,4096]{2,1,0:T(8,128)} %get-tuple-element.125.r_ref), custom_call_target="tpu_custom_call" | custom-call | flops 98304 | bytes 768 | tf_op jit(solution)/shard_map/cond/branch_1_fun/project/pallas_call | solution.py:84
  11.3 5.2 %conditional.7 = (f32[128,256]{1,0:T(8,128)}, f32[64,256]{1,0:T(8,128)S(1)}) conditional(s32[]{:T(128)} %convert_element_type.44, () %tuple.100, (f32[128,256]{1,0:T(8,128)S(1)}, f32[2,32,4096]{2,1,0:T(8,128)}, bf16[2,4096,256]{2,1,0:T(8,128)(2,1)}) %tuple.128), branch_computations={%region_2.3_spmd, %region_3.4_spmd} | conditional | flops 98304 | bytes 525624 | solution.py:546
  12.7 3.8 %feedback.1 = f32[64,256]{1,0:T(8,128)S(1)} custom-call(f32[2,32,4096]{2,1,0:T(8,128)} %get-tuple-element.128.r_ref, bf16[2,4096,256]{2,1,0:T(8,128)(2,1)} %get-tuple-element.129.e_ref), custom_call_target="tpu_custom_call" | custom-call | flops 98304 | bytes 1280 | tf_op jit(solution)/shard_map/cond/branch_1_fun/feedback/pallas_call | solution.py:114
  18.4 22.4 %conditional.8 = (f32[64,256]{1,0:T(8,128)S(1)}, bf16[512,2048]{1,0:T(8,128)(2,1)S(1)}, bf16[512,2048]{1,0:T(8,128)(2,1)}, bf16[256,2048]{1,0:T(8,128)(2,1)}, bf16[256,2048]{1,0:T(8,128)(2,1)}) conditional(s32[]{:T(128)} %convert_element_type.44, () %tuple.99, (f32[128,256]{1,0:T(8,128)}, s32[1]{0:T(128)}, f32[64,256]{1,0:T(8,128)}, ...), branch_computations={%region_4.5_spmd, %region_5.6_spmd} | conditional | flops 2171136 | bytes 18681880 | solution.py:546
  18.5 2.9 %collective-permute-start.1 = (f32[128,256]{1,0:T(8,128)}, f32[128,256]{1,0:T(8,128)S(1)}, u32[]{:S(2)}, u32[]{:S(2)}) collective-permute-start(f32[128,256]{1,0:T(8,128)} %get-tuple-element.134.far1), channel_id=1, source_target_pairs={{0,1},{1,0},{2,3},{3,2},{4,5},{5,4},{6,7},{7,6},{8,9},{9,8},{10,11... | collective-permute-start | bytes 393224 | tf_op jit(solution)/shard_map/cond/branch_1_fun/ppermute | solution.py:521
  25.5 4.1 %grad.2 = (bf16[512,2048]{1,0:T(8,128)(2,1)S(1)}, bf16[512,2048]{1,0:T(8,128)(2,1)S(1)}) custom-call(s32[1]{0:T(128)} %get-tuple-element.131.t_ref, bf16[2,1024,256]{2,1,0:T(8,128)(2,1)S(1)} %get-tuple-element.135.g_ref, bf16[2,4096,256]{2,1,0:T(8,128)(2,1)} %get-tuple-element.141.w_ref), custom_call_target="tpu_custom_call" | custom-call | flops 1048576 | bytes 1024 | tf_op jit(solution)/shard_map/cond/branch_1_fun/grad/pallas_call | solution.py:393
  29.7 2.7 %collective-permute-start.3 = (f32[64,256]{1,0:T(8,128)S(1)}, f32[64,256]{1,0:T(8,128)S(1)}, u32[]{:S(2)}, u32[]{:S(2)}) collective-permute-start(f32[64,256]{1,0:T(8,128)S(1)} %add.28), channel_id=1, source_target_pairs={{0,16},{1,9},{2,18},{3,11},{4,20},{5,13},{6,22},{7,15},{8,24},{9,1... | collective-permute-start | bytes 196616 | tf_op jit(solution)/shard_map/cond/branch_1_fun/ppermute | solution.py:533
  32.3 4.1 %grad.3 = (bf16[512,2048]{1,0:T(8,128)(2,1)S(1)}, bf16[512,2048]{1,0:T(8,128)(2,1)S(1)}) custom-call(s32[1]{0:T(128)} %get-tuple-element.131.t_ref, bf16[2,1024,256]{2,1,0:T(8,128)(2,1)S(1)} %get-tuple-element.135.g_ref, bf16[2,4096,256]{2,1,0:T(8,128)(2,1)} %get-tuple-element.141.w_ref), custom_call_target="tpu_custom_call" | custom-call | flops 1048576 | bytes 1024 | tf_op jit(solution)/shard_map/cond/branch_1_fun/grad/pallas_call | solution.py:393
  40.9 12.8 %conditional.9 = (f32[64,256]{1,0:T(8,128)S(1)}, f32[64,256]{1,0:T(8,128)S(1)}, f32[144,256]{1,0:T(8,128)}, f32[144,256]{1,0:T(8,128)}, f32[144,256]{1,0:T(8,128...) conditional(s32[]{:T(128)} %convert_element_type.44, () %tuple.98, ...), branch_computations={%region_6.7_spmd, %region_7.8_spmd} | conditional | flops 114944 | bytes 11421672 | solution.py:546
  48.2 4.1 %collective-permute-start.12 = (f32[144,256]{1,0:T(8,128)}, f32[144,256]{1,0:T(8,128)}, u32[]{:S(2)}, u32[]{:S(2)}) collective-permute-start(f32[144,256]{1,0:T(8,128)} %collective-permute-done.10), channel_id=1, source_target_pairs={{0,1},{1,0},{2,3},{3,2},{4,5},{5,4},{6,7},{7,6},{8,9},{9,8},{10,11... | collective-permute-start | bytes 442376 | tf_op jit(solution)/shard_map/cond/branch_1_fun/ppermute | solution.py:521
  55.7 30.1 %conditional.10 = (bf16[64,1024]{1,0:T(8,128)(2,1)S(1)}, f32[64,256]{1,0:T(8,128)S(1)}, f32[2,4096,256]{2,1,0:T(8,128)}, bf16[256,4096]{1,0:T(8,128)(2,1)}) conditional(s32[]{:T(128)} %convert_element_type.44, () %tuple.97, (s32[]{:T(128)}, s32[]{:T(128)}, s32[]{:T(128)}, s32[1]{0:T(128)}, f32[64,256]{1,0:T(8,128)S(1)}, ...), branch_computations={%region_8.9_spmd, %region_9.10_spmd} | conditional | flops 1968534 | bytes 23210224 | solution.py:546
  55.7 4.0 %solve.1 = (f32[64,256]{1,0:T(8,128)S(1)}, f32[64,256]{1,0:T(8,128)S(1)}) custom-call(s32[1]{0:T(128)} %get-tuple-element.171.t_ref, f32[64,256]{1,0:T(8,128)S(1)} %get-tuple-element.172.own_ref, f32[64,256]{1,0:T(8,128)S(1)} %get-tuple-element.173.near_ref, f32[144,256]{1,0:T(8,128)} %get-tuple-element.174.chip_ref, f32[144,256]{1,0:T(8,128)} %get-tuple-element.175.got0, ...), custom_call_target="tpu_custom_call" | custom-call | flops 2441 | bytes 2441 | tf_op jit(solution)/shard_map/cond/branch_1_fun/solve/pallas_call | solution.py:232
  59.8 4.5 %right.1 = (f32[64,2048]{1,0:T(8,128)S(1)}, f32[64,2048]{1,0:T(8,128)S(1)}) custom-call(s32[4]{0:T(128)S(1)} %pad_add_fusion.h_ref, f32[64,256]{1,0:T(8,128)S(1)} %get-tuple-element.178.z_ref, f32[64,256]{1,0:T(8,128)S(1)} %get-tuple-element.350.b_ref, bf16[256,4096]{1,0:T(8,128)(2,1)} %get-tuple-element.180.x_ref.x0, ...), custom_call_target="tpu_custom_call" | custom-call | flops 262144 | bytes 1536 | tf_op jit(solution)/shard_map/cond/branch_1_fun/right/pallas_call | solution.py:272
  68.2 4.0 %moment.4.refs_0_ = f32[2,4096,256]{2,1,0:T(8,128)} custom-call(s32[1]{0:T(128)} %get-tuple-element.171.t_ref, bf16[256,4096]{1,0:T(8,128)(2,1)S(1)} %copy-done, bf16[256,4096]{1,0:T(8,128)(2,1)} %get-tuple-element.186.x1, bf16[256,4096]{1,0:T(8,128)(2,1)} %get-tuple-element.187.a0, bf16[256,4096]{1,0:T(8,128)(2,1)} %get-tuple-element.188.a1, ...), custom_call_target="tpu_custom_call" | custom-call | flops 262144 | bytes 2048 | tf_op jit(solution)/shard_map/cond/branch_1_fun/moment/pallas_call | solution.py:314
  72.3 2.7 %collective-permute-start.16 = (bf16[64,1024]{1,0:T(8,128)(2,1)S(1)}, bf16[64,1024]{1,0:T(8,128)(2,1)S(1)}, u32[]{:S(2)}, u32[]{:S(2)}) collective-permute-start(bf16[64,1024]{1,0:T(8,128)(2,1)S(1)} %fusion.2), channel_id=1, source_target_pairs={{0,16},{1,9},{2,18},{3,11},{4,20},{5,13},{6,22},{7,15},{8,24},{9,1... | collective-permute-start | bytes 393224 | tf_op jit(solution)/shard_map/cond/branch_1_fun/ppermute | solution.py:533
  74.9 4.0 %moment.5.refs_0_ = f32[2,4096,256]{2,1,0:T(8,128)} custom-call(s32[1]{0:T(128)} %get-tuple-element.171.t_ref, bf16[256,4096]{1,0:T(8,128)(2,1)S(1)} %copy-done, bf16[256,4096]{1,0:T(8,128)(2,1)} %get-tuple-element.186.x1, bf16[256,4096]{1,0:T(8,128)(2,1)} %get-tuple-element.187.a0, ...), custom_call_target="tpu_custom_call", output_to_operand_aliasing={{}: (9, {})} | custom-call | flops 262144 | bytes 2048 | tf_op jit(solution)/shard_map/cond/branch_1_fun/moment/pallas_call | solution.py:314
  81.8 4.0 %moment.6 = f32[2,4096,256]{2,1,0:T(8,128)} custom-call(s32[1]{0:T(128)} %get-tuple-element.171.t_ref, bf16[256,4096]{1,0:T(8,128)(2,1)S(1)} %copy-done, bf16[256,4096]{1,0:T(8,128)(2,1)} %get-tuple-element.186.x1, bf16[256,4096]{1,0:T(8,128)(2,1)} %get-tuple-element.187.a0, ...), custom_call_target="tpu_custom_call", output_to_operand_aliasing={{}: (9, {})} | custom-call | flops 262144 | bytes 2048 | tf_op jit(solution)/shard_map/cond/branch_1_fun/moment/pallas_call | solution.py:314
  87.7 20.9 %conditional.11 = (bf16[256,4096]{1,0:T(8,128)(2,1)}, bf16[256,1280]{1,0:T(8,128)(2,1)}, f32[1,2,4096,256]{3,2,1,0:T(8,128)}, f32[2,32,4096]{2,1,0:T(8,128)}) conditional(s32[]{:T(128)} %convert_element_type.44, () %tuple.96, (bf16[64,1024]{1,0:T(8,128)(2,1)S(1)}, bf16[2,1024,256]{2,1,0:T(8,128)(2,1)S(1)}, s32[1]{0:T(128)}, ...), branch_computations={%region_10.11_spmd, %region_11.12_spmd} | conditional | flops 590707 | bytes 12189740 | solution.py:546
  88.4 4.1 %moment.7.m_ref = f32[2,4096,256]{2,1,0:T(8,128)} custom-call(s32[1]{0:T(128)} %get-tuple-element.199.t_ref, bf16[256,4096]{1,0:T(8,128)(2,1)} %get-tuple-element.200.x0, bf16[256,4096]{1,0:T(8,128)(2,1)} %get-tuple-element.201.x1, bf16[256,4096]{1,0:T(8,128)(2,1)} %get-tuple-element.202.a0, ...), custom_call_target="tpu_custom_call", output_to_operand_aliasing={{}: (9, {})} | custom-call | flops 262144 | bytes 2048 | tf_op jit(solution)/shard_map/cond/branch_1_fun/moment/pallas_call | solution.py:314
  95.5 4.8 %error.2 = (f32[2,4096,256]{2,1,0:T(8,128)}, f32[64,4096]{1,0:T(8,128)}) custom-call(s32[2]{0:T(128)S(1)} %pad_add_fusion.1.q_ref, f32[2,4096,256]{2,1,0:T(8,128)} %moment.7.m_ref, bf16[64,1024]{1,0:T(8,128)(2,1)S(1)} %multiply_convert_fusion.r0, bf16[64,1024]{1,0:T(8,128)(2,1)S(1)} %collective-permute-done.20.r1, ...), custom_call_target="tpu_custom_call", output_to_operand_aliasing={{0}: (1, {})} | custom-call | flops 244 | bytes 2048 | tf_op jit(solution)/shard_map/cond/branch_1_fun/error/pallas_call | solution.py:358
  101.1 2.4 %finish_grad.2 = bf16[256,4096]{1,0:T(8,128)(2,1)} custom-call(bf16[256,2048]{1,0:T(8,128)(2,1)} %get-tuple-element.196.own_ref, bf16[256,2048]{1,0:T(8,128)(2,1)} %get-tuple-element.217.refs_0_), custom_call_target="tpu_custom_call" | custom-call | flops 384 | bytes 1024 | tf_op jit(solution)/shard_map/cond/branch_1_fun/finish_grad/pallas_call | solution.py:447
  103.5 4.8 %error.3 = (f32[2,4096,256]{2,1,0:T(8,128)}, f32[64,4096]{1,0:T(8,128)}) custom-call(s32[2]{0:T(128)S(1)} %pad_add_fusion.2.q_ref, f32[2,4096,256]{2,1,0:T(8,128)} %get-tuple-element.220.m_ref, bf16[64,1024]{1,0:T(8,128)(2,1)S(1)} %collective-permute-done.19.r0, ...), custom_call_target="tpu_custom_call", output_to_operand_aliasing={{0}: (1, {}), {1}: (5, {})} | custom-call | flops 244 | bytes 2048 | tf_op jit(solution)/shard_map/cond/branch_1_fun/error/pallas_call | solution.py:358
  (77 shorter events, 41.0 us)
Async XLA Ops:
  0.6 40.2 %collective-permute-start.23 = (bf16[256,4096]{1,0:T(8,128)(2,1)}, bf16[256,4096]{1,0:T(8,128)(2,1)}, u32[]{:S(2)}, u32[]{:S(2)}) collective-permute-start(bf16[256,4096]{1,0:T(8,128)(2,1)} %param.17), channel_id=1, source_target_pairs={{0,2},{2,0},{4,6},{6,4},{8,10},{10,8},{12,14},{14,12},{16,18},{18,... | collective-permute-start | bytes 6291464 | tf_op jit(solution)/shard_map/ppermute | solution.py:525
  5.5 5.7 %collective-permute-start.7 = (bf16[256,4096]{1,0:T(8,128)(2,1)}, bf16[256,4096]{1,0:T(8,128)(2,1)}, u32[]{:S(2)}, u32[]{:S(2)}) collective-permute-start(bf16[256,4096]{1,0:T(8,128)(2,1)} %get-tuple-element.124.x_ref), channel_id=1, source_target_pairs={{0,1},{1,0},{2,3},{3,2},{4,5},{5,4},{6,7},{7,6},{8,9},{9,8},{10,11... | collective-permute-start | bytes 6291464 | tf_op jit(solution)/shard_map/cond/branch_1_fun/ppermute | solution.py:521
  11.3 5.2 %collective-permute-start = (f32[128,256]{1,0:T(8,128)S(1)}, f32[128,256]{1,0:T(8,128)}, u32[]{:S(2)}, u32[]{:S(2)}) collective-permute-start(f32[128,256]{1,0:T(8,128)S(1)} %get-tuple-element.126), channel_id=1, source_target_pairs={{1,3},{3,1},{5,7},{7,5},{9,11},{11,9},{13,15},{15,13},{17,19},{19,... | collective-permute-start | bytes 393224 | tf_op jit(solution)/shard_map/cond/branch_1_fun/ppermute | solution.py:525
  16.5 39.2 %collective-permute-start.24 = (bf16[256,4096]{1,0:T(8,128)(2,1)}, bf16[256,4096]{1,0:T(8,128)(2,1)}, u32[]{:S(2)}, u32[]{:S(2)}) collective-permute-start(bf16[256,4096]{1,0:T(8,128)(2,1)} %get-tuple-element.279), channel_id=1, source_target_pairs={{0,2},{2,0},{4,6},{6,4},{8,10},{10,8},{12,14},{14,12},{16,18},{18,... | collective-permute-start | bytes 6291464 | tf_op jit(solution)/shard_map/ppermute | solution.py:525
  18.5 4.1 %collective-permute-start.1 = (f32[128,256]{1,0:T(8,128)}, f32[128,256]{1,0:T(8,128)S(1)}, u32[]{:S(2)}, u32[]{:S(2)}) collective-permute-start(f32[128,256]{1,0:T(8,128)} %get-tuple-element.134.far1), channel_id=1, source_target_pairs={{0,1},{1,0},{2,3},{3,2},{4,5},{5,4},{6,7},{7,6},{8,9},{9,8},{10,11... | collective-permute-start | bytes 393224 | tf_op jit(solution)/shard_map/cond/branch_1_fun/ppermute | solution.py:521
  23.8 5.7 %collective-permute-start.2 = (f32[64,256]{1,0:T(8,128)S(1)}, f32[64,256]{1,0:T(8,128)S(1)}, u32[]{:S(2)}, u32[]{:S(2)}) collective-permute-start(f32[64,256]{1,0:T(8,128)S(1)} %left.1), channel_id=1, source_target_pairs={{0,8},{1,5},{2,10},{3,7},{4,12},{5,1},{6,14},{7,3},{8,0},{9,13},{1... | collective-permute-start | bytes 196616 | tf_op jit(solution)/shard_map/cond/branch_1_fun/ppermute | solution.py:533
  29.6 6.8 %collective-permute-start.4 = (bf16[512,2048]{1,0:T(8,128)(2,1)S(1)}, bf16[512,2048]{1,0:T(8,128)(2,1)S(1)}, u32[]{:S(2)}, u32[]{:S(2)}) collective-permute-start(bf16[512,2048]{1,0:T(8,128)(2,1)S(1)} %get-tuple-element.145), channel_id=1, source_target_pairs={{0,1},{1,0},{2,3},{3,2},{4,5},{5,4},{6,7},{7,6},{8,9},{9,8},{10,11... | collective-permute-start | bytes 6291464 | tf_op jit(solution)/shard_map/cond/branch_1_fun/ppermute | solution.py:521
  29.7 6.7 %collective-permute-start.3 = (f32[64,256]{1,0:T(8,128)S(1)}, f32[64,256]{1,0:T(8,128)S(1)}, u32[]{:S(2)}, u32[]{:S(2)}) collective-permute-start(f32[64,256]{1,0:T(8,128)S(1)} %add.28), channel_id=1, source_target_pairs={{0,16},{1,9},{2,18},{3,11},{4,20},{5,13},{6,22},{7,15},{8,24},{9,1... | collective-permute-start | bytes 196616 | tf_op jit(solution)/shard_map/cond/branch_1_fun/ppermute | solution.py:533
  36.4 4.4 %collective-permute-start.6 = (bf16[512,2048]{1,0:T(8,128)(2,1)S(1)}, bf16[512,2048]{1,0:T(8,128)(2,1)}, u32[]{:S(2)}, u32[]{:S(2)}) collective-permute-start(bf16[512,2048]{1,0:T(8,128)(2,1)S(1)} %get-tuple-element.150), channel_id=1, source_target_pairs={{0,1},{1,0},{2,3},{3,2},{4,5},{5,4},{6,7},{7,6},{8,9},{9,8},{10,11... | collective-permute-start | bytes 6291464 | tf_op jit(solution)/shard_map/cond/branch_1_fun/ppermute | solution.py:521
  36.5 4.3 %collective-permute-start.5 = (f32[64,256]{1,0:T(8,128)S(1)}, f32[64,256]{1,0:T(8,128)S(1)}, u32[]{:S(2)}, u32[]{:S(2)}) collective-permute-start(f32[64,256]{1,0:T(8,128)S(1)} %add.29), channel_id=1, source_target_pairs={{0,4},{1,17},{2,6},{3,19},{4,0},{5,21},{6,2},{7,23},{8,12},{9,25},... | collective-permute-start | bytes 196616 | tf_op jit(solution)/shard_map/cond/branch_1_fun/ppermute | solution.py:533
  43.7 4.5 %collective-permute-start.11 = (bf16[256,4096]{1,0:T(8,128)(2,1)}, bf16[256,4096]{1,0:T(8,128)(2,1)}, u32[]{:S(2)}, u32[]{:S(2)}) collective-permute-start(bf16[256,4096]{1,0:T(8,128)(2,1)} %get-tuple-element.160), channel_id=1, source_target_pairs={{0,1},{1,0},{2,3},{3,2},{4,5},{5,4},{6,7},{7,6},{8,9},{9,8},{10,11... | collective-permute-start | bytes 6291464 | tf_op jit(solution)/shard_map/cond/branch_1_fun/ppermute | solution.py:521
  43.9 3.7 %collective-permute-start.10 = (f32[144,256]{1,0:T(8,128)}, f32[144,256]{1,0:T(8,128)}, u32[]{:S(2)}, u32[]{:S(2)}) collective-permute-start(f32[144,256]{1,0:T(8,128)} %slice_add_fusion), channel_id=1, source_target_pairs={{1,3},{3,1},{5,7},{7,5},{9,11},{11,9},{13,15},{15,13},{17,19},{19,... | collective-permute-start | bytes 442376 | tf_op jit(solution)/shard_map/cond/branch_1_fun/ppermute | solution.py:525
  48.2 5.5 %collective-permute-start.12 = (f32[144,256]{1,0:T(8,128)}, f32[144,256]{1,0:T(8,128)}, u32[]{:S(2)}, u32[]{:S(2)}) collective-permute-start(f32[144,256]{1,0:T(8,128)} %collective-permute-done.10), channel_id=1, source_target_pairs={{0,1},{1,0},{2,3},{3,2},{4,5},{5,4},{6,7},{7,6},{8,9},{9,8},{10,11... | collective-permute-start | bytes 442376 | tf_op jit(solution)/shard_map/cond/branch_1_fun/ppermute | solution.py:521
  53.7 34.1 %collective-permute-start.25 = (bf16[256,2048]{1,0:T(8,128)(2,1)}, bf16[256,2048]{1,0:T(8,128)(2,1)}, u32[]{:S(2)}, u32[]{:S(2)}) collective-permute-start(bf16[256,2048]{1,0:T(8,128)(2,1)} %get-tuple-element.287), channel_id=1, source_target_pairs={{0,2},{1,3},{2,0},{3,1},{4,6},{5,7},{6,4},{7,5},{8,10},{9,11},{10,... | collective-permute-start | bytes 3145736 | tf_op jit(solution)/shard_map/ppermute | solution.py:525
  54.2 33.5 %collective-permute-start.26 = (bf16[256,768]{1,0:T(8,128)(2,1)S(1)}, bf16[256,768]{1,0:T(8,128)(2,1)S(1)}, u32[]{:S(2)}, u32[]{:S(2)}) collective-permute-start(bf16[256,768]{1,0:T(8,128)(2,1)S(1)} %get-tuple-element.289), channel_id=1, source_target_pairs={{0,2},{1,3},{2,0},{3,1},{4,6},{5,7},{6,4},{7,5},{8,10},{9,11},{10,... | collective-permute-start | bytes 1179656 | tf_op jit(solution)/shard_map/ppermute | solution.py:525
  55.7 8.6 %collective-permute-start.13 = (bf16[256,4096]{1,0:T(8,128)(2,1)}, bf16[256,4096]{1,0:T(8,128)(2,1)}, u32[]{:S(2)}, u32[]{:S(2)}) collective-permute-start(bf16[256,4096]{1,0:T(8,128)(2,1)} %get-tuple-element.184.b0), channel_id=1, source_target_pairs={{0,1},{1,0},{2,3},{3,2},{4,5},{5,4},{6,7},{7,6},{8,9},{9,8},{10,11... | collective-permute-start | bytes 6291464 | tf_op jit(solution)/shard_map/cond/branch_1_fun/ppermute | solution.py:521
  64.4 2.1 %collective-permute-start.14 = (f32[64,2048]{1,0:T(8,128)S(1)}, f32[64,2048]{1,0:T(8,128)S(1)}, u32[]{:S(2)}, u32[]{:S(2)}) collective-permute-start(f32[64,2048]{1,0:T(8,128)S(1)} %get-tuple-element.185), channel_id=1, source_target_pairs={{0,1},{1,0},{2,3},{3,2},{4,5},{5,4},{6,7},{7,6},{8,9},{9,8},{10,11... | collective-permute-start | bytes 1572872 | tf_op jit(solution)/shard_map/cond/branch_1_fun/ppermute | solution.py:521
  66.5 5.7 %collective-permute-start.15 = (bf16[64,1024]{1,0:T(8,128)(2,1)S(1)}, bf16[64,1024]{1,0:T(8,128)(2,1)S(1)}, u32[]{:S(2)}, u32[]{:S(2)}) collective-permute-start(bf16[64,1024]{1,0:T(8,128)(2,1)S(1)} %fusion), channel_id=1, source_target_pairs={{0,8},{1,5},{2,10},{3,7},{4,12},{5,1},{6,14},{7,3},{8,0},{9,13},{1... | collective-permute-start | bytes 393224 | tf_op jit(solution)/shard_map/cond/branch_1_fun/ppermute | solution.py:533
  72.3 7.3 %collective-permute-start.16 = (bf16[64,1024]{1,0:T(8,128)(2,1)S(1)}, bf16[64,1024]{1,0:T(8,128)(2,1)S(1)}, u32[]{:S(2)}, u32[]{:S(2)}) collective-permute-start(bf16[64,1024]{1,0:T(8,128)(2,1)S(1)} %fusion.2), channel_id=1, source_target_pairs={{0,16},{1,9},{2,18},{3,11},{4,20},{5,13},{6,22},{7,15},{8,24},{9,1... | collective-permute-start | bytes 393224 | tf_op jit(solution)/shard_map/cond/branch_1_fun/ppermute | solution.py:533
  79.7 6.1 %collective-permute-start.17 = (bf16[64,1024]{1,0:T(8,128)(2,1)S(1)}, bf16[64,1024]{1,0:T(8,128)(2,1)S(1)}, u32[]{:S(2)}, u32[]{:S(2)}) collective-permute-start(bf16[64,1024]{1,0:T(8,128)(2,1)S(1)} %add_convert_fusion.1), channel_id=1, source_target_pairs={{0,4},{1,17},{2,6},{3,19},{4,0},{5,21},{6,2},{7,23},{8,12},{9,25},... | collective-permute-start | bytes 393224 | tf_op jit(solution)/shard_map/cond/branch_1_fun/ppermute | solution.py:533
  87.7 5.0 %collective-permute-start.18 = (bf16[64,1024]{1,0:T(8,128)(2,1)S(1)}, bf16[64,1024]{1,0:T(8,128)(2,1)S(1)}, u32[]{:S(2)}, u32[]{:S(2)}) collective-permute-start(bf16[64,1024]{1,0:T(8,128)(2,1)S(1)} %get-tuple-element.198), channel_id=1, source_target_pairs={{0,2},{1,3},{2,0},{3,1},{4,6},{5,7},{6,4},{7,5},{8,10},{9,11},{10,... | collective-permute-start | bytes 393224 | tf_op jit(solution)/shard_map/cond/branch_1_fun/ppermute | solution.py:525
  92.8 15.9 %collective-permute-start.21 = (bf16[256,1280]{1,0:T(8,128)(2,1)}, bf16[256,1280]{1,0:T(8,128)(2,1)}, u32[]{:S(2)}, u32[]{:S(2)}) collective-permute-start(bf16[256,1280]{1,0:T(8,128)(2,1)} %get-tuple-element.219), channel_id=1, source_target_pairs={{0,2},{1,3},{2,0},{3,1},{4,6},{5,7},{6,4},{7,5},{8,10},{9,11},{10,... | collective-permute-start | bytes 1966088 | tf_op jit(solution)/shard_map/cond/branch_1_fun/ppermute | solution.py:525
  94.0 6.4 %collective-permute-start.19 = (bf16[64,1024]{1,0:T(8,128)(2,1)S(1)}, bf16[64,1024]{1,0:T(8,128)(2,1)S(1)}, u32[]{:S(2)}, u32[]{:S(2)}) collective-permute-start(bf16[64,1024]{1,0:T(8,128)(2,1)S(1)} %multiply_convert_fusion.r0), channel_id=1, source_target_pairs={{0,8},{1,5},{2,10},{3,7},{4,12},{5,1},{6,14},{7,3},{8,0},{9,13},{1... | collective-permute-start | bytes 393224 | tf_op jit(solution)/shard_map/cond/branch_1_fun/ppermute | solution.py:533
  100.3 3.2 %collective-permute-start.22 = (bf16[64,1024]{1,0:T(8,128)(2,1)S(1)}, bf16[64,1024]{1,0:T(8,128)(2,1)S(1)}, u32[]{:S(2)}, u32[]{:S(2)}) collective-permute-start(bf16[64,1024]{1,0:T(8,128)(2,1)S(1)} %collective-permute-done.19.r0), channel_id=1, source_target_pairs={{0,1},{1,0},{2,3},{3,2},{4,5},{5,4},{6,7},{7,6},{8,9},{9,8},{10,11... | collective-permute-start | bytes 393224 | tf_op jit(solution)/shard_map/cond/branch_1_fun/ppermute | solution.py:521
  (7 other events, 31.2 us)

commit v6 on v5

--- a/solution.py
+++ b/solution.py
@@ -108,7 +108,7 @@
         out_ref[...] += term
 
 
-def feedback(r, e, chunk=2048):
+def feedback(r, e, chunk=4096):
     modes, rank, depth = r.shape
     cols = e.shape[-1]
     return pl.pallas_call(

time: 111 us -> 111 us (level)
  transfers between devices with their start and end apart: 27 -> 27, of which waited for: 11 -> 11; matrix products, arithmetic and copies ran while one was open for 2% -> 2% of each run, Pallas kernels for 52% -> 51%
where the time goes in v6:
time: 111 us
  Pallas kernels  58.6 us (53%)
  starting transfers between devices  37.4 us (34%)
  waiting for transfers between devices  11.7 us (11%)
  other arithmetic  2.02 us (2%)
    pallas_call x4, Pallas kernels, moment_quarter(): pl.pallas_call(moment_kernel, grid_spec=pltpu.PrefetchScalarGridSpec(num_...  16.1 us
    ppermute x7, starting transfers between devices, hop(): return lax.ppermute(value, ('dp', 'tensor'), pairs)  13.8 us
    ppermute x8, starting transfers between devices, cross(): return lax.ppermute(value, 'tensor', [(i, i ^ 2) for i in cores])  13.4 us
    ppermute x12, starting transfers between devices, swap(): return lax.ppermute(value, 'tensor', [(i, i ^ 1) for i in range(tensor)])  10.2 us
    pallas_call x2, Pallas kernels, error_quarters(): pl.pallas_call(error_kernel, grid_spec=pltpu.PrefetchScalarGridSpec(num_s...  9.61 us
    pallas_call x2, Pallas kernels, grad_half(): pl.pallas_call(grad_kernel, grid=(steps,), in_specs=[SMEM, pl.BlockSpec(g...  8.15 us
    ppermute x12, waiting for transfers between devices, swap(): return lax.ppermute(value, 'tensor', [(i, i ^ 1) for i in range(tensor)])  7.22 us
    pallas_call x1, Pallas kernels, right_halves(): pl.pallas_call(right_kernel, grid_spec=pltpu.PrefetchScalarGridSpec(num_s...  4.5 us
  transfers between devices with their start and end apart: 27, of which 11 were waited for; matrix products, arithmetic and copies ran while one was open for 2% of the time, Pallas kernels for 51%

profile of v6, /device:TPU:0, one launch (start us, length us, event | category | flops | bytes accessed | tf_op | source)
XLA Modules:
  0.0 110.7 jit_solution(16889099576033101556)
XLA Ops:
  0.6 4.8 %collective-permute-start.23 = (bf16[256,4096]{1,0:T(8,128)(2,1)}, bf16[256,4096]{1,0:T(8,128)(2,1)}, u32[]{:S(2)}, u32[]{:S(2)}) collective-permute-start(bf16[256,4096]{1,0:T(8,128)(2,1)} %param.17), channel_id=1, source_target_pairs={{0,2},{2,0},{4,6},{6,4},{8,10},{10,8},{12,14},{14,12},{16,18},{18,... | collective-permute-start | bytes 6291464 | tf_op jit(solution)/shard_map/ppermute | solution.py:525
  5.5 5.7 %conditional.6 = (bf16[256,4096]{1,0:T(8,128)(2,1)}, f32[64,256]{1,0:T(8,128)}, f32[64,256]{1,0:T(8,128)}, f32[128,256]{1,0:T(8,128)S(1)}) conditional(s32[]{:T(128)} %convert_element_type.44, () %tuple.101, (bf16[256,4096]{1,0:T(8,128)(2,1)}, f32[2,32,4096]{2,1,0:T(8,128)}) %tuple.102), branch_computations={%region_0.1_spmd, %region_1.2_spmd} | conditional | flops 131072 | bytes 8913776 | solution.py:546
  5.6 3.0 %project.1 = f32[64,256]{1,0:T(8,128)} custom-call(bf16[256,4096]{1,0:T(8,128)(2,1)} %get-tuple-element.124.x_ref, f32[2,32,4096]{2,1,0:T(8,128)} %get-tuple-element.125.r_ref), custom_call_target="tpu_custom_call" | custom-call | flops 98304 | bytes 768 | tf_op jit(solution)/shard_map/cond/branch_1_fun/project/pallas_call | solution.py:84
  11.3 4.5 %conditional.7 = (f32[128,256]{1,0:T(8,128)}, f32[64,256]{1,0:T(8,128)S(1)}) conditional(s32[]{:T(128)} %convert_element_type.44, () %tuple.100, (f32[128,256]{1,0:T(8,128)S(1)}, f32[2,32,4096]{2,1,0:T(8,128)}, bf16[2,4096,256]{2,1,0:T(8,128)(2,1)}) %tuple.128), branch_computations={%region_2.3_spmd, %region_3.4_spmd} | conditional | flops 98304 | bytes 525624 | solution.py:546
  12.7 3.0 %feedback.1 = f32[64,256]{1,0:T(8,128)S(1)} custom-call(f32[2,32,4096]{2,1,0:T(8,128)} %get-tuple-element.128.r_ref, bf16[2,4096,256]{2,1,0:T(8,128)(2,1)} %get-tuple-element.129.e_ref), custom_call_target="tpu_custom_call" | custom-call | flops 98304 | bytes 1280 | tf_op jit(solution)/shard_map/cond/branch_1_fun/feedback/pallas_call | solution.py:114
  17.7 23.2 %conditional.8 = (f32[64,256]{1,0:T(8,128)S(1)}, bf16[512,2048]{1,0:T(8,128)(2,1)S(1)}, bf16[512,2048]{1,0:T(8,128)(2,1)}, bf16[256,2048]{1,0:T(8,128)(2,1)}, bf16[256,2048]{1,0:T(8,128)(2,1)}) conditional(s32[]{:T(128)} %convert_element_type.44, () %tuple.99, (f32[128,256]{1,0:T(8,128)}, s32[1]{0:T(128)}, f32[64,256]{1,0:T(8,128)}, ...), branch_computations={%region_4.5_spmd, %region_5.6_spmd} | conditional | flops 2171136 | bytes 18681880 | solution.py:546
  17.7 3.6 %collective-permute-start.1 = (f32[128,256]{1,0:T(8,128)}, f32[128,256]{1,0:T(8,128)S(1)}, u32[]{:S(2)}, u32[]{:S(2)}) collective-permute-start(f32[128,256]{1,0:T(8,128)} %get-tuple-element.134.far1), channel_id=1, source_target_pairs={{0,1},{1,0},{2,3},{3,2},{4,5},{5,4},{6,7},{7,6},{8,9},{9,8},{10,11... | collective-permute-start | bytes 393224 | tf_op jit(solution)/shard_map/cond/branch_1_fun/ppermute | solution.py:521
  25.5 4.1 %grad.2 = (bf16[512,2048]{1,0:T(8,128)(2,1)S(1)}, bf16[512,2048]{1,0:T(8,128)(2,1)S(1)}) custom-call(s32[1]{0:T(128)} %get-tuple-element.131.t_ref, bf16[2,1024,256]{2,1,0:T(8,128)(2,1)S(1)} %get-tuple-element.135.g_ref, bf16[2,4096,256]{2,1,0:T(8,128)(2,1)} %get-tuple-element.141.w_ref), custom_call_target="tpu_custom_call" | custom-call | flops 1048576 | bytes 1024 | tf_op jit(solution)/shard_map/cond/branch_1_fun/grad/pallas_call | solution.py:393
  29.7 2.7 %collective-permute-start.3 = (f32[64,256]{1,0:T(8,128)S(1)}, f32[64,256]{1,0:T(8,128)S(1)}, u32[]{:S(2)}, u32[]{:S(2)}) collective-permute-start(f32[64,256]{1,0:T(8,128)S(1)} %add.28), channel_id=1, source_target_pairs={{0,16},{1,9},{2,18},{3,11},{4,20},{5,13},{6,22},{7,15},{8,24},{9,1... | collective-permute-start | bytes 196616 | tf_op jit(solution)/shard_map/cond/branch_1_fun/ppermute | solution.py:533
  32.3 4.1 %grad.3 = (bf16[512,2048]{1,0:T(8,128)(2,1)S(1)}, bf16[512,2048]{1,0:T(8,128)(2,1)S(1)}) custom-call(s32[1]{0:T(128)} %get-tuple-element.131.t_ref, bf16[2,1024,256]{2,1,0:T(8,128)(2,1)S(1)} %get-tuple-element.135.g_ref, bf16[2,4096,256]{2,1,0:T(8,128)(2,1)} %get-tuple-element.141.w_ref), custom_call_target="tpu_custom_call" | custom-call | flops 1048576 | bytes 1024 | tf_op jit(solution)/shard_map/cond/branch_1_fun/grad/pallas_call | solution.py:393
  40.9 12.8 %conditional.9 = (f32[64,256]{1,0:T(8,128)S(1)}, f32[64,256]{1,0:T(8,128)S(1)}, f32[144,256]{1,0:T(8,128)}, f32[144,256]{1,0:T(8,128)}, f32[144,256]{1,0:T(8,128...) conditional(s32[]{:T(128)} %convert_element_type.44, () %tuple.98, ...), branch_computations={%region_6.7_spmd, %region_7.8_spmd} | conditional | flops 114944 | bytes 11421672 | solution.py:546
  48.2 4.1 %collective-permute-start.12 = (f32[144,256]{1,0:T(8,128)}, f32[144,256]{1,0:T(8,128)}, u32[]{:S(2)}, u32[]{:S(2)}) collective-permute-start(f32[144,256]{1,0:T(8,128)} %collective-permute-done.10), channel_id=1, source_target_pairs={{0,1},{1,0},{2,3},{3,2},{4,5},{5,4},{6,7},{7,6},{8,9},{9,8},{10,11... | collective-permute-start | bytes 442376 | tf_op jit(solution)/shard_map/cond/branch_1_fun/ppermute | solution.py:521
  55.7 30.1 %conditional.10 = (bf16[64,1024]{1,0:T(8,128)(2,1)S(1)}, f32[64,256]{1,0:T(8,128)S(1)}, f32[2,4096,256]{2,1,0:T(8,128)}, bf16[256,4096]{1,0:T(8,128)(2,1)}) conditional(s32[]{:T(128)} %convert_element_type.44, () %tuple.97, (s32[]{:T(128)}, s32[]{:T(128)}, s32[]{:T(128)}, s32[1]{0:T(128)}, f32[64,256]{1,0:T(8,128)S(1)}, ...), branch_computations={%region_8.9_spmd, %region_9.10_spmd} | conditional | flops 1968534 | bytes 23210224 | solution.py:546
  55.7 4.0 %solve.1 = (f32[64,256]{1,0:T(8,128)S(1)}, f32[64,256]{1,0:T(8,128)S(1)}) custom-call(s32[1]{0:T(128)} %get-tuple-element.171.t_ref, f32[64,256]{1,0:T(8,128)S(1)} %get-tuple-element.172.own_ref, f32[64,256]{1,0:T(8,128)S(1)} %get-tuple-element.173.near_ref, f32[144,256]{1,0:T(8,128)} %get-tuple-element.174.chip_ref, f32[144,256]{1,0:T(8,128)} %get-tuple-element.175.got0, ...), custom_call_target="tpu_custom_call" | custom-call | flops 2441 | bytes 2441 | tf_op jit(solution)/shard_map/cond/branch_1_fun/solve/pallas_call | solution.py:232
  59.8 4.5 %right.1 = (f32[64,2048]{1,0:T(8,128)S(1)}, f32[64,2048]{1,0:T(8,128)S(1)}) custom-call(s32[4]{0:T(128)S(1)} %pad_add_fusion.h_ref, f32[64,256]{1,0:T(8,128)S(1)} %get-tuple-element.178.z_ref, f32[64,256]{1,0:T(8,128)S(1)} %get-tuple-element.350.b_ref, bf16[256,4096]{1,0:T(8,128)(2,1)} %get-tuple-element.180.x_ref.x0, ...), custom_call_target="tpu_custom_call" | custom-call | flops 262144 | bytes 1536 | tf_op jit(solution)/shard_map/cond/branch_1_fun/right/pallas_call | solution.py:272
  68.2 4.0 %moment.4.refs_0_ = f32[2,4096,256]{2,1,0:T(8,128)} custom-call(s32[1]{0:T(128)} %get-tuple-element.171.t_ref, bf16[256,4096]{1,0:T(8,128)(2,1)S(1)} %copy-done, bf16[256,4096]{1,0:T(8,128)(2,1)} %get-tuple-element.186.x1, bf16[256,4096]{1,0:T(8,128)(2,1)} %get-tuple-element.187.a0, bf16[256,4096]{1,0:T(8,128)(2,1)} %get-tuple-element.188.a1, ...), custom_call_target="tpu_custom_call" | custom-call | flops 262144 | bytes 2048 | tf_op jit(solution)/shard_map/cond/branch_1_fun/moment/pallas_call | solution.py:314
  72.3 2.7 %collective-permute-start.16 = (bf16[64,1024]{1,0:T(8,128)(2,1)S(1)}, bf16[64,1024]{1,0:T(8,128)(2,1)S(1)}, u32[]{:S(2)}, u32[]{:S(2)}) collective-permute-start(bf16[64,1024]{1,0:T(8,128)(2,1)S(1)} %fusion.2), channel_id=1, source_target_pairs={{0,16},{1,9},{2,18},{3,11},{4,20},{5,13},{6,22},{7,15},{8,24},{9,1... | collective-permute-start | bytes 393224 | tf_op jit(solution)/shard_map/cond/branch_1_fun/ppermute | solution.py:533
  74.9 4.0 %moment.5.refs_0_ = f32[2,4096,256]{2,1,0:T(8,128)} custom-call(s32[1]{0:T(128)} %get-tuple-element.171.t_ref, bf16[256,4096]{1,0:T(8,128)(2,1)S(1)} %copy-done, bf16[256,4096]{1,0:T(8,128)(2,1)} %get-tuple-element.186.x1, bf16[256,4096]{1,0:T(8,128)(2,1)} %get-tuple-element.187.a0, ...), custom_call_target="tpu_custom_call", output_to_operand_aliasing={{}: (9, {})} | custom-call | flops 262144 | bytes 2048 | tf_op jit(solution)/shard_map/cond/branch_1_fun/moment/pallas_call | solution.py:314
  81.8 4.0 %moment.6 = f32[2,4096,256]{2,1,0:T(8,128)} custom-call(s32[1]{0:T(128)} %get-tuple-element.171.t_ref, bf16[256,4096]{1,0:T(8,128)(2,1)S(1)} %copy-done, bf16[256,4096]{1,0:T(8,128)(2,1)} %get-tuple-element.186.x1, bf16[256,4096]{1,0:T(8,128)(2,1)} %get-tuple-element.187.a0, ...), custom_call_target="tpu_custom_call", output_to_operand_aliasing={{}: (9, {})} | custom-call | flops 262144 | bytes 2048 | tf_op jit(solution)/shard_map/cond/branch_1_fun/moment/pallas_call | solution.py:314
  87.7 20.9 %conditional.11 = (bf16[256,4096]{1,0:T(8,128)(2,1)}, bf16[256,1280]{1,0:T(8,128)(2,1)}, f32[1,2,4096,256]{3,2,1,0:T(8,128)}, f32[2,32,4096]{2,1,0:T(8,128)}) conditional(s32[]{:T(128)} %convert_element_type.44, () %tuple.96, (bf16[64,1024]{1,0:T(8,128)(2,1)S(1)}, bf16[2,1024,256]{2,1,0:T(8,128)(2,1)S(1)}, s32[1]{0:T(128)}, ...), branch_computations={%region_10.11_spmd, %region_11.12_spmd} | conditional | flops 590707 | bytes 12189740 | solution.py:546
  88.4 4.1 %moment.7.m_ref = f32[2,4096,256]{2,1,0:T(8,128)} custom-call(s32[1]{0:T(128)} %get-tuple-element.199.t_ref, bf16[256,4096]{1,0:T(8,128)(2,1)} %get-tuple-element.200.x0, bf16[256,4096]{1,0:T(8,128)(2,1)} %get-tuple-element.201.x1, bf16[256,4096]{1,0:T(8,128)(2,1)} %get-tuple-element.202.a0, ...), custom_call_target="tpu_custom_call", output_to_operand_aliasing={{}: (9, {})} | custom-call | flops 262144 | bytes 2048 | tf_op jit(solution)/shard_map/cond/branch_1_fun/moment/pallas_call | solution.py:314
  95.5 4.8 %error.2 = (f32[2,4096,256]{2,1,0:T(8,128)}, f32[64,4096]{1,0:T(8,128)}) custom-call(s32[2]{0:T(128)S(1)} %pad_add_fusion.1.q_ref, f32[2,4096,256]{2,1,0:T(8,128)} %moment.7.m_ref, bf16[64,1024]{1,0:T(8,128)(2,1)S(1)} %multiply_convert_fusion.r0, bf16[64,1024]{1,0:T(8,128)(2,1)S(1)} %collective-permute-done.20.r1, ...), custom_call_target="tpu_custom_call", output_to_operand_aliasing={{0}: (1, {})} | custom-call | flops 244 | bytes 2048 | tf_op jit(solution)/shard_map/cond/branch_1_fun/error/pallas_call | solution.py:358
  101.1 2.4 %finish_grad.2 = bf16[256,4096]{1,0:T(8,128)(2,1)} custom-call(bf16[256,2048]{1,0:T(8,128)(2,1)} %get-tuple-element.196.own_ref, bf16[256,2048]{1,0:T(8,128)(2,1)} %get-tuple-element.217.refs_0_), custom_call_target="tpu_custom_call" | custom-call | flops 384 | bytes 1024 | tf_op jit(solution)/shard_map/cond/branch_1_fun/finish_grad/pallas_call | solution.py:447
  103.5 4.8 %error.3 = (f32[2,4096,256]{2,1,0:T(8,128)}, f32[64,4096]{1,0:T(8,128)}) custom-call(s32[2]{0:T(128)S(1)} %pad_add_fusion.2.q_ref, f32[2,4096,256]{2,1,0:T(8,128)} %get-tuple-element.220.m_ref, bf16[64,1024]{1,0:T(8,128)(2,1)S(1)} %collective-permute-done.19.r0, ...), custom_call_target="tpu_custom_call", output_to_operand_aliasing={{0}: (1, {}), {1}: (5, {})} | custom-call | flops 244 | bytes 2048 | tf_op jit(solution)/shard_map/cond/branch_1_fun/error/pallas_call | solution.py:358
  (77 shorter events, 41.0 us)
Async XLA Ops:
  0.6 40.2 %collective-permute-start.23 = (bf16[256,4096]{1,0:T(8,128)(2,1)}, bf16[256,4096]{1,0:T(8,128)(2,1)}, u32[]{:S(2)}, u32[]{:S(2)}) collective-permute-start(bf16[256,4096]{1,0:T(8,128)(2,1)} %param.17), channel_id=1, source_target_pairs={{0,2},{2,0},{4,6},{6,4},{8,10},{10,8},{12,14},{14,12},{16,18},{18,... | collective-permute-start | bytes 6291464 | tf_op jit(solution)/shard_map/ppermute | solution.py:525
  5.5 5.7 %collective-permute-start.7 = (bf16[256,4096]{1,0:T(8,128)(2,1)}, bf16[256,4096]{1,0:T(8,128)(2,1)}, u32[]{:S(2)}, u32[]{:S(2)}) collective-permute-start(bf16[256,4096]{1,0:T(8,128)(2,1)} %get-tuple-element.124.x_ref), channel_id=1, source_target_pairs={{0,1},{1,0},{2,3},{3,2},{4,5},{5,4},{6,7},{7,6},{8,9},{9,8},{10,11... | collective-permute-start | bytes 6291464 | tf_op jit(solution)/shard_map/cond/branch_1_fun/ppermute | solution.py:521
  11.3 4.5 %collective-permute-start = (f32[128,256]{1,0:T(8,128)S(1)}, f32[128,256]{1,0:T(8,128)}, u32[]{:S(2)}, u32[]{:S(2)}) collective-permute-start(f32[128,256]{1,0:T(8,128)S(1)} %get-tuple-element.126), channel_id=1, source_target_pairs={{1,3},{3,1},{5,7},{7,5},{9,11},{11,9},{13,15},{15,13},{17,19},{19,... | collective-permute-start | bytes 393224 | tf_op jit(solution)/shard_map/cond/branch_1_fun/ppermute | solution.py:525
  15.8 40.0 %collective-permute-start.24 = (bf16[256,4096]{1,0:T(8,128)(2,1)}, bf16[256,4096]{1,0:T(8,128)(2,1)}, u32[]{:S(2)}, u32[]{:S(2)}) collective-permute-start(bf16[256,4096]{1,0:T(8,128)(2,1)} %get-tuple-element.279), channel_id=1, source_target_pairs={{0,2},{2,0},{4,6},{6,4},{8,10},{10,8},{12,14},{14,12},{16,18},{18,... | collective-permute-start | bytes 6291464 | tf_op jit(solution)/shard_map/ppermute | solution.py:525
  17.7 4.8 %collective-permute-start.1 = (f32[128,256]{1,0:T(8,128)}, f32[128,256]{1,0:T(8,128)S(1)}, u32[]{:S(2)}, u32[]{:S(2)}) collective-permute-start(f32[128,256]{1,0:T(8,128)} %get-tuple-element.134.far1), channel_id=1, source_target_pairs={{0,1},{1,0},{2,3},{3,2},{4,5},{5,4},{6,7},{7,6},{8,9},{9,8},{10,11... | collective-permute-start | bytes 393224 | tf_op jit(solution)/shard_map/cond/branch_1_fun/ppermute | solution.py:521
  23.8 5.7 %collective-permute-start.2 = (f32[64,256]{1,0:T(8,128)S(1)}, f32[64,256]{1,0:T(8,128)S(1)}, u32[]{:S(2)}, u32[]{:S(2)}) collective-permute-start(f32[64,256]{1,0:T(8,128)S(1)} %left.1), channel_id=1, source_target_pairs={{0,8},{1,5},{2,10},{3,7},{4,12},{5,1},{6,14},{7,3},{8,0},{9,13},{1... | collective-permute-start | bytes 196616 | tf_op jit(solution)/shard_map/cond/branch_1_fun/ppermute | solution.py:533
  29.6 6.8 %collective-permute-start.4 = (bf16[512,2048]{1,0:T(8,128)(2,1)S(1)}, bf16[512,2048]{1,0:T(8,128)(2,1)S(1)}, u32[]{:S(2)}, u32[]{:S(2)}) collective-permute-start(bf16[512,2048]{1,0:T(8,128)(2,1)S(1)} %get-tuple-element.145), channel_id=1, source_target_pairs={{0,1},{1,0},{2,3},{3,2},{4,5},{5,4},{6,7},{7,6},{8,9},{9,8},{10,11... | collective-permute-start | bytes 6291464 | tf_op jit(solution)/shard_map/cond/branch_1_fun/ppermute | solution.py:521
  29.7 6.7 %collective-permute-start.3 = (f32[64,256]{1,0:T(8,128)S(1)}, f32[64,256]{1,0:T(8,128)S(1)}, u32[]{:S(2)}, u32[]{:S(2)}) collective-permute-start(f32[64,256]{1,0:T(8,128)S(1)} %add.28), channel_id=1, source_target_pairs={{0,16},{1,9},{2,18},{3,11},{4,20},{5,13},{6,22},{7,15},{8,24},{9,1... | collective-permute-start | bytes 196616 | tf_op jit(solution)/shard_map/cond/branch_1_fun/ppermute | solution.py:533
  36.4 4.4 %collective-permute-start.6 = (bf16[512,2048]{1,0:T(8,128)(2,1)S(1)}, bf16[512,2048]{1,0:T(8,128)(2,1)}, u32[]{:S(2)}, u32[]{:S(2)}) collective-permute-start(bf16[512,2048]{1,0:T(8,128)(2,1)S(1)} %get-tuple-element.150), channel_id=1, source_target_pairs={{0,1},{1,0},{2,3},{3,2},{4,5},{5,4},{6,7},{7,6},{8,9},{9,8},{10,11... | collective-permute-start | bytes 6291464 | tf_op jit(solution)/shard_map/cond/branch_1_fun/ppermute | solution.py:521
  36.5 4.3 %collective-permute-start.5 = (f32[64,256]{1,0:T(8,128)S(1)}, f32[64,256]{1,0:T(8,128)S(1)}, u32[]{:S(2)}, u32[]{:S(2)}) collective-permute-start(f32[64,256]{1,0:T(8,128)S(1)} %add.29), channel_id=1, source_target_pairs={{0,4},{1,17},{2,6},{3,19},{4,0},{5,21},{6,2},{7,23},{8,12},{9,25},... | collective-permute-start | bytes 196616 | tf_op jit(solution)/shard_map/cond/branch_1_fun/ppermute | solution.py:533
  43.7 4.5 %collective-permute-start.11 = (bf16[256,4096]{1,0:T(8,128)(2,1)}, bf16[256,4096]{1,0:T(8,128)(2,1)}, u32[]{:S(2)}, u32[]{:S(2)}) collective-permute-start(bf16[256,4096]{1,0:T(8,128)(2,1)} %get-tuple-element.160), channel_id=1, source_target_pairs={{0,1},{1,0},{2,3},{3,2},{4,5},{5,4},{6,7},{7,6},{8,9},{9,8},{10,11... | collective-permute-start | bytes 6291464 | tf_op jit(solution)/shard_map/cond/branch_1_fun/ppermute | solution.py:521
  43.9 3.7 %collective-permute-start.10 = (f32[144,256]{1,0:T(8,128)}, f32[144,256]{1,0:T(8,128)}, u32[]{:S(2)}, u32[]{:S(2)}) collective-permute-start(f32[144,256]{1,0:T(8,128)} %slice_add_fusion), channel_id=1, source_target_pairs={{1,3},{3,1},{5,7},{7,5},{9,11},{11,9},{13,15},{15,13},{17,19},{19,... | collective-permute-start | bytes 442376 | tf_op jit(solution)/shard_map/cond/branch_1_fun/ppermute | solution.py:525
  48.2 5.5 %collective-permute-start.12 = (f32[144,256]{1,0:T(8,128)}, f32[144,256]{1,0:T(8,128)}, u32[]{:S(2)}, u32[]{:S(2)}) collective-permute-start(f32[144,256]{1,0:T(8,128)} %collective-permute-done.10), channel_id=1, source_target_pairs={{0,1},{1,0},{2,3},{3,2},{4,5},{5,4},{6,7},{7,6},{8,9},{9,8},{10,11... | collective-permute-start | bytes 442376 | tf_op jit(solution)/shard_map/cond/branch_1_fun/ppermute | solution.py:521
  53.7 34.1 %collective-permute-start.25 = (bf16[256,2048]{1,0:T(8,128)(2,1)}, bf16[256,2048]{1,0:T(8,128)(2,1)}, u32[]{:S(2)}, u32[]{:S(2)}) collective-permute-start(bf16[256,2048]{1,0:T(8,128)(2,1)} %get-tuple-element.287), channel_id=1, source_target_pairs={{0,2},{1,3},{2,0},{3,1},{4,6},{5,7},{6,4},{7,5},{8,10},{9,11},{10,... | collective-permute-start | bytes 3145736 | tf_op jit(solution)/shard_map/ppermute | solution.py:525
  54.2 33.5 %collective-permute-start.26 = (bf16[256,768]{1,0:T(8,128)(2,1)S(1)}, bf16[256,768]{1,0:T(8,128)(2,1)S(1)}, u32[]{:S(2)}, u32[]{:S(2)}) collective-permute-start(bf16[256,768]{1,0:T(8,128)(2,1)S(1)} %get-tuple-element.289), channel_id=1, source_target_pairs={{0,2},{1,3},{2,0},{3,1},{4,6},{5,7},{6,4},{7,5},{8,10},{9,11},{10,... | collective-permute-start | bytes 1179656 | tf_op jit(solution)/shard_map/ppermute | solution.py:525
  55.7 8.6 %collective-permute-start.13 = (bf16[256,4096]{1,0:T(8,128)(2,1)}, bf16[256,4096]{1,0:T(8,128)(2,1)}, u32[]{:S(2)}, u32[]{:S(2)}) collective-permute-start(bf16[256,4096]{1,0:T(8,128)(2,1)} %get-tuple-element.184.b0), channel_id=1, source_target_pairs={{0,1},{1,0},{2,3},{3,2},{4,5},{5,4},{6,7},{7,6},{8,9},{9,8},{10,11... | collective-permute-start | bytes 6291464 | tf_op jit(solution)/shard_map/cond/branch_1_fun/ppermute | solution.py:521
  64.4 2.1 %collective-permute-start.14 = (f32[64,2048]{1,0:T(8,128)S(1)}, f32[64,2048]{1,0:T(8,128)S(1)}, u32[]{:S(2)}, u32[]{:S(2)}) collective-permute-start(f32[64,2048]{1,0:T(8,128)S(1)} %get-tuple-element.185), channel_id=1, source_target_pairs={{0,1},{1,0},{2,3},{3,2},{4,5},{5,4},{6,7},{7,6},{8,9},{9,8},{10,11... | collective-permute-start | bytes 1572872 | tf_op jit(solution)/shard_map/cond/branch_1_fun/ppermute | solution.py:521
  66.5 5.7 %collective-permute-start.15 = (bf16[64,1024]{1,0:T(8,128)(2,1)S(1)}, bf16[64,1024]{1,0:T(8,128)(2,1)S(1)}, u32[]{:S(2)}, u32[]{:S(2)}) collective-permute-start(bf16[64,1024]{1,0:T(8,128)(2,1)S(1)} %fusion), channel_id=1, source_target_pairs={{0,8},{1,5},{2,10},{3,7},{4,12},{5,1},{6,14},{7,3},{8,0},{9,13},{1... | collective-permute-start | bytes 393224 | tf_op jit(solution)/shard_map/cond/branch_1_fun/ppermute | solution.py:533
  72.3 7.3 %collective-permute-start.16 = (bf16[64,1024]{1,0:T(8,128)(2,1)S(1)}, bf16[64,1024]{1,0:T(8,128)(2,1)S(1)}, u32[]{:S(2)}, u32[]{:S(2)}) collective-permute-start(bf16[64,1024]{1,0:T(8,128)(2,1)S(1)} %fusion.2), channel_id=1, source_target_pairs={{0,16},{1,9},{2,18},{3,11},{4,20},{5,13},{6,22},{7,15},{8,24},{9,1... | collective-permute-start | bytes 393224 | tf_op jit(solution)/shard_map/cond/branch_1_fun/ppermute | solution.py:533
  79.7 6.1 %collective-permute-start.17 = (bf16[64,1024]{1,0:T(8,128)(2,1)S(1)}, bf16[64,1024]{1,0:T(8,128)(2,1)S(1)}, u32[]{:S(2)}, u32[]{:S(2)}) collective-permute-start(bf16[64,1024]{1,0:T(8,128)(2,1)S(1)} %add_convert_fusion.1), channel_id=1, source_target_pairs={{0,4},{1,17},{2,6},{3,19},{4,0},{5,21},{6,2},{7,23},{8,12},{9,25},... | collective-permute-start | bytes 393224 | tf_op jit(solution)/shard_map/cond/branch_1_fun/ppermute | solution.py:533
  87.7 5.0 %collective-permute-start.18 = (bf16[64,1024]{1,0:T(8,128)(2,1)S(1)}, bf16[64,1024]{1,0:T(8,128)(2,1)S(1)}, u32[]{:S(2)}, u32[]{:S(2)}) collective-permute-start(bf16[64,1024]{1,0:T(8,128)(2,1)S(1)} %get-tuple-element.198), channel_id=1, source_target_pairs={{0,2},{1,3},{2,0},{3,1},{4,6},{5,7},{6,4},{7,5},{8,10},{9,11},{10,... | collective-permute-start | bytes 393224 | tf_op jit(solution)/shard_map/cond/branch_1_fun/ppermute | solution.py:525
  92.8 15.9 %collective-permute-start.21 = (bf16[256,1280]{1,0:T(8,128)(2,1)}, bf16[256,1280]{1,0:T(8,128)(2,1)}, u32[]{:S(2)}, u32[]{:S(2)}) collective-permute-start(bf16[256,1280]{1,0:T(8,128)(2,1)} %get-tuple-element.219), channel_id=1, source_target_pairs={{0,2},{1,3},{2,0},{3,1},{4,6},{5,7},{6,4},{7,5},{8,10},{9,11},{10,... | collective-permute-start | bytes 1966088 | tf_op jit(solution)/shard_map/cond/branch_1_fun/ppermute | solution.py:525
  94.0 6.4 %collective-permute-start.19 = (bf16[64,1024]{1,0:T(8,128)(2,1)S(1)}, bf16[64,1024]{1,0:T(8,128)(2,1)S(1)}, u32[]{:S(2)}, u32[]{:S(2)}) collective-permute-start(bf16[64,1024]{1,0:T(8,128)(2,1)S(1)} %multiply_convert_fusion.r0), channel_id=1, source_target_pairs={{0,8},{1,5},{2,10},{3,7},{4,12},{5,1},{6,14},{7,3},{8,0},{9,13},{1... | collective-permute-start | bytes 393224 | tf_op jit(solution)/shard_map/cond/branch_1_fun/ppermute | solution.py:533
  100.3 3.2 %collective-permute-start.22 = (bf16[64,1024]{1,0:T(8,128)(2,1)S(1)}, bf16[64,1024]{1,0:T(8,128)(2,1)S(1)}, u32[]{:S(2)}, u32[]{:S(2)}) collective-permute-start(bf16[64,1024]{1,0:T(8,128)(2,1)S(1)} %collective-permute-done.19.r0), channel_id=1, source_target_pairs={{0,1},{1,0},{2,3},{3,2},{4,5},{5,4},{6,7},{7,6},{8,9},{9,8},{10,11... | collective-permute-start | bytes 393224 | tf_op jit(solution)/shard_map/cond/branch_1_fun/ppermute | solution.py:521
  (7 other events, 30.4 us)
